TPU v7x, 32 devices: a whole 2x2x4 slice. The times are simulated.
32 devices in a mesh: dp: 4 (over y, x), chan: 8 (over z, core).
Axes of the slice: x: 2, y: 2, z: 4, core: 2. Of those that a mesh axis runs over, the one named last changes fastest.
Arguments:
- x_in: bfloat16 [4, 48, 360, 800], P('dp', None, None, 'chan'), may hold values from -12 to 12
- cotangent: bfloat16 [4, 48, 360, 800], P('dp', None, None, 'chan'), may hold values from -9 to 9
- land: int32 [4, 48, 360], P('dp'), may hold values 0 or 1
- grid_res: int32 [4], P('dp'), may hold values from 0 to 1
- dw_kernel: bfloat16 [49, 800], replicated, may hold values from -0.875 to 0.875
- gain: float32 [800], replicated, may hold values from 0.5 to 1.5
- shift: float32 [800], replicated, may hold values from -1.75 to 1.75
- res_bias: float32 [2, 800], replicated, may hold values from -3 to 3
- w_in: bfloat16 [800, 3200], replicated, may hold values from -0.21875 to 0.21875
- b_in: float32 [3200], replicated, may hold values from -1.75 to 1.75
- w_out: bfloat16 [3200, 800], replicated, may hold values from -0.109375 to 0.109375
- b_out: float32 [800], replicated, may hold values from -1.75 to 1.75
Outputs:
- mixed: bfloat16 [4, 48, 360, 800], P('dp', None, None, 'chan')
- x_grad: bfloat16 [4, 48, 360, 800], P('dp', None, None, 'chan')
- g_kernel: float32 [49, 800], replicated
- g_gain: float32 [800], replicated
- g_shift: float32 [800], replicated
- g_res_bias: float32 [2, 800], replicated
- g_w_in: float32 [800, 3200], replicated
- g_b_in: float32 [3200], replicated
- g_w_out: float32 [3200, 800], replicated
- g_b_out: float32 [800], replicated
All inputs are finite; a program needn't handle non-finite values. No bound on the sum of `land` on one device may be relied on, other than what follows from the above.
Results may differ from a plain program's by a relative error of at most 0.01.
Values may be sent and summed in bfloat16 or wider, within the bound.
No kernel may reach another device: no remote copies, remote signals or barrier semaphores. Data moves between devices by JAX's collectives and lax.ppermute only.
A program may use at most 320 MiB of HBM per device.

v0:
```python
from functools import partial
import math

import jax
import jax.numpy as jnp
from jax import lax
from jax.experimental import pallas as pl
from jax.experimental.pallas import tpu as pltpu
from jax.sharding import PartitionSpec as P

LANES = 128
SUBL = 8
VMEM_LIMIT = 56 * 1024 * 1024
CHAN = ("pair", "core")
CORES = 2
F32 = jnp.float32
BF16 = jnp.bfloat16


def round_up(value, step):
    return (value + step - 1) // step * step


def block_of(total, most):
    return max(size for size in range(1, most + 1) if total % size == 0)


class Sizes:
    def __init__(self, chan, height, width, bands, taps):
        self.chan, self.height, self.width, self.bands = chan, height, width, bands
        self.side = math.isqrt(taps)
        self.margin = self.side // 2
        self.rows = height // bands
        self.wide = round_up(width + 2 * self.margin, LANES)
        self.tiles = self.wide // LANES
        self.tail = width - (self.tiles - 1) * LANES
        self.pad = round_up(chan + 1, SUBL)
        self.packed_rows = bands * self.pad
        self.tail_units = round_up(self.rows * self.tail, LANES) // LANES
        self.units = self.rows * (self.tiles - 1) + self.tail_units


def params(semantics=("arbitrary",)):
    return pltpu.CompilerParams(dimension_semantics=semantics, vmem_limit_bytes=VMEM_LIMIT)


def roll_tiles(z, tiles, shift):
    jump, low = divmod(shift % z.wide, LANES)
    count = z.tiles
    if low == 0:
        return [tiles[(j - jump) % count] for j in range(count)]
    lane = lax.broadcasted_iota(jnp.int32, tiles[0].shape, 1)
    moved = [pltpu.roll(tile, low, 1) for tile in tiles]
    return [
        jnp.where(lane < low, moved[(j - jump - 1) % count], moved[(j - jump) % count])
        for j in range(count)
    ]


def wrap_tiles(z, tiles):
    last = tiles[-1]
    lane = lax.broadcasted_iota(jnp.int32, last.shape, 1)
    ahead = pltpu.roll(tiles[0], z.tail, 1)
    behind = pltpu.roll(last, LANES - z.tail, 1)
    last = jnp.where(lane < z.tail, last, jnp.where(lane < z.tail + z.margin, ahead, behind))
    return tiles[:-1] + [last]


def row_tiles(z, value):
    tiles = [value[:, LANES * j : LANES * (j + 1)] for j in range(z.tiles - 1)]
    tail = value[:, LANES * (z.tiles - 1) :]
    zeros = jnp.zeros((value.shape[0], LANES - z.tail), F32)
    return tiles + [jnp.concatenate([tail, zeros], axis=1)]


def pack_tails(z, tails):
    lane = lax.broadcasted_iota(jnp.int32, tails[0].shape, 1)
    tiles = []
    for t in range(z.tail_units):
        begin, tile = LANES * t, None
        for row, tail in enumerate(tails):
            low = z.tail * row - begin
            if low >= LANES or low + z.tail <= 0:
                continue
            moved = pltpu.roll(tail, low % LANES, 1) if low % LANES else tail
            tile = moved if tile is None else jnp.where(lane >= low, moved, tile)
        end = z.tail * z.rows - begin
        tiles.append(jnp.where(lane < end, tile, 0.0) if end < LANES else tile)
    return tiles


def unpack_tails(z, tiles):
    lane = lax.broadcasted_iota(jnp.int32, tiles[0].shape, 1)
    tails = []
    for row in range(z.rows):
        t, low = divmod(z.tail * row, LANES)
        tail = pltpu.roll(tiles[t], LANES - low, 1) if low else tiles[t]
        if LANES - low < z.tail:
            tail = jnp.where(lane < LANES - low, tail, pltpu.roll(tiles[t + 1], LANES - low, 1))
        tails.append(jnp.where(lane < z.tail, tail, 0.0))
    return tails


def pack_rows(z, rows):
    full = z.tiles - 1
    return [row[j] for row in rows for j in range(full)] + pack_tails(z, [row[full] for row in rows])


def unpack_rows(z, tiles):
    full = z.tiles - 1
    tails = unpack_tails(z, tiles[z.rows * full :])
    return [tiles[row * full : (row + 1) * full] + [tails[row]] for row in range(z.rows)]


def packed_tiles(refs, read):
    return [
        read(ref, slice(LANES * k, LANES * (k + 1)))
        for ref in refs
        for k in range(ref.shape[-1] // LANES)
    ]


def whole(shape):
    return pl.BlockSpec(shape, lambda *_: (0,) * len(shape))


def smem():
    return pl.BlockSpec(memory_space=pltpu.SMEM)


def cost(bytes_accessed, flops=10**7):
    return pl.CostEstimate(flops=flops, bytes_accessed=bytes_accessed, transcendentals=0)


PAIR = 2
GROUP = 16


def pair_rows(z):
    return pl.BlockSpec((PAIR * z.rows, z.pad, z.width), lambda g: (g, 0, 0))


def pair_wide(z):
    return pl.BlockSpec((PAIR * z.rows, z.pad, z.wide), lambda g: (g, 0, 0))


def pair_land(z):
    return pl.BlockSpec((PAIR * z.rows, 1, z.width), lambda g: (g, 0, 0))


def pair_packed(z, cells):
    return pl.BlockSpec((PAIR * z.pad, cells), lambda g: (g, 0))


def group_rows(z):
    return pl.BlockSpec((z.height, GROUP, z.width), lambda c: (0, c, 0))


def group_wide(z):
    return pl.BlockSpec((z.height, GROUP, z.wide), lambda c: (0, c, 0))


def group_lanes(count):
    return pl.BlockSpec((count, GROUP, LANES), lambda c: (0, c, 0))


def write_pair(z, refs, bands):
    tiles = [jnp.concatenate(both, axis=0).astype(BF16) for both in zip(*bands)]
    unit = 0
    for ref in refs:
        for k in range(ref.shape[1] // LANES):
            ref[:, LANES * k : LANES * (k + 1)] = tiles[unit]
            unit += 1


def pack_out_grad(z, cells, cot, land):
    def kernel(cot_ref, land_ref, out_ref, sum_ref):
        @pl.when(pl.program_id(0) == 0)
        def _():
            sum_ref[...] = jnp.zeros_like(sum_ref)

        channel = lax.broadcasted_iota(jnp.int32, (z.pad, z.width), 0)
        total = jnp.zeros((z.pad, LANES), F32)
        bands = []
        for band in range(PAIR):
            rows = []
            for row in range(z.rows * band, z.rows * (band + 1)):
                value = cot_ref[row].astype(F32) * land_ref[row].astype(F32)
                rows.append(row_tiles(z, jnp.where(channel < z.chan, value, 0.0)))
                total = total + sum(rows[-1])
            bands.append(pack_rows(z, rows))
        sum_ref[...] += total
        write_pair(z, [out_ref], bands)

    out, sums = pl.pallas_call(
        kernel,
        grid=(z.bands // PAIR,),
        in_specs=[pair_rows(z), pair_land(z)],
        out_specs=[pair_packed(z, cells), whole((z.pad, LANES))],
        out_shape=[
            jax.ShapeDtypeStruct((z.packed_rows, cells), BF16),
            jax.ShapeDtypeStruct((z.pad, LANES), F32),
        ],
        compiler_params=params(),
        cost_estimate=cost(8 * 10**6),
    )(cot, land)
    return out, jnp.sum(sums, axis=1)[: z.chan]


def fill_rows(z, target, read, wrap):
    zeros = jnp.zeros(target.shape[1:], F32)
    for k in range(z.margin):
        target[k] = zeros
        target[z.margin + z.height + k] = zeros

    def body(h, carry):
        tiles = row_tiles(z, read(h))
        if wrap:
            tiles = wrap_tiles(z, tiles)
        for j, tile in enumerate(tiles):
            target[z.margin + h, :, LANES * j : LANES * (j + 1)] = tile
        return carry

    lax.fori_loop(0, z.height, body, 0, unroll=8)


def convolve(z, steps, at, taps_ref, source, flip, put, carry):
    span = steps + 2 * z.margin

    def body(block, carry):
        h0 = block * steps
        rows = [
            [source[h0 + m, at, LANES * j : LANES * (j + 1)] for j in range(z.tiles)]
            for m in range(span)
        ]
        sums = [None] * steps
        for b in range(z.side):
            weights = [taps_ref[z.side * a + b, at, :] for a in range(z.side)]
            for r in range(steps):
                part = None
                for a in range(z.side):
                    row = rows[r + 2 * z.margin - a] if flip else rows[r + a]
                    terms = [weights[a] * tile for tile in row]
                    part = terms if part is None else [p + t for p, t in zip(part, terms)]
                part = roll_tiles(z, part, b - z.margin if flip else z.margin - b)
                sums[r] = part if b == 0 else [s + p for s, p in zip(sums[r], part)]
        for r in range(steps):
            carry = put(h0 + r, sums[r], carry)
        return carry

    return lax.fori_loop(0, z.height // steps, body, carry, unroll=2)


def conv_forward(z, taps, x):
    def kernel(taps_ref, x_ref, conv_ref, sum_ref, square_ref, source):
        fill_rows(z, source, lambda h: x_ref[h].astype(F32), True)
        lane = lax.broadcasted_iota(jnp.int32, (SUBL, LANES), 1)
        for part in range(GROUP // SUBL):
            at = slice(SUBL * part, SUBL * (part + 1))

            def put(h, tiles, carry):
                for j, tile in enumerate(tiles):
                    conv_ref[h, at, LANES * j : LANES * (j + 1)] = tile
                tiles = tiles[:-1] + [jnp.where(lane < z.tail, tiles[-1], 0.0)]
                return carry[0] + sum(tiles), carry[1] + sum(t * t for t in tiles)

            @pl.when(pl.program_id(0) * GROUP + SUBL * part < z.chan)
            def _():
                zero = jnp.zeros((SUBL, LANES), F32)
                total, square = convolve(z, 4, at, taps_ref, source, False, put, (zero, zero))
                sum_ref[at, :] = total
                square_ref[at, :] = square

    lane_spec = pl.BlockSpec((GROUP, LANES), lambda c: (c, 0))
    lane_shape = jax.ShapeDtypeStruct((z.pad, LANES), F32)
    conv, total, square = pl.pallas_call(
        kernel,
        grid=(pl.cdiv(z.chan, GROUP),),
        in_specs=[group_lanes(taps.shape[0]), group_rows(z)],
        out_specs=[group_wide(z), lane_spec, lane_spec],
        out_shape=[
            jax.ShapeDtypeStruct((z.height, z.pad, z.wide), F32), lane_shape, lane_shape,
        ],
        scratch_shapes=[pltpu.VMEM((z.height + 2 * z.margin, GROUP, z.wide), F32)],
        compiler_params=params(),
        cost_estimate=cost(16 * 10**6, 10**10),
    )(taps, x)
    return conv, jnp.sum(total, axis=1)[: z.chan], jnp.sum(square, axis=1)[: z.chan]


def pack_normed(z, lengths, conv, columns):
    def kernel(columns_ref, conv_ref, *outs):
        channel = lax.broadcasted_iota(jnp.int32, (z.pad, LANES), 0)
        filler = jnp.where(channel == z.chan, 1.0, 0.0)
        mean, factor, offset = columns_ref[0], columns_ref[1], columns_ref[2]
        bands = []
        for band in range(PAIR):
            rows = []
            for row in range(z.rows * band, z.rows * (band + 1)):
                tiles = [conv_ref[row, :, LANES * j : LANES * (j + 1)] for j in range(z.tiles)]
                rows.append(
                    [
                        jnp.where(channel < z.chan, (tile - mean) * factor + offset, filler)
                        for tile in tiles
                    ]
                )
            bands.append(pack_rows(z, rows))
        write_pair(z, outs, bands)

    return pl.pallas_call(
        kernel,
        grid=(z.bands // PAIR,),
        in_specs=[whole(columns.shape), pair_wide(z)],
        out_specs=[pair_packed(z, n) for n in lengths],
        out_shape=[jax.ShapeDtypeStruct((z.packed_rows, n), BF16) for n in lengths],
        compiler_params=params(),
        cost_estimate=cost(12 * 10**6),
    )(columns, conv)


def norm_sums(z, parts, conv, columns):
    count = len(parts)

    def kernel(columns_ref, conv_ref, *rest):
        ins, (shift_ref, gain_ref) = rest[:count], rest[count:]

        @pl.when(pl.program_id(0) == 0)
        def _():
            shift_ref[...] = jnp.zeros_like(shift_ref)
            gain_ref[...] = jnp.zeros_like(gain_ref)

        mean = columns_ref[0]
        tiles = packed_tiles(ins, lambda ref, lanes: ref[:, lanes].astype(F32))
        shift = jnp.zeros((z.pad, LANES), F32)
        gain = jnp.zeros((z.pad, LANES), F32)
        for band in range(PAIR):
            rows = unpack_rows(z, [tile[z.pad * band : z.pad * (band + 1)] for tile in tiles])
            for row, grads in enumerate(rows):
                for j, grad in enumerate(grads):
                    value = conv_ref[z.rows * band + row, :, LANES * j : LANES * (j + 1)]
                    shift = shift + grad
                    gain = gain + grad * (value - mean)
        shift_ref[...] += shift
        gain_ref[...] += gain * columns_ref[1]

    lane_shape = jax.ShapeDtypeStruct((z.pad, LANES), F32)
    shift, gain = pl.pallas_call(
        kernel,
        grid=(z.bands // PAIR,),
        in_specs=[whole(columns.shape), pair_wide(z)] + [pair_packed(z, p.shape[1]) for p in parts],
        out_specs=[whole((z.pad, LANES))] * 2,
        out_shape=[lane_shape, lane_shape],
        compiler_params=params(),
        cost_estimate=cost(12 * 10**6),
    )(columns, conv, *parts)
    return jnp.sum(shift, axis=1)[: z.chan], jnp.sum(gain, axis=1)[: z.chan]


def conv_gradient(z, begin, end, columns, parts, conv, x, ntaps, before):
    count = len(parts)
    parts = [part.reshape(z.bands, z.pad, part.shape[1]) for part in parts]
    steps = 4
    before = [] if before is None else list(before)

    def kernel(columns_ref, conv_ref, x_ref, *rest):
        ins, (grad_ref, product_ref, grads, source) = rest[:count], rest[-4:]
        mean, scale, factor, shift, gain = (columns_ref[k] for k in range(5))

        def band_body(band, carry):
            tiles = packed_tiles(ins, lambda ref, lanes: ref[band, :, lanes].astype(F32))
            for row, values in enumerate(unpack_rows(z, tiles)):
                h = band * z.rows + row
                made = []
                for j, value in enumerate(values):
                    centred = (conv_ref[h, :, LANES * j : LANES * (j + 1)] - mean) * scale
                    made.append(factor * (value - (shift + centred * gain)))
                for j, tile in enumerate(wrap_tiles(z, made)):
                    at = slice(LANES * j, LANES * (j + 1))
                    grads[h, :, at] = tile
                    grad_ref[h, :, at] = tile.astype(BF16)
            return carry

        lax.fori_loop(0, z.bands, band_body, 0)
        fill_rows(z, source, lambda h: x_ref[h].astype(F32), False)
        for part in range(GROUP // SUBL):
            at = slice(SUBL * part, SUBL * (part + 1))

            @pl.when((begin + pl.program_id(0)) * GROUP + SUBL * part < z.chan)
            def _():
                for b in range(z.side):

                    def body(block, totals):
                        h0 = block * steps
                        rows = [
                            [source[h0 + m, at, LANES * j : LANES * (j + 1)] for j in range(z.tiles)]
                            for m in range(steps + 2 * z.margin)
                        ]
                        totals = list(totals)
                        for r in range(steps):
                            moved = roll_tiles(
                                z,
                                [grads[h0 + r, at, LANES * j : LANES * (j + 1)] for j in range(z.tiles)],
                                b - z.margin,
                            )
                            for a in range(z.side):
                                for m, tile in zip(moved, rows[r + a]):
                                    totals[a] = totals[a] + m * tile
                        return tuple(totals)

                    zero = jnp.zeros((SUBL, LANES), F32)
                    totals = lax.fori_loop(0, z.height // steps, body, (zero,) * z.side, unroll=4)
                    for a in range(z.side):
                        product_ref[z.side * a + b, at, :] = totals[a]

    def group(shape):
        return pl.BlockSpec(shape, lambda c: (0, begin + c, 0))

    operands = [columns, conv, x, *parts, *before]
    return pl.pallas_call(
        kernel,
        grid=(end - begin,),
        in_specs=[
            group((5, GROUP, LANES)), group((z.height, GROUP, z.wide)),
            group((z.height, GROUP, z.width)),
        ]
        + [group((z.bands, GROUP, p.shape[2])) for p in parts]
        + [pl.BlockSpec(memory_space=pl.ANY)] * len(before),
        out_specs=[group((z.height, GROUP, z.wide)), group((ntaps, GROUP, LANES))],
        out_shape=[
            jax.ShapeDtypeStruct((z.height, z.pad, z.wide), BF16),
            jax.ShapeDtypeStruct((ntaps, z.pad, LANES), F32),
        ],
        scratch_shapes=[
            pltpu.VMEM((z.height, GROUP, z.wide), F32),
            pltpu.VMEM((z.height + 2 * z.margin, GROUP, z.wide), F32),
        ],
        input_output_aliases={len(operands) - 2 + k: k for k in range(len(before))},
        compiler_params=params(),
        cost_estimate=cost(10 * 10**6, 4 * 10**9),
    )(*operands)


def conv_backward(z, taps, grad, cot, land):
    def kernel(taps_ref, grad_ref, cot_ref, land_ref, out_ref, source, result):
        zeros = jnp.zeros(source.shape[1:], F32)
        for k in range(z.margin):
            source[k] = zeros
            source[z.margin + z.height + k] = zeros

        def fill(h, carry):
            source[z.margin + h] = grad_ref[h].astype(F32)
            return carry

        lax.fori_loop(0, z.height, fill, 0, unroll=8)
        for part in range(GROUP // SUBL):
            at = slice(SUBL * part, SUBL * (part + 1))

            def put(h, tiles, carry):
                for j, tile in enumerate(tiles):
                    result[h, at, LANES * j : LANES * (j + 1)] = tile
                return carry

            @pl.when(pl.program_id(0) * GROUP + SUBL * part < z.chan)
            def _():
                convolve(z, 4, at, taps_ref, source, True, put, 0)

        def finish(h, carry):
            direct = cot_ref[h].astype(F32) * land_ref[h].astype(F32)
            out_ref[h] = (direct + result[h][:, : z.width]).astype(BF16)
            return carry

        lax.fori_loop(0, z.height, finish, 0, unroll=8)

    return pl.pallas_call(
        kernel,
        grid=(pl.cdiv(z.chan, GROUP),),
        in_specs=[
            group_lanes(taps.shape[0]), group_wide(z), group_rows(z),
            whole((z.height, 1, z.width)),
        ],
        out_specs=group_rows(z),
        out_shape=jax.ShapeDtypeStruct((z.height, z.chan, z.width), BF16),
        scratch_shapes=[
            pltpu.VMEM((z.height + 2 * z.margin, GROUP, z.wide), F32),
            pltpu.VMEM((z.height, GROUP, z.wide), F32),
        ],
        compiler_params=params(),
        cost_estimate=cost(16 * 10**6, 10**10),
    )(taps, grad, cot, land)


def mix_branch(z, branch, x, land):
    def kernel(x_ref, land_ref, branch_ref, out_ref):
        tiles = packed_tiles([branch_ref], lambda ref, lanes: ref[:, lanes].astype(F32))
        for band in range(PAIR):
            rows = unpack_rows(z, [tile[z.pad * band : z.pad * (band + 1)] for tile in tiles])
            for k, row in enumerate(rows):
                h = z.rows * band + k
                value = jnp.concatenate(row, axis=1)[:, : z.width]
                value = land_ref[h].astype(F32) * (x_ref[h].astype(F32) + value)
                out_ref[h] = value.astype(BF16)

    return pl.pallas_call(
        kernel,
        grid=(z.bands // PAIR,),
        in_specs=[pair_rows(z), pair_land(z), pair_packed(z, branch.shape[1])],
        out_specs=pair_rows(z),
        out_shape=jax.ShapeDtypeStruct((z.height, z.chan, z.width), BF16),
        compiler_params=params(),
        cost_estimate=cost(12 * 10**6),
    )(x, land, branch)


def gelu_parts(h):
    span = 1.0 + (0.3275911 * math.sqrt(0.5)) * jnp.abs(h)
    t = pl.reciprocal(span, approx=True)
    t = t * (2.0 - span * t)
    bell = jnp.exp2((-0.5 / math.log(2.0)) * (h * h))
    poly = t * (
        0.5 * 0.254829592
        + t
        * (
            0.5 * -0.284496736
            + t * (0.5 * 1.421413741 + t * (0.5 * -1.453152027 + t * (0.5 * 1.061405429)))
        )
    )
    tail = poly * bell
    phi = jnp.where(h >= 0, 1.0 - tail, tail)
    return h * phi, phi + h * ((1.0 / math.sqrt(2.0 * math.pi)) * bell)


def pad_weight(z, matrix):
    groups, hidden = matrix.shape[0] // z.chan, matrix.shape[1]
    block = block_of(hidden, 640)
    rows = groups * z.pad

    def kernel(in_ref, out_ref, transposed_ref, wide):
        value = in_ref[...].astype(F32)
        zeros = jnp.zeros((z.pad - z.chan, block), F32)
        for k in range(groups):
            wide[z.pad * k : z.pad * (k + 1), :] = jnp.concatenate(
                [value[z.chan * k : z.chan * (k + 1), :], zeros], axis=0
            )
        padded = wide[...]
        out_ref[...] = padded.astype(BF16)
        transposed_ref[...] = padded.T.astype(BF16)

    return pl.pallas_call(
        kernel,
        grid=(hidden // block,),
        in_specs=[pl.BlockSpec((groups * z.chan, block), lambda f: (0, f))],
        out_specs=[
            pl.BlockSpec((rows, block), lambda f: (0, f)),
            pl.BlockSpec((block, rows), lambda f: (f, 0)),
        ],
        out_shape=[
            jax.ShapeDtypeStruct((rows, hidden), BF16),
            jax.ShapeDtypeStruct((hidden, rows), BF16),
        ],
        scratch_shapes=[pltpu.VMEM((rows, block), F32)],
        compiler_params=params(),
        cost_estimate=cost(16 * 10**6),
    )(matrix)


def lane_block(rows, cells, part):
    return pl.BlockSpec((rows, cells), lambda *_: (0, part))


def row_step(rows, most):
    return max(n for n in range(16, most + 1, 16) if rows % n == 0)


def mlp(part, length, normed, out_grad, w_in_t, w_in, w_out, w_out_t, b_in, b_out, branch_all):
    packed, cells = normed.shape
    hidden = w_in_t.shape[0]
    block = block_of(hidden, 640)
    inner = row_step(block, 320)
    blocks = hidden // block
    pairs = block // inner // 2
    rows = row_step(packed, 416)
    outs = packed // rows

    def kernel(
        n_ref, g_ref, w_in_t_ref, w_in_ref, w_out_ref, w_out_t_ref, b_in_ref, b_out_ref, *rest
    ):
        (
            branch_ref, norm_ref, active_out, hidden_out,
            h_0, h_1, back_0, back_1, active, grads, sems,
        ) = rest[-11:]
        step = pl.program_id(0)

        def products(k, h, back):
            at = pl.ds(k * inner, inner)
            h[...] = (
                jnp.dot(w_in_t_ref[at, :], n_ref[...], preferred_element_type=F32) + b_in_ref[at, :]
            )
            back[...] = jnp.dot(w_out_ref[at, :], g_ref[:, :cells], preferred_element_type=F32)

        def gelu(k, h, back):
            at = pl.ds(pl.multiple_of(jnp.maximum(k, 0) * inner, inner), inner)
            value, slope = gelu_parts(h[...])
            active[at, :] = value.astype(BF16)
            grads[at, :] = (back[...] * slope).astype(BF16)

        @pl.when(step < blocks)
        def _():
            first = step * (2 * pairs)

            def body(i, carry):
                products(2 * i, h_0, back_0)
                gelu(first + 2 * i - 1, h_1, back_1)
                products(2 * i + 1, h_1, back_1)
                gelu(first + 2 * i, h_0, back_0)
                return carry

            lax.fori_loop(0, pairs, body, 0)

        copies = [
            pltpu.make_async_copy(active, active_out, sems.at[0]),
            pltpu.make_async_copy(grads, hidden_out, sems.at[1]),
        ]

        @pl.when(step == blocks)
        def _():
            gelu(2 * pairs * blocks - 1, h_1, back_1)
            for copy in copies:
                copy.start()

        @pl.when(step >= blocks)
        def _():
            branch = jnp.dot(w_out_t_ref[...], active[...], preferred_element_type=F32)
            branch_ref[:, :cells] = (branch + b_out_ref[...]).astype(BF16)
            norm = jnp.dot(w_in_ref[...], grads[...], preferred_element_type=F32)
            norm_ref[...] = norm.astype(BF16)

        @pl.when(step == blocks + outs - 1)
        def _():
            for copy in copies:
                copy.wait()

    def at_in(f):
        return jnp.minimum(f, blocks - 1)

    def at_out(f):
        return jnp.maximum(f - blocks, 0)

    tall_block = pl.BlockSpec((block, packed), lambda f: (at_in(f), 0))
    wide_block = pl.BlockSpec((rows, hidden), lambda f: (at_out(f), 0))
    anywhere = pl.BlockSpec(memory_space=pl.ANY)
    operands = [normed, out_grad, w_in_t, w_in, w_out, w_out_t, b_in, b_out]
    in_specs = [
        whole((packed, cells)), lane_block(packed, length, part),
        tall_block, wide_block, tall_block, wide_block,
        pl.BlockSpec((block, 1), lambda f: (at_in(f), 0)),
        pl.BlockSpec((rows, 1), lambda f: (at_out(f), 0)),
    ]
    aliases = {}
    if branch_all is not None:
        aliases = {len(operands): 0}
        operands.append(branch_all)
        in_specs.append(anywhere)
    buffer = pltpu.VMEM((inner, cells), F32)
    return pl.pallas_call(
        kernel,
        grid=(blocks + outs,),
        in_specs=in_specs,
        out_specs=[
            pl.BlockSpec((rows, length), lambda f: (at_out(f), part)),
            pl.BlockSpec((rows, cells), lambda f: (at_out(f), 0)),
            anywhere, anywhere,
        ],
        out_shape=[
            jax.ShapeDtypeStruct(out_grad.shape, BF16),
            jax.ShapeDtypeStruct((packed, cells), BF16),
            jax.ShapeDtypeStruct((hidden, cells), BF16),
            jax.ShapeDtypeStruct((hidden, cells), BF16),
        ],
        scratch_shapes=[buffer] * 4
        + [pltpu.VMEM((hidden, cells), BF16)] * 2
        + [pltpu.SemaphoreType.DMA((2,))],
        input_output_aliases=aliases,
        compiler_params=params(),
        cost_estimate=pl.CostEstimate(
            flops=8 * packed * cells * hidden, bytes_accessed=4 * 10**7, transcendentals=cells * hidden
        ),
    )(*operands)


def weight_grad(core, lefts, rights):
    rows, hidden = lefts[0][0].shape[0], rights[0].shape[0]
    half = rows // CORES
    block = block_of(hidden, 640)
    arrays = []
    for array, _ in lefts:
        if not any(array is known for known in arrays):
            arrays.append(array)
    which = [next(k for k, known in enumerate(arrays) if known is array) for array, _ in lefts]

    def kernel(core_ref, *refs):
        mine_ref, sent_ref, both = refs[-3:]
        total = None
        for k, (_, start), right in zip(which, lefts, refs[len(arrays) : -3]):
            part = lax.dot_general(
                refs[k][:, start : start + right.shape[1]], right[...],
                (((1,), (1,)), ((), ())), preferred_element_type=F32,
            )
            total = part if total is None else total + part
        both[0] = total[:half].astype(BF16)
        both[1] = total[half:].astype(BF16)
        mine_ref[...] = both[core_ref[0]]
        sent_ref[...] = both[1 - core_ref[0]]

    cells = sum(right.shape[1] for right in rights)
    out = jax.ShapeDtypeStruct((half, hidden), BF16)
    return pl.pallas_call(
        kernel,
        grid=(hidden // block,),
        in_specs=[smem()] + [whole(array.shape) for array in arrays]
        + [pl.BlockSpec((block, right.shape[1]), lambda f: (f, 0)) for right in rights],
        out_specs=[pl.BlockSpec((half, block), lambda f: (0, f))] * 2,
        out_shape=[out, out],
        scratch_shapes=[pltpu.VMEM((CORES, half, block), BF16)],
        compiler_params=params(),
        cost_estimate=cost(24 * 10**6, 2 * rows * cells * hidden),
    )(core[None], *arrays, *rights)


def unpad_rows(z, place, pieces):
    groups, hidden = pieces[0].shape[0] // z.pad, pieces[0].shape[1]

    def kernel(place_ref, *refs):
        out_ref = refs[-1]

        def put(ref):
            value = ref[...].astype(F32)
            for k in range(groups):
                out_ref[z.chan * k : z.chan * (k + 1), :] = value[z.pad * k : z.pad * k + z.chan, :]

        wanted = jnp.bitwise_xor(pl.program_id(0), place_ref[0])
        for k, ref in enumerate(refs[:-1]):
            pl.when(wanted == k)(partial(put, ref))

    return pl.pallas_call(
        kernel,
        grid=(4,),
        in_specs=[smem()] + [whole(pieces[0].shape)] * 4,
        out_specs=pl.BlockSpec((groups * z.chan, hidden), lambda q: (q, 0)),
        out_shape=jax.ShapeDtypeStruct((4 * groups * z.chan, hidden), F32),
        compiler_params=params(),
        cost_estimate=cost(16 * 10**6),
    )(place[None], *pieces)


def exchange(value):
    return lax.all_to_all(value, CHAN, split_axis=0, concat_axis=0, tiled=True)


def after(value, *others):
    return lax.optimization_barrier((value, *others))[0]


def dp_sum(value):
    ways = lax.axis_size("dp")
    total = value
    for turn in range(1, ways):
        total = total + lax.ppermute(value, "dp", [(i, i ^ turn) for i in range(ways)])
    return total


def swap_cores(value):
    return lax.ppermute(value, "core", [(0, 1), (1, 0)])


class HalvingSum:
    def __init__(self, turns, mine, sent):
        place = lax.axis_index("dp")
        self.turns = turns
        self.bits = [jnp.bitwise_and(place // turn, 1) for turn in turns]
        self.core = lax.axis_index("core")
        self.mine, self.other = mine, swap_cores(sent)

    def meet(self, value, turn):
        ways = lax.axis_size("dp")
        return lax.ppermute(value, "dp", [(i, i ^ turn) for i in range(ways)])

    def pair(self, half):
        rows = self.mine.shape[0] // 2
        at = half * rows
        return lax.dynamic_slice_in_dim(self.mine, at, rows, 0).astype(
            F32
        ) + lax.dynamic_slice_in_dim(self.other, at, rows, 0).astype(F32)

    def first(self):
        self.arrived = self.meet(self.pair(1 - self.bits[0]).astype(BF16), self.turns[0])

    def second(self, ready):
        arrived = after(self.arrived, ready)
        total = self.pair(self.bits[0]) + arrived.astype(F32)
        rows = total.shape[0] // 2
        send = lax.dynamic_slice_in_dim(total, (1 - self.bits[1]) * rows, rows, 0).astype(BF16)
        self.kept = lax.dynamic_slice_in_dim(total, self.bits[1] * rows, rows, 0)
        self.sent = send
        self.arrived = self.meet(send, self.turns[1])

    def share(self, ready):
        return (self.kept + after(self.arrived, ready).astype(F32)).astype(BF16)

    def back_first(self, share):
        self.own = share
        self.arrived = self.meet(share, self.turns[1])

    def back_second(self, ready):
        other = after(self.arrived, ready)
        low = self.bits[1] == 0
        self.own = jnp.concatenate(
            [jnp.where(low, self.own, other), jnp.where(low, other, self.own)], axis=0
        )
        self.arrived = self.meet(self.own, self.turns[0])
        self.swapped = swap_cores(self.own)

    def finish(self, z, ready):
        other = after(self.arrived, ready)
        pieces = [self.own, other, self.swapped, swap_cores(other)]
        return unpad_rows(z, self.core * 2 + self.bits[0], pieces), pieces

    def first_row(self, pieces, row):
        place = self.core * 2 + self.bits[0]
        found = pieces[0][row]
        for k in range(1, 4):
            found = jnp.where(place == k, pieces[k][row], found)
        return found.astype(F32)


def per_device(
    x_in, cotangent, land, grid_res, dw_kernel, gain, shift, res_bias, w_in, b_in, w_out, b_out
):
    samples, height, columns, chan = x_in.shape
    groups = lax.axis_size("pair") * CORES
    first = (lax.axis_index("pair") * CORES + lax.axis_index("core")) * chan
    width = chan * groups
    ntaps = dw_kernel.shape[0]
    z = Sizes(chan, height, columns, groups, ntaps)
    pixels = float(samples * lax.axis_size("dp") * height * columns)
    part = (z.units + 1) // 2 * LANES
    lengths = [part, z.units * LANES - part]
    starts = [0, part]

    def own(values, axis=0):
        return lax.dynamic_slice_in_dim(values, first, chan, axis)

    def over_lanes(rows):
        rows = jnp.pad(rows, ((0, 0), (0, z.pad - chan)))
        return jnp.broadcast_to(rows[:, :, None], rows.shape + (LANES,))

    x = jnp.transpose(x_in[0], (0, 2, 1))
    cot = jnp.transpose(cotangent[0], (0, 2, 1))
    land3 = land[0][:, None, :]

    grad_packed, part_b_out = pack_out_grad(z, sum(lengths), cot, land3)
    grad_band = exchange(grad_packed)

    taps = over_lanes(own(dw_kernel, 1).astype(F32))
    conv, total, square = conv_forward(z, taps, after(x, grad_packed))
    total, square = lax.psum((total, square), "dp")
    mean = total / pixels
    var = square / pixels - mean * mean
    scale = lax.rsqrt(var + 1e-05)
    own_gain = own(gain)
    chooser = (grid_res[:, None] == jnp.arange(2, dtype=jnp.int32)[None, :]).astype(F32)
    sample_bias = jnp.sum(chooser[0][:, None] * own(res_bias, 1), axis=0)
    affine = over_lanes(jnp.stack([mean, own_gain * scale, own(shift) + sample_bias]))
    packed = pack_normed(z, lengths, conv, affine)

    w_in_p, w_in_t = pad_weight(z, after(w_in, packed[0]))
    w_out_t, w_out_p = pad_weight(z, after(w_out.T, packed[0]))
    b_out_p = jnp.pad(b_out.reshape(groups, chan), ((0, 0), (0, z.pad - chan))).reshape(-1, 1)
    weights = (w_in_t, w_in_p, w_out_p, w_out_t, b_in[:, None], b_out_p)

    normed = [exchange(after(packed[0], grad_band))]
    normed.append(exchange(after(packed[1], normed[0], w_in_t, w_out_p)))
    branch, norm1, active1, hidden1 = mlp(0, part, normed[0], grad_band, *weights, None)
    norm_parts = [exchange(after(norm1, normed[1]))]
    branch, norm2, active2, hidden2 = mlp(1, part, normed[1], grad_band, *weights, branch)
    norm_parts.append(exchange(after(norm2, norm_parts[0])))
    core = lax.axis_index("core")
    mine, sent_out = weight_grad(
        core, [(grad_band, start) for start in starts], [active1, after(active2, norm_parts[0])]
    )
    sum_out = HalvingSum((1, 2), mine, sent_out)
    mine, sent_in = weight_grad(
        core, [(value, 0) for value in normed], [hidden1, after(hidden2, sent_out)]
    )
    sum_in = HalvingSum((2, 1), mine, sent_in)
    branch = exchange(after(branch, norm_parts[1], sent_in))
    sum_out.first()
    sum_in.first()

    part_shift, part_gain = norm_sums(z, norm_parts, conv, over_lanes(jnp.stack([mean, scale])))
    small = jnp.concatenate(
        [part_shift[None], part_gain[None], chooser[0][:, None] * part_shift[None], part_b_out[None]],
        axis=0,
    )
    small = lax.psum(small, "dp")
    terms = over_lanes(
        jnp.stack([mean, scale, own_gain * scale, small[0] / pixels, small[1] / pixels])
    )
    calls = pl.cdiv(chan, GROUP)
    cuts = [0, min(2, calls), min(4, calls), calls]
    cuts = [cut for k, cut in enumerate(cuts) if k == 0 or cut > cuts[k - 1]]
    made = conv_gradient(z, cuts[0], cuts[1], terms, norm_parts, conv, x, ntaps, None)
    sum_out.second(made[1])
    sum_in.second(made[1])
    if len(cuts) > 2:
        made = conv_gradient(
            z, cuts[1], cuts[2], after(terms, sum_out.sent, sum_in.sent), norm_parts, conv, x, ntaps, made
        )
    shares = sum_out.share(made[1]), sum_in.share(made[1])
    if len(cuts) > 3:
        made = conv_gradient(
            z, cuts[2], cuts[3], after(terms, *shares), norm_parts, conv, x, ntaps, made
        )
    conv_grad, products = made
    shares = lax.psum(shares, "pair")
    g_kernel = dp_sum(jnp.sum(products, axis=2)[:, :chan])
    x_grad = conv_backward(z, taps, conv_grad, cot, land3)
    sum_out.back_first(after(shares[0], x_grad))
    sum_in.back_first(after(shares[1], x_grad))
    mixed = mix_branch(z, branch, after(x, sum_out.own, sum_in.own), land3)
    sum_out.back_second(mixed)
    sum_in.back_second(mixed)
    rows = jnp.concatenate([after(g_kernel, x_grad, sum_out.own, sum_in.own), small], axis=0)
    gathered = lax.all_gather(rows, CHAN)
    placed = jnp.transpose(gathered, (1, 0, 2)).reshape(rows.shape[0], width)
    g_w_out_t, _ = sum_out.finish(z, placed)
    g_w_in, pieces = sum_in.finish(z, placed)

    return (
        jnp.transpose(mixed, (0, 2, 1))[None],
        jnp.transpose(x_grad, (0, 2, 1))[None],
        placed[:ntaps],
        placed[ntaps + 1],
        placed[ntaps],
        placed[ntaps + 2 : ntaps + 4],
        g_w_in,
        sum_in.first_row(pieces, chan),
        g_w_out_t.T,
        placed[ntaps + 4],
    )


def solution(mesh):
    shape = mesh.shape
    mesh = jax.sharding.Mesh(
        mesh.devices.reshape(shape["dp"], shape["chan"] // CORES, CORES), ("dp",) + CHAN
    )
    cells = P("dp", None, None, CHAN)
    return jax.shard_map(
        per_device,
        mesh=mesh,
        in_specs=(cells, cells, P("dp", None, None), P("dp")) + (P(),) * 8,
        out_specs=(cells, cells) + (P(),) * 8,
        check_vma=False,
    )
```

profile of v0, /device:TPU:0, one launch (start us, length us, event | category | flops | bytes accessed | tf_op | source)
XLA Modules:
  0.0 587.3 jit_solution(11836547644726101046)
XLA Ops:
  7.2 1.6 broadcast_in_dim_squeeze.2.land_ref
  8.8 4.7 copy.60
  13.5 5.0 shard_map.195
  18.5 6.3 %all-to-all-start = ((bf16[8,104,2176]{2,1,0:T(8,128)(2,1)}), bf16[8,104,2176]{2,1,0:T(8,128)(2,1)}, u32[]{:S(2)}, u32[]{:S(2)}) async-start(bf16[8,104,2176]{2,1,0:T(8,128)(2,1)} %bitcast.68), calls=%async_computation | async-start | bytes 7241728 | tf_op jit(solution)/shard_map/all_to_all | solution.py:756
  24.9 4.7 copy.61
  29.7 1.9 broadcast_in_dim.27.taps_ref
  31.6 36.3 %shard_map.196 = (f32[48,104,384]{2,1,0:T(8,128)}, f32[104,128]{1,0:T(8,128)}, f32[104,128]{1,0:T(8,128)}) custom-call(f32[49,104,128]{2,1,0:T(8,128)} %broadcast_in_dim.27.taps_ref, bf16[48,100,360]{2,1,0:T(8,128)(2,1)} %bitcast.55), custom_call_target="tpu_custom_call" | custom-call | flops 10000000000 | bytes 16000000 | tf_op jit(solution)/shard_map/pallas_call | solution.py:276
  70.4 9.9 %all-reduce.5 = (f32[100]{0:T(128)S(1)}, f32[100]{0:T(128)S(1)}) all-reduce(f32[100]{0:T(128)S(1)} %bitcast.83, f32[100]{0:T(128)S(1)} %bitcast.84), channel_id=1, replica_groups=mesh['dp'=4,'pair'=4,'core'=2] {'dp'}, use_global_device_ids=true, to_apply=%region_3.4 | all-reduce | flops 200 | bytes 1600 | tf_op jit(solution)/shard_map/psum | solution.py:865
  83.4 5.9 %shard_map.197 = (bf16[832,1152]{1,0:T(8,128)(2,1)}, bf16[832,1024]{1,0:T(8,128)(2,1)}) custom-call(f32[3,104,128]{2,1,0:T(8,128)} %broadcast_in_dim.28.columns_ref, f32[48,104,384]{2,1,0:T(8,128)} %get-tuple-element.69.conv_ref), custom_call_target="tpu_custom_call" | custom-call | flops 10000000 | bytes 12000000 | tf_op jit(solution)/shard_map/pallas_call | solution.py:310
  89.3 17.4 %all-to-all-done = bf16[8,104,2176]{2,1,0:T(8,128)(2,1)} async-done(((bf16[8,104,2176]{2,1,0:T(8,128)(2,1)}), bf16[8,104,2176]{2,1,0:T(8,128)(2,1)}, u32[]{:S(2)}, u32[]{:S(2)}) %all-to-all-start) | async-done | bytes 3620896 | tf_op jit(solution)/shard_map/all_to_all | solution.py:756
  106.7 3.6 all-to-all-start.1
  110.3 7.9 %shard_map.198 = (bf16[832,3200]{1,0:T(8,128)(2,1)}, bf16[3200,832]{1,0:T(8,128)(2,1)}) custom-call(bf16[800,3200]{1,0:T(8,128)(2,1)} %in_ref), custom_call_target="tpu_custom_call" | custom-call | flops 10000000 | bytes 16000000 | tf_op jit(solution)/shard_map/pallas_call | solution.py:548
  118.2 7.8 %shard_map.199 = (bf16[832,3200]{1,0:T(8,128)(2,1)}, bf16[3200,832]{1,0:T(8,128)(2,1)}) custom-call(bf16[800,3200]{1,0:T(8,128)(2,1)} %bitcast.66), custom_call_target="tpu_custom_call" | custom-call | flops 10000000 | bytes 16000000 | tf_op jit(solution)/shard_map/pallas_call | solution.py:548
  126.0 29.4 %all-to-all-done.1 = bf16[8,104,1152]{2,1,0:T(8,128)(2,1)S(1)} async-done(((bf16[8,104,1152]{2,1,0:T(8,128)(2,1)}), bf16[8,104,1152]{2,1,0:T(8,128)(2,1)S(1)}, u32[]{:S(2)}, u32[]{:S(2)}) %all-to-all-start.1) | async-done | bytes 1916960 | tf_op jit(solution)/shard_map/all_to_all | solution.py:756
  155.4 4.5 all-to-all-start.2
  159.9 1.7 broadcast_in_dim.68.b_in_ref
  162.6 43.3 %shard_map.200 = (bf16[832,2176]{1,0:T(8,128)(2,1)}, bf16[832,1152]{1,0:T(8,128)(2,1)}, bf16[3200,1152]{1,0:T(8,128)(2,1)}, bf16[3200,1152]{1,0:T(8,128)(2,1)}) custom-call(bf16[832,1152]{1,0:T(8,128)(2,1)} %bitcast.70, bf16[832,2176]{1,0:T(8,128)(2,1)} %bitcast.6.g_ref.refs_0_, bf16[3200,832]{1,0:T(8,128)(2,1)} %get-tuple-element.73.w_in_t_ref, ...), custom_call_target="tpu_custom_call" | custom-call | flops 24536678400 | bytes 40000000 | tf_op jit(solution)/shard_map/pallas_call | solution.py:664
  206.0 5.5 all-to-all-start.3
  211.5 37.8 %shard_map.201 = (bf16[832,2176]{1,0:T(8,128)(2,1)}, bf16[832,1024]{1,0:T(8,128)(2,1)}, bf16[3200,1024]{1,0:T(8,128)(2,1)}, bf16[3200,1024]{1,0:T(8,128)(2,1)}) custom-call(bf16[832,1024]{1,0:T(8,128)(2,1)} %bitcast.16.n_ref.refs_1_, bf16[832,2176]{1,0:T(8,128)(2,1)} %bitcast.6.g_ref.refs_0_, ...), custom_call_target="tpu_custom_call", output_to_operand_aliasing={{0}: (8, {})} | custom-call | flops 21810380800 | bytes 40000000 | tf_op jit(solution)/shard_map/pallas_call | solution.py:664
  249.4 7.3 %all-to-all-done.3.rest_0_ = bf16[8,104,1152]{2,1,0:T(8,128)(2,1)S(1)} async-done(((bf16[8,104,1152]{2,1,0:T(8,128)(2,1)}), bf16[8,104,1152]{2,1,0:T(8,128)(2,1)S(1)}, u32[]{:S(2)}, u32[]{:S(2)}) %all-to-all-start.3) | async-done | bytes 1916960 | tf_op jit(solution)/shard_map/all_to_all | solution.py:756
  256.7 21.1 %shard_map.202 = (bf16[416,3200]{1,0:T(8,128)(2,1)}, bf16[416,3200]{1,0:T(8,128)(2,1)}) custom-call(s32[1]{0:T(128)} %bitcast.2.core_ref, bf16[832,2176]{1,0:T(8,128)(2,1)} %bitcast.6.g_ref.refs_0_, bf16[3200,1152]{1,0:T(8,128)(2,1)} %get-tuple-element.78.refs_1_, bf16[3200,1024]{1,0:T(8,128)(2,1)} %get-tuple-element.85.refs_2_), custom_call_target="tpu_custom_call" | custom-call | flops 11586764800 | bytes 24000000 | tf_op jit(solution)/shard_map/pallas_call | solution.py:716
  277.8 20.0 %shard_map.205 = (bf16[416,3200]{1,0:T(8,128)(2,1)}, bf16[416,3200]{1,0:T(8,128)(2,1)}) custom-call(s32[1]{0:T(128)} %bitcast.2.core_ref, bf16[832,1152]{1,0:T(8,128)(2,1)} %bitcast.71, bf16[832,1024]{1,0:T(8,128)(2,1)} %bitcast.16.n_ref.refs_1_, bf16[3200,1152]{1,0:T(8,128)(2,1)} %get-tuple-element.95.refs_2_, bf16[3200,1024]{1,0:T(8,128)(2,1)} %get-tuple-element.97.refs_3_), custom_call_target="tpu_custom_call" | custom-call | flops 11586764800 | bytes 24000000 | tf_op jit(solution)/shard_map/pallas_call | solution.py:716
  298.3 3.6 all-to-all-start.4
  302.1 3.3 add_convert_fusion.1
  305.3 1.5 collective-permute-start.1
  306.9 2.7 add_convert_fusion
  309.6 1.5 collective-permute-start.4
  311.1 31.4 %all-to-all-done.4.rest_1_ = bf16[8,104,1024]{2,1,0:T(8,128)(2,1)S(1)} async-done(((bf16[8,104,1024]{2,1,0:T(8,128)(2,1)}), bf16[8,104,1024]{2,1,0:T(8,128)(2,1)S(1)}, u32[]{:S(2)}, u32[]{:S(2)}) %all-to-all-start.4) | async-done | bytes 1703968 | tf_op jit(solution)/shard_map/all_to_all | solution.py:756
  342.5 1.2 copy-done.3
  343.7 4.5 all-to-all-start.5
  349.0 6.1 %shard_map.203 = (f32[104,128]{1,0:T(8,128)}, f32[104,128]{1,0:T(8,128)}) custom-call(f32[2,104,128]{2,1,0:T(8,128)} %broadcast_in_dim.59.columns_ref, f32[48,104,384]{2,1,0:T(8,128)} %get-tuple-element.69.conv_ref, bf16[832,1152]{1,0:T(8,128)(2,1)} %bitcast.60, bf16[832,1024]{1,0:T(8,128)(2,1)} %bitcast.61), custom_call_target="tpu_custom_call" | custom-call | flops 10000000 | bytes 12000000 | tf_op jit(solution)/shard_map/pallas_call | solution.py:347
  357.0 9.9 %psum.37 = f32[5,100]{1,0:T(8,128)S(1)} all-reduce(f32[5,100]{1,0:T(8,128)S(1)} %pad_maximum_fusion.2), channel_id=1, replica_groups=mesh['dp'=4,'pair'=4,'core'=2] {'dp'}, use_global_device_ids=true, to_apply=%region_8.9 | all-reduce | flops 500 | bytes 4000 | tf_op jit(solution)/shard_map/psum | solution.py:904
  367.8 18.8 %shard_map.204 = (bf16[48,104,384]{2,1,0:T(8,128)(2,1)}, f32[49,104,128]{2,1,0:T(8,128)}) custom-call(f32[5,104,128]{2,1,0:T(8,128)} %broadcast_in_dim.63.columns_ref, f32[48,104,384]{2,1,0:T(8,128)} %get-tuple-element.69.conv_ref, bf16[48,100,360]{2,1,0:T(8,128)(2,1)} %bitcast.56, bf16[8,104,1152]{2,1,0:T(8,128)(2,1)} %copy-done.2, ...), custom_call_target="tpu_custom_call" | custom-call | flops 4000000000 | bytes 10000000 | tf_op jit(solution)/shard_map/pallas_call | solution.py:419
  386.7 1.1 copy-done.12
  387.7 2.4 convert_add_fusion.1
  390.1 1.0 dynamic-slice_convert_fusion.1
  391.7 2.2 convert_add_fusion
  393.8 1.5 copy-done.5
  396.8 18.7 %shard_map.206 = (bf16[48,104,384]{2,1,0:T(8,128)(2,1)}, f32[49,104,128]{2,1,0:T(8,128)}) custom-call(f32[5,104,128]{2,1,0:T(8,128)} %broadcast_in_dim.63.columns_ref, f32[48,104,384]{2,1,0:T(8,128)} %get-tuple-element.69.conv_ref, bf16[48,100,360]{2,1,0:T(8,128)(2,1)} %bitcast.57, ...), custom_call_target="tpu_custom_call", output_to_operand_aliasing={{0}: (5, {}), {1}: (6, {})} | custom-call | flops 4000000000 | bytes 10000000 | tf_op jit(solution)/shard_map/pallas_call | solution.py:419
  415.5 2.4 add_convert_fusion.2
  417.9 23.1 %shard_map.207 = (bf16[48,104,384]{2,1,0:T(8,128)(2,1)}, f32[49,104,128]{2,1,0:T(8,128)}) custom-call(f32[5,104,128]{2,1,0:T(8,128)} %broadcast_in_dim.63.columns_ref, f32[48,104,384]{2,1,0:T(8,128)} %get-tuple-element.69.conv_ref, bf16[48,100,360]{2,1,0:T(8,128)(2,1)} %bitcast.58, ...), custom_call_target="tpu_custom_call", output_to_operand_aliasing={{0}: (5, {}), {1}: (6, {})} | custom-call | flops 4000000000 | bytes 10000000 | tf_op jit(solution)/shard_map/pallas_call | solution.py:419
  441.0 33.8 %shard_map.208 = bf16[48,100,360]{2,1,0:T(8,128)(2,1)} custom-call(f32[49,104,128]{2,1,0:T(8,128)} %broadcast_in_dim.27.taps_ref, bf16[48,104,384]{2,1,0:T(8,128)(2,1)} %get-tuple-element.108.grad_ref, bf16[48,100,360]{2,1,0:T(8,128)(2,1)} %bitcast.64, s32[48,1,360]{2,1,0:T(1,128)} %broadcast_in_dim_squeeze.2.land_ref), custom_call_target="tpu_custom_call" | custom-call | flops 10000000000 | bytes 16000000 | tf_op jit(solution)/shard_map/pallas_call | solution.py:474
  474.8 7.8 %all-reduce.9.cloned.1.call-done = (bf16[104,3200]{1,0:T(8,128)(2,1)}, bf16[104,3200]{1,0:T(8,128)(2,1)}) async-done(((bf16[104,3200]{1,0:T(8,128)(2,1)}, bf16[104,3200]{1,0:T(8,128)(2,1)}), (bf16[104,3200]{1,0:T(8,128)(2,1)}, bf16[104,3200]{1,0:T(8,128)(2,1)})) %all-reduce.9.cloned.1.call-update) | async-done | bytes 1331216 | tf_op jit(solution)/shard_map/psum | solution.py:924
  482.6 1.5 collective-permute-start.10
  484.1 1.5 collective-permute-start.9
  485.5 6.1 %shard_map.209 = bf16[48,100,360]{2,1,0:T(8,128)(2,1)} custom-call(bf16[48,100,360]{2,1,0:T(8,128)(2,1)} %bitcast.59, s32[48,1,360]{2,1,0:T(1,128)} %broadcast_in_dim_squeeze.2.land_ref, bf16[832,2176]{1,0:T(8,128)(2,1)} %bitcast.27.branch_ref), custom_call_target="tpu_custom_call" | custom-call | flops 10000000 | bytes 12000000 | tf_op jit(solution)/shard_map/pallas_call | solution.py:503
  491.6 7.7 %collective-permute-done.10 = bf16[104,3200]{1,0:T(8,128)(2,1)S(1)} collective-permute-done((bf16[104,3200]{1,0:T(8,128)(2,1)}, bf16[104,3200]{1,0:T(8,128)(2,1)S(1)}, u32[]{:S(2)}, u32[]{:S(2)}) %collective-permute-start.10) | collective-permute-done | bytes 665632 | tf_op jit(solution)/shard_map/ppermute | solution.py:785
  499.3 1.2 collective-permute-done.9
  500.6 1.2 pad_maximum_fusion.refs_0_
  501.8 1.0 collective-permute-start.14
  502.8 1.2 broadcast_select_fusion.1
  504.0 1.2 pad_maximum_fusion.1.refs_0_
  505.2 1.5 collective-permute-start.11
  507.6 1.1 collective-permute-start.6
  509.2 1.9 collective-permute-start.8
  511.1 21.4 %collective-permute-done.6 = f32[49,100]{1,0:T(8,128)S(1)} collective-permute-done((f32[49,100]{1,0:T(8,128)S(1)}, f32[49,100]{1,0:T(8,128)S(1)}, u32[]{:S(2)}, u32[]{:S(2)}) %collective-permute-start.6) | collective-permute-done | bytes 19632 | tf_op jit(solution)/shard_map/ppermute | solution.py:767
  532.5 3.7 collective-permute-done.7
  536.3 14.5 %all-gather.1 = f32[8,54,100]{2,1,0:T(8,128)S(1)} all-gather(f32[1,54,100]{2,1,0:T(8,128)S(1)} %maximum_bitcast_fusion), channel_id=2, replica_groups=mesh['dp'=4,'pair'=4,'core'=2] {'pair','core'}, dimensions={0}, use_global_device_ids=true | all-gather | bytes 194400 | tf_op jit(solution)/shard_map/all_gather | solution.py:933
  551.7 4.4 copy.57
  559.7 4.4 copy.56
  564.1 6.8 %shard_map.211 = f32[800,3200]{1,0:T(8,128)} custom-call(s32[1]{0:T(128)} %bitcast.35.place_ref, bf16[208,3200]{1,0:T(8,128)(2,1)} %pad_maximum_fusion.refs_0_, bf16[208,3200]{1,0:T(8,128)(2,1)} %collective-permute-done.14.refs_1_, bf16[208,3200]{1,0:T(8,128)(2,1)} %collective-permute-done.15.refs_2_, bf16[208,3200]{1,0:T(8,128)(2,1)} %collective-permute-done.16.refs_3_), custom_call_target="tpu_custom_call" | custom-call | flops 10000000 | bytes 16000000 | tf_op jit(solution)/shard_map/pallas_call | solution.py:744
  570.9 1.1 copy-done.11
  571.9 6.8 %shard_map.210 = f32[800,3200]{1,0:T(8,128)} custom-call(s32[1]{0:T(128)} %bitcast.34.place_ref, bf16[208,3200]{1,0:T(8,128)(2,1)} %pad_maximum_fusion.1.refs_0_, bf16[208,3200]{1,0:T(8,128)(2,1)} %collective-permute-done.11.refs_1_, bf16[208,3200]{1,0:T(8,128)(2,1)} %copy-done.11, bf16[208,3200]{1,0:T(8,128)(2,1)} %collective-permute-done.13.refs_3_), custom_call_target="tpu_custom_call" | custom-call | flops 10000000 | bytes 16000000 | tf_op jit(solution)/shard_map/pallas_call | solution.py:744
  578.7 1.5 fusion.1
  (101 shorter events, 18.4 us)
Async XLA Ops:
  7.2 22.4 %copy-start = (bf16[49,800]{1,0:T(8,128)(2,1)S(1)}, bf16[49,800]{1,0:T(8,128)(2,1)}, u32[]{:S(2)}) copy-start(bf16[49,800]{1,0:T(8,128)(2,1)} %param.16) | copy-start | bytes 235204
  18.5 88.2 %all-to-all-start = ((bf16[8,104,2176]{2,1,0:T(8,128)(2,1)}), bf16[8,104,2176]{2,1,0:T(8,128)(2,1)}, u32[]{:S(2)}, u32[]{:S(2)}) async-start(bf16[8,104,2176]{2,1,0:T(8,128)(2,1)} %bitcast.68), calls=%async_computation | async-start | bytes 7241728 | tf_op jit(solution)/shard_map/all_to_all | solution.py:756
  106.7 48.7 %all-to-all-start.1 = ((bf16[8,104,1152]{2,1,0:T(8,128)(2,1)}), bf16[8,104,1152]{2,1,0:T(8,128)(2,1)S(1)}, u32[]{:S(2)}, u32[]{:S(2)}) async-start(bf16[8,104,1152]{2,1,0:T(8,128)(2,1)} %bitcast.73), calls=%async_computation.1 | async-start | bytes 3833856 | tf_op jit(solution)/shard_map/all_to_all | solution.py:756
  126.0 33.9 %copy-start.17 = (f32[3200]{0:T(1024)S(1)}, f32[3200]{0:T(1024)}, u32[]{:S(2)}) copy-start(f32[3200]{0:T(1024)} %param.21) | copy-start | bytes 38404
  126.0 35.6 %copy-start.18 = (f32[800]{0:T(1024)S(1)}, f32[800]{0:T(1024)}, u32[]{:S(2)}) copy-start(f32[800]{0:T(1024)} %param.23) | copy-start | bytes 9604
  155.4 7.2 %copy-start.10 = (bf16[8,104,1152]{2,1,0:T(8,128)(2,1)}, bf16[8,104,1152]{2,1,0:T(8,128)(2,1)S(1)}, u32[]{:S(2)}) copy-start(bf16[8,104,1152]{2,1,0:T(8,128)(2,1)S(1)} %all-to-all-done.1) | copy-start | bytes 5750788
  155.4 50.6 %all-to-all-start.2 = ((bf16[8,104,1024]{2,1,0:T(8,128)(2,1)}), bf16[8,104,1024]{2,1,0:T(8,128)(2,1)}, u32[]{:S(2)}, u32[]{:S(2)}) async-start(bf16[8,104,1024]{2,1,0:T(8,128)(2,1)} %bitcast.74), calls=%async_computation.2 | async-start | bytes 3407872 | tf_op jit(solution)/shard_map/all_to_all | solution.py:756
  206.0 50.7 %all-to-all-start.3 = ((bf16[8,104,1152]{2,1,0:T(8,128)(2,1)}), bf16[8,104,1152]{2,1,0:T(8,128)(2,1)S(1)}, u32[]{:S(2)}, u32[]{:S(2)}) async-start(bf16[8,104,1152]{2,1,0:T(8,128)(2,1)} %bitcast.72), calls=%async_computation.3 | async-start | bytes 3833856 | tf_op jit(solution)/shard_map/all_to_all | solution.py:756
  256.7 21.1 %copy-start.2 = (bf16[8,104,1152]{2,1,0:T(8,128)(2,1)}, bf16[8,104,1152]{2,1,0:T(8,128)(2,1)S(1)}, u32[]{:S(2)}) copy-start(bf16[8,104,1152]{2,1,0:T(8,128)(2,1)S(1)} %all-to-all-done.3.rest_0_) | copy-start | bytes 5750788
  277.8 24.3 %collective-permute-start = (bf16[416,3200]{1,0:T(8,128)(2,1)}, bf16[416,3200]{1,0:T(8,128)(2,1)}, u32[]{:S(2)}, u32[]{:S(2)}) collective-permute-start(bf16[416,3200]{1,0:T(8,128)(2,1)} %get-tuple-element.87), channel_id=1, source_target_pairs={{0,1},{1,0},{2,3},{3,2},{4,5},{5,4},{6,7},{7,6},{8,9},{9,8},{10,11... | collective-permute-start | bytes 7987208 | tf_op jit(solution)/shard_map/ppermute | solution.py:772
  297.8 4.1 copy-start.16
  297.8 9.0 %collective-permute-start.3 = (bf16[416,3200]{1,0:T(8,128)(2,1)}, bf16[416,3200]{1,0:T(8,128)(2,1)}, u32[]{:S(2)}, u32[]{:S(2)}) collective-permute-start(bf16[416,3200]{1,0:T(8,128)(2,1)} %get-tuple-element.99), channel_id=1, source_target_pairs={{0,1},{1,0},{2,3},{3,2},{4,5},{5,4},{6,7},{7,6},{8,9},{9,8},{10,11... | collective-permute-start | bytes 7987208 | tf_op jit(solution)/shard_map/ppermute | solution.py:772
  298.3 44.2 %all-to-all-start.4 = ((bf16[8,104,1024]{2,1,0:T(8,128)(2,1)}), bf16[8,104,1024]{2,1,0:T(8,128)(2,1)S(1)}, u32[]{:S(2)}, u32[]{:S(2)}) async-start(bf16[8,104,1024]{2,1,0:T(8,128)(2,1)} %bitcast.20), calls=%async_computation.4 | async-start | bytes 3407872 | tf_op jit(solution)/shard_map/all_to_all | solution.py:756
  302.0 4.8 copy-start.8
  305.3 81.3 %collective-permute-start.1 = (bf16[208,3200]{1,0:T(8,128)(2,1)}, bf16[208,3200]{1,0:T(8,128)(2,1)S(1)}, u32[]{:S(2)}, u32[]{:S(2)}) collective-permute-start(bf16[208,3200]{1,0:T(8,128)(2,1)} %add_convert_fusion.1), channel_id=1, source_target_pairs={{0,8},{8,0},{16,24},{24,16},{1,9},{9,1},{17,25},{25,17},{2,10},{10... | collective-permute-start | bytes 3993608 | tf_op jit(solution)/shard_map/ppermute | solution.py:785
  309.6 78.2 %collective-permute-start.4 = (bf16[208,3200]{1,0:T(8,128)(2,1)}, bf16[208,3200]{1,0:T(8,128)(2,1)}, u32[]{:S(2)}, u32[]{:S(2)}) collective-permute-start(bf16[208,3200]{1,0:T(8,128)(2,1)} %add_convert_fusion), channel_id=1, source_target_pairs={{0,16},{8,24},{16,0},{24,8},{1,17},{9,25},{17,1},{25,9},{2,18},{10... | collective-permute-start | bytes 3993608 | tf_op jit(solution)/shard_map/ppermute | solution.py:785
  342.5 1.2 copy-start.3
  343.7 141.9 %all-to-all-start.5 = ((bf16[8,104,2176]{2,1,0:T(8,128)(2,1)}), bf16[8,104,2176]{2,1,0:T(8,128)(2,1)}, u32[]{:S(2)}, u32[]{:S(2)}) async-start(bf16[8,104,2176]{2,1,0:T(8,128)(2,1)} %bitcast.69), calls=%async_computation.5 | async-start | bytes 7241728 | tf_op jit(solution)/shard_map/all_to_all | solution.py:756
  348.2 134.4 %all-reduce.9.cloned.1.call-start = ((), (), s32[]{:S(2)}) async-start(), calls=%async_computation.6 | async-start | bytes 2662400 | tf_op jit(solution)/shard_map/psum | solution.py:924
  367.8 19.9 %copy-start.7 = (bf16[416,3200]{1,0:T(8,128)(2,1)S(1)}, bf16[416,3200]{1,0:T(8,128)(2,1)}, u32[]{:S(2)}) copy-start(bf16[416,3200]{1,0:T(8,128)(2,1)} %get-tuple-element.86) | copy-start | bytes 7987204
  386.7 1.1 copy-start.12
  387.7 4.0 copy-start.9
  391.1 24.3 %collective-permute-start.2 = (bf16[104,3200]{1,0:T(8,128)(2,1)}, bf16[104,3200]{1,0:T(8,128)(2,1)S(1)}, u32[]{:S(2)}, u32[]{:S(2)}) collective-permute-start(bf16[104,3200]{1,0:T(8,128)(2,1)} %dynamic-slice_convert_fusion.1), channel_id=1, source_target_pairs={{0,16},{8,24},{16,0},{24,8},{1,17},{9,25},{17,1},{25,9},{2,18},{10... | collective-permute-start | bytes 1996808 | tf_op jit(solution)/shard_map/ppermute | solution.py:785
  393.8 1.5 copy-start.5
  396.3 19.2 %collective-permute-start.5 = (bf16[104,3200]{1,0:T(8,128)(2,1)}, bf16[104,3200]{1,0:T(8,128)(2,1)}, u32[]{:S(2)}, u32[]{:S(2)}) collective-permute-start(bf16[104,3200]{1,0:T(8,128)(2,1)} %dynamic-slice_convert_fusion), channel_id=1, source_target_pairs={{0,8},{8,0},{16,24},{24,16},{1,9},{9,1},{17,25},{25,17},{2,10},{10... | collective-permute-start | bytes 1996808 | tf_op jit(solution)/shard_map/ppermute | solution.py:785
  396.8 18.7 %copy-start.6 = (f32[208,3200]{1,0:T(8,128)S(1)}, f32[208,3200]{1,0:T(8,128)}, u32[]{:S(2)}) copy-start(f32[208,3200]{1,0:T(8,128)} %copy-done.5) | copy-start | bytes 7987204
  482.6 16.7 %collective-permute-start.10 = (bf16[104,3200]{1,0:T(8,128)(2,1)}, bf16[104,3200]{1,0:T(8,128)(2,1)S(1)}, u32[]{:S(2)}, u32[]{:S(2)}) collective-permute-start(bf16[104,3200]{1,0:T(8,128)(2,1)} %get-tuple-element.110), channel_id=1, source_target_pairs={{0,8},{8,0},{16,24},{24,16},{1,9},{9,1},{17,25},{25,17},{2,10},{10... | collective-permute-start | bytes 1996808 | tf_op jit(solution)/shard_map/ppermute | solution.py:785
  484.1 16.4 %collective-permute-start.9 = (bf16[104,3200]{1,0:T(8,128)(2,1)}, bf16[104,3200]{1,0:T(8,128)(2,1)S(1)}, u32[]{:S(2)}, u32[]{:S(2)}) collective-permute-start(bf16[104,3200]{1,0:T(8,128)(2,1)} %get-tuple-element.109), channel_id=1, source_target_pairs={{0,16},{8,24},{16,0},{24,8},{1,17},{9,25},{17,1},{25,9},{2,18},{10... | collective-permute-start | bytes 1996808 | tf_op jit(solution)/shard_map/ppermute | solution.py:785
  485.5 15.0 %copy-start.14 = (bf16[104,3200]{1,0:T(8,128)(2,1)S(1)}, bf16[104,3200]{1,0:T(8,128)(2,1)}, u32[]{:S(2)}) copy-start(bf16[104,3200]{1,0:T(8,128)(2,1)} %get-tuple-element.109) | copy-start | bytes 1996804
  491.6 11.2 %copy-start.13 = (bf16[104,3200]{1,0:T(8,128)(2,1)S(1)}, bf16[104,3200]{1,0:T(8,128)(2,1)}, u32[]{:S(2)}) copy-start(bf16[104,3200]{1,0:T(8,128)(2,1)} %get-tuple-element.110) | copy-start | bytes 1996804
  499.3 1.3 copy-start.15
  501.8 4.9 copy-start.4
  501.8 49.1 %collective-permute-start.14 = (bf16[208,3200]{1,0:T(8,128)(2,1)}, bf16[208,3200]{1,0:T(8,128)(2,1)}, u32[]{:S(2)}, u32[]{:S(2)}) collective-permute-start(bf16[208,3200]{1,0:T(8,128)(2,1)} %pad_maximum_fusion.refs_0_), channel_id=1, source_target_pairs={{0,8},{8,0},{16,24},{24,16},{1,9},{9,1},{17,25},{25,17},{2,10},{10... | collective-permute-start | bytes 3993608 | tf_op jit(solution)/shard_map/ppermute | solution.py:785
  505.2 46.2 %collective-permute-start.11 = (bf16[208,3200]{1,0:T(8,128)(2,1)}, bf16[208,3200]{1,0:T(8,128)(2,1)}, u32[]{:S(2)}, u32[]{:S(2)}) collective-permute-start(bf16[208,3200]{1,0:T(8,128)(2,1)} %pad_maximum_fusion.1.refs_0_), channel_id=1, source_target_pairs={{0,16},{8,24},{16,0},{24,8},{1,17},{9,25},{17,1},{25,9},{2,18},{10... | collective-permute-start | bytes 3993608 | tf_op jit(solution)/shard_map/ppermute | solution.py:785
  507.6 24.9 %collective-permute-start.6 = (f32[49,100]{1,0:T(8,128)S(1)}, f32[49,100]{1,0:T(8,128)S(1)}, u32[]{:S(2)}, u32[]{:S(2)}) collective-permute-start(f32[49,100]{1,0:T(8,128)S(1)} %bitcast.78), channel_id=1, source_target_pairs={{0,8},{8,0},{16,24},{24,16},{1,9},{9,1},{17,25},{25,17},{2,10},{10... | collective-permute-start | bytes 58808 | tf_op jit(solution)/shard_map/ppermute | solution.py:767
  508.6 27.6 %collective-permute-start.7 = (f32[49,100]{1,0:T(8,128)S(1)}, f32[49,100]{1,0:T(8,128)S(1)}, u32[]{:S(2)}, u32[]{:S(2)}) collective-permute-start(f32[49,100]{1,0:T(8,128)S(1)} %bitcast.79), channel_id=1, source_target_pairs={{0,16},{8,24},{16,0},{24,8},{1,17},{9,25},{17,1},{25,9},{2,18},{10... | collective-permute-start | bytes 58808 | tf_op jit(solution)/shard_map/ppermute | solution.py:767
  509.2 27.0 %collective-permute-start.8 = (f32[49,100]{1,0:T(8,128)S(1)}, f32[49,100]{1,0:T(8,128)S(1)}, u32[]{:S(2)}, u32[]{:S(2)}) collective-permute-start(f32[49,100]{1,0:T(8,128)S(1)} %bitcast.80), channel_id=1, source_target_pairs={{0,24},{8,16},{16,8},{24,0},{1,25},{9,17},{17,9},{25,1},{2,26},{10... | collective-permute-start | bytes 58808 | tf_op jit(solution)/shard_map/ppermute | solution.py:767
  536.2 27.9 %collective-permute-start.15 = (bf16[208,3200]{1,0:T(8,128)(2,1)}, bf16[208,3200]{1,0:T(8,128)(2,1)}, u32[]{:S(2)}, u32[]{:S(2)}) collective-permute-start(bf16[208,3200]{1,0:T(8,128)(2,1)} %pad_maximum_fusion.refs_0_), channel_id=1, source_target_pairs={{0,1},{1,0},{2,3},{3,2},{4,5},{5,4},{6,7},{7,6},{8,9},{9,8},{10,11... | collective-permute-start | bytes 3993608 | tf_op jit(solution)/shard_map/ppermute | solution.py:772
  550.9 13.2 %collective-permute-start.16 = (bf16[208,3200]{1,0:T(8,128)(2,1)}, bf16[208,3200]{1,0:T(8,128)(2,1)}, u32[]{:S(2)}, u32[]{:S(2)}) collective-permute-start(bf16[208,3200]{1,0:T(8,128)(2,1)} %collective-permute-done.14.refs_1_), channel_id=1, source_target_pairs={{0,1},{1,0},{2,3},{3,2},{4,5},{5,4},{6,7},{7,6},{8,9},{9,8},{10,11... | collective-permute-start | bytes 3993608 | tf_op jit(solution)/shard_map/ppermute | solution.py:772
  551.2 19.7 %collective-permute-start.12 = (bf16[208,3200]{1,0:T(8,128)(2,1)}, bf16[208,3200]{1,0:T(8,128)(2,1)S(1)}, u32[]{:S(2)}, u32[]{:S(2)}) collective-permute-start(bf16[208,3200]{1,0:T(8,128)(2,1)} %pad_maximum_fusion.1.refs_0_), channel_id=1, source_target_pairs={{0,1},{1,0},{2,3},{3,2},{4,5},{5,4},{6,7},{7,6},{8,9},{9,8},{10,11... | collective-permute-start | bytes 3993608 | tf_op jit(solution)/shard_map/ppermute | solution.py:772
  551.4 19.5 %collective-permute-start.13 = (bf16[208,3200]{1,0:T(8,128)(2,1)}, bf16[208,3200]{1,0:T(8,128)(2,1)}, u32[]{:S(2)}, u32[]{:S(2)}) collective-permute-start(bf16[208,3200]{1,0:T(8,128)(2,1)} %collective-permute-done.11.refs_1_), channel_id=1, source_target_pairs={{0,1},{1,0},{2,3},{3,2},{4,5},{5,4},{6,7},{7,6},{8,9},{9,8},{10,11... | collective-permute-start | bytes 3993608 | tf_op jit(solution)/shard_map/ppermute | solution.py:772
  570.9 1.1 copy-start.11
  571.9 8.3 %copy-start.1 = (bf16[49,800]{1,0:T(8,128)(2,1)S(1)}, bf16[49,800]{1,0:T(8,128)(2,1)}, u32[]{:S(2)}) copy-start(bf16[49,800]{1,0:T(8,128)(2,1)} %param.16) | copy-start | bytes 235204
Sparse Core Ops, SparseCore 0:
  418.0 64.5 all-reduce.8
where the time goes:
time: 594 us; the launch traced here: 587 us
  Pallas kernels  305 us (51%)
  waiting for transfers between devices  127 us (21%)
  starting transfers between devices  42.6 us (7%)
  local copies, waits for them, and re-layouts  37.4 us (6%)
  blocking collectives  34.4 us (6%)
  other arithmetic  25.2 us (4%)
  between operations  15.3 us (3%)
    all_to_all x6, waiting for transfers between devices, exchange(): return lax.all_to_all(value, CHAN, split_axis=0, concat_axis=0, tiled=True)  85.5 us
    pallas_call x2, Pallas kernels, mlp(): pl.pallas_call(kernel, grid=(blocks + outs,), in_specs=in_specs, out_spec...  81.2 us
    pallas_call x3, Pallas kernels, conv_gradient(): pl.pallas_call(kernel, grid=(end - begin,), in_specs=[group((5, GROUP, LA...  60.6 us
    pallas_call x2, Pallas kernels, weight_grad(): pl.pallas_call(kernel, grid=(hidden // block,), in_specs=[smem()] + [whol...  41.1 us
    pallas_call x1, Pallas kernels, conv_forward(): pl.pallas_call(kernel, grid=(pl.cdiv(z.chan, GROUP),), in_specs=[group_la...  36.3 us
    pallas_call x1, Pallas kernels, conv_backward(): pl.pallas_call(kernel, grid=(pl.cdiv(z.chan, GROUP),), in_specs=[group_la...  33.8 us
    all_to_all x6, starting transfers between devices, exchange(): return lax.all_to_all(value, CHAN, split_axis=0, concat_axis=0, tiled=True)  28 us
    ppermute x3, waiting for transfers between devices, dp_sum(): lax.ppermute(value, 'dp', [(i, i ^ turn) for i in range(ways)])  25.1 us
  transfers between devices with their start and end apart: 24, of which 9 were waited for; matrix products, arithmetic and copies ran while one was open for 8% of the time, Pallas kernels for 46%

commit v1 on v0

--- a/solution.py
+++ b/solution.py
@@ -575,23 +575,22 @@
     packed, cells = normed.shape
     hidden = w_in_t.shape[0]
     block = block_of(hidden, 640)
-    inner = row_step(block, 320)
+    slices = 4
+    inner, rows = block // slices, packed // slices
     blocks = hidden // block
-    pairs = block // inner // 2
-    rows = row_step(packed, 416)
-    outs = packed // rows
 
     def kernel(
         n_ref, g_ref, w_in_t_ref, w_in_ref, w_out_ref, w_out_t_ref, b_in_ref, b_out_ref, *rest
     ):
         (
             branch_ref, norm_ref, active_out, hidden_out,
-            h_0, h_1, back_0, back_1, active, grads, sems,
-        ) = rest[-11:]
+            h_0, h_1, back_0, back_1, active, grads, branch_acc, norm_acc, sems,
+        ) = rest[-13:]
         step = pl.program_id(0)
-
-        def products(k, h, back):
-            at = pl.ds(k * inner, inner)
+        buffers = ((h_0, back_0), (h_1, back_1))
+
+        def products_in(q, h, back):
+            at = pl.ds(pl.multiple_of(q * inner, inner), inner)
             h[...] = (
                 jnp.dot(w_in_t_ref[at, :], n_ref[...], preferred_element_type=F32) + b_in_ref[at, :]
             )
@@ -603,39 +602,53 @@
             active[at, :] = value.astype(BF16)
             grads[at, :] = (back[...] * slope).astype(BF16)
 
-        @pl.when(step < blocks)
+        def products_out(q):
+            at = pl.ds(pl.multiple_of(q * rows, rows), rows)
+            block_at = pl.ds(pl.multiple_of((step - 2) * block, block), block)
+            branch_acc[at, :] += jnp.dot(
+                w_out_t_ref[at, :], active[block_at, :], preferred_element_type=F32
+            )
+            norm_acc[at, :] += jnp.dot(
+                w_in_ref[at, :], grads[block_at, :], preferred_element_type=F32
+            )
+
+        def loop(enter, leave):
+            def body(i, carry):
+                for turn in range(2):
+                    q = 2 * i + turn
+                    if leave:
+                        products_out(q)
+                    if enter:
+                        products_in(q, *buffers[turn])
+                        gelu(step * slices + q - 1, *buffers[1 - turn])
+                return carry
+
+            lax.fori_loop(0, slices // 2, body, 0)
+
+        @pl.when(step == 0)
         def _():
-            first = step * (2 * pairs)
-
-            def body(i, carry):
-                products(2 * i, h_0, back_0)
-                gelu(first + 2 * i - 1, h_1, back_1)
-                products(2 * i + 1, h_1, back_1)
-                gelu(first + 2 * i, h_0, back_0)
-                return carry
-
-            lax.fori_loop(0, pairs, body, 0)
+            branch_acc[...] = jnp.broadcast_to(b_out_ref[...], branch_acc.shape)
+            norm_acc[...] = jnp.zeros_like(norm_acc)
 
         copies = [
             pltpu.make_async_copy(active, active_out, sems.at[0]),
             pltpu.make_async_copy(grads, hidden_out, sems.at[1]),
         ]
+        pl.when(step < 2)(lambda: loop(True, False))
+        pl.when((step >= 2) & (step < blocks))(lambda: loop(True, True))
 
         @pl.when(step == blocks)
         def _():
-            gelu(2 * pairs * blocks - 1, h_1, back_1)
+            gelu(slices * blocks - 1, *buffers[1])
             for copy in copies:
                 copy.start()
 
-        @pl.when(step >= blocks)
+        pl.when(step >= blocks)(lambda: loop(False, True))
+
+        @pl.when(step == blocks + 1)
         def _():
-            branch = jnp.dot(w_out_t_ref[...], active[...], preferred_element_type=F32)
-            branch_ref[:, :cells] = (branch + b_out_ref[...]).astype(BF16)
-            norm = jnp.dot(w_in_ref[...], grads[...], preferred_element_type=F32)
-            norm_ref[...] = norm.astype(BF16)
-
-        @pl.when(step == blocks + outs - 1)
-        def _():
+            branch_ref[:, :cells] = branch_acc[...].astype(BF16)
+            norm_ref[...] = norm_acc[...].astype(BF16)
             for copy in copies:
                 copy.wait()
 
@@ -643,41 +656,36 @@
         return jnp.minimum(f, blocks - 1)
 
     def at_out(f):
-        return jnp.maximum(f - blocks, 0)
+        return jnp.maximum(f - 2, 0)
 
     tall_block = pl.BlockSpec((block, packed), lambda f: (at_in(f), 0))
-    wide_block = pl.BlockSpec((rows, hidden), lambda f: (at_out(f), 0))
+    wide_block = pl.BlockSpec((packed, block), lambda f: (0, at_out(f)))
     anywhere = pl.BlockSpec(memory_space=pl.ANY)
     operands = [normed, out_grad, w_in_t, w_in, w_out, w_out_t, b_in, b_out]
     in_specs = [
         whole((packed, cells)), lane_block(packed, length, part),
         tall_block, wide_block, tall_block, wide_block,
-        pl.BlockSpec((block, 1), lambda f: (at_in(f), 0)),
-        pl.BlockSpec((rows, 1), lambda f: (at_out(f), 0)),
+        pl.BlockSpec((block, 1), lambda f: (at_in(f), 0)), whole((packed, 1)),
     ]
     aliases = {}
     if branch_all is not None:
         aliases = {len(operands): 0}
         operands.append(branch_all)
         in_specs.append(anywhere)
-    buffer = pltpu.VMEM((inner, cells), F32)
     return pl.pallas_call(
         kernel,
-        grid=(blocks + outs,),
+        grid=(blocks + 2,),
         in_specs=in_specs,
-        out_specs=[
-            pl.BlockSpec((rows, length), lambda f: (at_out(f), part)),
-            pl.BlockSpec((rows, cells), lambda f: (at_out(f), 0)),
-            anywhere, anywhere,
-        ],
+        out_specs=[lane_block(packed, length, part), whole((packed, cells)), anywhere, anywhere],
         out_shape=[
             jax.ShapeDtypeStruct(out_grad.shape, BF16),
             jax.ShapeDtypeStruct((packed, cells), BF16),
             jax.ShapeDtypeStruct((hidden, cells), BF16),
             jax.ShapeDtypeStruct((hidden, cells), BF16),
         ],
-        scratch_shapes=[buffer] * 4
+        scratch_shapes=[pltpu.VMEM((inner, cells), F32)] * 4
         + [pltpu.VMEM((hidden, cells), BF16)] * 2
+        + [pltpu.VMEM((packed, cells), F32)] * 2
         + [pltpu.SemaphoreType.DMA((2,))],
         input_output_aliases=aliases,
         compiler_params=params(),
@@ -791,7 +799,8 @@
             F32
         ) + lax.dynamic_slice_in_dim(self.other, at, rows, 0).astype(F32)
 
-    def first(self):
+    def first(self, ready):
+        self.mine = after(self.mine, ready)
         self.arrived = self.meet(self.pair(1 - self.bits[0]).astype(BF16), self.turns[0])
 
     def second(self, ready):
@@ -893,8 +902,8 @@
     )
     sum_in = HalvingSum((2, 1), mine, sent_in)
     branch = exchange(after(branch, norm_parts[1], sent_in))
-    sum_out.first()
-    sum_in.first()
+    sum_out.first(norm_parts[1])
+    sum_in.first(norm_parts[1])
 
     part_shift, part_gain = norm_sums(z, norm_parts, conv, over_lanes(jnp.stack([mean, scale])))
     small = jnp.concatenate(
@@ -926,18 +935,20 @@
     x_grad = conv_backward(z, taps, conv_grad, cot, land3)
     sum_out.back_first(after(shares[0], x_grad))
     sum_in.back_first(after(shares[1], x_grad))
-    mixed = mix_branch(z, branch, after(x, sum_out.own, sum_in.own), land3)
-    sum_out.back_second(mixed)
-    sum_in.back_second(mixed)
-    rows = jnp.concatenate([after(g_kernel, x_grad, sum_out.own, sum_in.own), small], axis=0)
+    rows = jnp.concatenate([after(g_kernel, sum_out.own, sum_in.own), small], axis=0)
     gathered = lax.all_gather(rows, CHAN)
     placed = jnp.transpose(gathered, (1, 0, 2)).reshape(rows.shape[0], width)
-    g_w_out_t, _ = sum_out.finish(z, placed)
-    g_w_in, pieces = sum_in.finish(z, placed)
+    sum_out.back_second(gathered)
+    sum_in.back_second(gathered)
+    mixed = mix_branch(z, branch, after(x, sum_out.own, sum_in.own), land3)
+    mixed_out = jnp.transpose(mixed, (0, 2, 1))[None]
+    x_grad_out = jnp.transpose(after(x_grad, sum_out.own, sum_in.own), (0, 2, 1))[None]
+    g_w_out_t, _ = sum_out.finish(z, mixed)
+    g_w_in, pieces = sum_in.finish(z, mixed)
 
     return (
-        jnp.transpose(mixed, (0, 2, 1))[None],
-        jnp.transpose(x_grad, (0, 2, 1))[None],
+        mixed_out,
+        x_grad_out,
         placed[:ntaps],
         placed[ntaps + 1],
         placed[ntaps],

time: 594 us -> 657 us (1.11)
  Pallas kernels: 305 us -> 333 us
  waiting for transfers between devices: 127 us -> 151 us
  blocking collectives: 34.4 us -> 46.6 us
    psum x1, waiting for transfers between devices: 7.75 us -> 47.1 us  [per_device(): shares = lax.psum(shares, 'pair')]
    pallas_call x2, Pallas kernels: 81.2 us -> 109 us  [mlp(): pl.pallas_call(kernel, grid=(blocks + 2,), in_specs=in_specs, out_specs=[...]
    all_to_all x6, waiting for transfers between devices: 85.5 us -> 66.7 us  [exchange(): return lax.all_to_all(value, CHAN, split_axis=0, concat_axis=0, tiled=True)]
    ppermute x8, waiting for transfers between devices: 8.88 us -> 23.7 us  [meet(): return lax.ppermute(value, 'dp', [(i, i ^ turn) for i in range(ways)])]
    ppermute x3, waiting for transfers between devices: 25.1 us -> 13 us  [dp_sum(): lax.ppermute(value, 'dp', [(i, i ^ turn) for i in range(ways)])]
    psum x1, blocking collectives: 9.91 us -> 21.4 us  [per_device(): small = lax.psum(small, 'dp')]
  transfers between devices with their start and end apart: 24 -> 24, of which waited for: 9 -> 8; matrix products, arithmetic and copies ran while one was open for 8% -> 7% of each run, Pallas kernels for 46% -> 46%
where the time goes in v1:
time: 657 us; the launch traced here: 650 us
  Pallas kernels  333 us (51%)
  waiting for transfers between devices  151 us (23%)
  blocking collectives  46.6 us (7%)
  starting transfers between devices  43.8 us (7%)
  local copies, waits for them, and re-layouts  37.3 us (6%)
  other arithmetic  24.2 us (4%)
  between operations  15.2 us (2%)
    pallas_call x2, Pallas kernels, mlp(): pl.pallas_call(kernel, grid=(blocks + 2,), in_specs=in_specs, out_specs=[...  109 us
    all_to_all x6, waiting for transfers between devices, exchange(): return lax.all_to_all(value, CHAN, split_axis=0, concat_axis=0, tiled=True)  66.7 us
    pallas_call x3, Pallas kernels, conv_gradient(): pl.pallas_call(kernel, grid=(end - begin,), in_specs=[group((5, GROUP, LA...  60.4 us
    psum x1, waiting for transfers between devices, per_device(): shares = lax.psum(shares, 'pair')  47.1 us
    pallas_call x2, Pallas kernels, weight_grad(): pl.pallas_call(kernel, grid=(hidden // block,), in_specs=[smem()] + [whol...  41.1 us
    pallas_call x1, Pallas kernels, conv_forward(): pl.pallas_call(kernel, grid=(pl.cdiv(z.chan, GROUP),), in_specs=[group_la...  36.3 us
    pallas_call x1, Pallas kernels, conv_backward(): pl.pallas_call(kernel, grid=(pl.cdiv(z.chan, GROUP),), in_specs=[group_la...  34 us
    all_to_all x6, starting transfers between devices, exchange(): return lax.all_to_all(value, CHAN, split_axis=0, concat_axis=0, tiled=True)  29.5 us
  transfers between devices with their start and end apart: 24, of which 8 were waited for; matrix products, arithmetic and copies ran while one was open for 7% of the time, Pallas kernels for 46%

profile of v1, /device:TPU:0, one launch (start us, length us, event | category | flops | bytes accessed | tf_op | source)
XLA Modules:
  0.0 650.3 jit_solution(13213871912802460203)
XLA Ops:
  7.2 1.6 broadcast_in_dim_squeeze.2.land_ref
  8.8 4.7 copy.59
  13.5 5.0 shard_map.195
  18.5 6.3 all-to-all-start
  24.9 4.7 copy.60
  29.7 1.9 broadcast_in_dim.27.taps_ref
  31.6 36.3 %shard_map.196 = (f32[48,104,384]{2,1,0:T(8,128)}, f32[104,128]{1,0:T(8,128)}, f32[104,128]{1,0:T(8,128)}) custom-call(f32[49,104,128]{2,1,0:T(8,128)} %broadcast_in_dim.27.taps_ref, bf16[48,100,360]{2,1,0:T(8,128)(2,1)} %bitcast.55), custom_call_target="tpu_custom_call" | custom-call | flops 10000000000 | bytes 16000000 | tf_op jit(solution)/shard_map/pallas_call | solution.py:276
  70.4 9.9 %all-reduce.5 = (f32[100]{0:T(128)S(1)}, f32[100]{0:T(128)S(1)}) all-reduce(f32[100]{0:T(128)S(1)} %bitcast.84, f32[100]{0:T(128)S(1)} %bitcast.85), channel_id=1, replica_groups=mesh['dp'=4,'pair'=4,'core'=2] {'dp'}, use_global_device_ids=true, to_apply=%region_3.4 | all-reduce | flops 200 | bytes 1600 | tf_op jit(solution)/shard_map/psum | solution.py:874
  83.4 5.9 shard_map.197
  89.4 17.3 %all-to-all-done = bf16[8,104,2176]{2,1,0:T(8,128)(2,1)} async-done(((bf16[8,104,2176]{2,1,0:T(8,128)(2,1)}), bf16[8,104,2176]{2,1,0:T(8,128)(2,1)}, u32[]{:S(2)}, u32[]{:S(2)}) %all-to-all-start) | async-done | bytes 3620896 | tf_op jit(solution)/shard_map/all_to_all | solution.py:764
  106.7 3.6 all-to-all-start.1
  110.3 7.9 %shard_map.198 = (bf16[832,3200]{1,0:T(8,128)(2,1)}, bf16[3200,832]{1,0:T(8,128)(2,1)}) custom-call(bf16[800,3200]{1,0:T(8,128)(2,1)} %in_ref), custom_call_target="tpu_custom_call" | custom-call | flops 10000000 | bytes 16000000 | tf_op jit(solution)/shard_map/pallas_call | solution.py:548
  118.2 7.8 %shard_map.199 = (bf16[832,3200]{1,0:T(8,128)(2,1)}, bf16[3200,832]{1,0:T(8,128)(2,1)}) custom-call(bf16[800,3200]{1,0:T(8,128)(2,1)} %bitcast.66), custom_call_target="tpu_custom_call" | custom-call | flops 10000000 | bytes 16000000 | tf_op jit(solution)/shard_map/pallas_call | solution.py:548
  126.0 29.4 %all-to-all-done.1 = bf16[8,104,1152]{2,1,0:T(8,128)(2,1)S(1)} async-done(((bf16[8,104,1152]{2,1,0:T(8,128)(2,1)}), bf16[8,104,1152]{2,1,0:T(8,128)(2,1)S(1)}, u32[]{:S(2)}, u32[]{:S(2)}) %all-to-all-start.1) | async-done | bytes 1916960 | tf_op jit(solution)/shard_map/all_to_all | solution.py:764
  155.4 4.5 all-to-all-start.2
  159.9 1.7 broadcast_in_dim.68.b_in_ref
  161.7 0.9 reshape.86.b_out_ref
  162.7 58.2 %shard_map.200 = (bf16[832,2176]{1,0:T(8,128)(2,1)}, bf16[832,1152]{1,0:T(8,128)(2,1)}, bf16[3200,1152]{1,0:T(8,128)(2,1)}, bf16[3200,1152]{1,0:T(8,128)(2,1)}) custom-call(bf16[832,1152]{1,0:T(8,128)(2,1)} %bitcast.70, bf16[832,2176]{1,0:T(8,128)(2,1)} %bitcast.6.g_ref.refs_0_, bf16[3200,832]{1,0:T(8,128)(2,1)} %get-tuple-element.76.w_in_t_ref, ...), custom_call_target="tpu_custom_call" | custom-call | flops 24536678400 | bytes 40000000 | tf_op jit(solution)/shard_map/pallas_call | solution.py:675
  220.9 5.4 all-to-all-start.3
  226.3 50.4 %shard_map.201 = (bf16[832,2176]{1,0:T(8,128)(2,1)}, bf16[832,1024]{1,0:T(8,128)(2,1)}, bf16[3200,1024]{1,0:T(8,128)(2,1)}, bf16[3200,1024]{1,0:T(8,128)(2,1)}) custom-call(bf16[832,1024]{1,0:T(8,128)(2,1)} %bitcast.16.n_ref.refs_1_, bf16[832,2176]{1,0:T(8,128)(2,1)} %bitcast.6.g_ref.refs_0_, ...), custom_call_target="tpu_custom_call", output_to_operand_aliasing={{0}: (8, {})} | custom-call | flops 21810380800 | bytes 40000000 | tf_op jit(solution)/shard_map/pallas_call | solution.py:675
  276.7 21.1 %shard_map.202 = (bf16[416,3200]{1,0:T(8,128)(2,1)}, bf16[416,3200]{1,0:T(8,128)(2,1)}) custom-call(s32[1]{0:T(128)} %bitcast.2.core_ref, bf16[832,2176]{1,0:T(8,128)(2,1)} %bitcast.6.g_ref.refs_0_, bf16[3200,1152]{1,0:T(8,128)(2,1)} %get-tuple-element.81.refs_1_, bf16[3200,1024]{1,0:T(8,128)(2,1)} %get-tuple-element.88.refs_2_), custom_call_target="tpu_custom_call" | custom-call | flops 11586764800 | bytes 24000000 | tf_op jit(solution)/shard_map/pallas_call | solution.py:724
  298.3 5.2 all-to-all-start.4
  303.6 20.0 %shard_map.205 = (bf16[416,3200]{1,0:T(8,128)(2,1)}, bf16[416,3200]{1,0:T(8,128)(2,1)}) custom-call(s32[1]{0:T(128)} %bitcast.2.core_ref, bf16[832,1152]{1,0:T(8,128)(2,1)} %bitcast.71, bf16[832,1024]{1,0:T(8,128)(2,1)} %bitcast.16.n_ref.refs_1_, bf16[3200,1152]{1,0:T(8,128)(2,1)} %get-tuple-element.99.refs_2_, bf16[3200,1024]{1,0:T(8,128)(2,1)} %get-tuple-element.101.refs_3_), custom_call_target="tpu_custom_call" | custom-call | flops 11586764800 | bytes 24000000 | tf_op jit(solution)/shard_map/pallas_call | solution.py:724
  324.2 19.9 %all-to-all-done.4.rest_1_ = bf16[8,104,1024]{2,1,0:T(8,128)(2,1)S(1)} async-done(((bf16[8,104,1024]{2,1,0:T(8,128)(2,1)}), bf16[8,104,1024]{2,1,0:T(8,128)(2,1)S(1)}, u32[]{:S(2)}, u32[]{:S(2)}) %all-to-all-start.4) | async-done | bytes 1703968 | tf_op jit(solution)/shard_map/all_to_all | solution.py:764
  344.2 3.7 add_convert_fusion.1
  347.9 1.5 collective-permute-start.1
  350.1 6.1 shard_map.203
  357.2 0.9 reduce_sum.67
  358.1 2.0 add_convert_fusion
  360.2 1.6 collective-permute-start.4
  361.8 21.4 %psum.37 = f32[5,100]{1,0:T(8,128)S(1)} all-reduce(f32[5,100]{1,0:T(8,128)S(1)} %pad_maximum_fusion.2), channel_id=1, replica_groups=mesh['dp'=4,'pair'=4,'core'=2] {'dp'}, use_global_device_ids=true, to_apply=%region_8.9 | all-reduce | flops 500 | bytes 4000 | tf_op jit(solution)/shard_map/psum | solution.py:913
  384.1 18.6 %shard_map.204 = (bf16[48,104,384]{2,1,0:T(8,128)(2,1)}, f32[49,104,128]{2,1,0:T(8,128)}) custom-call(f32[5,104,128]{2,1,0:T(8,128)} %broadcast_in_dim.63.columns_ref, f32[48,104,384]{2,1,0:T(8,128)} %get-tuple-element.72.conv_ref, bf16[48,100,360]{2,1,0:T(8,128)(2,1)} %bitcast.56, bf16[8,104,1152]{2,1,0:T(8,128)(2,1)} %copy-done.2, ...), custom_call_target="tpu_custom_call" | custom-call | flops 4000000000 | bytes 10000000 | tf_op jit(solution)/shard_map/pallas_call | solution.py:419
  402.8 1.1 copy-done.13
  403.9 2.4 convert_add_fusion.1
  406.3 0.9 dynamic-slice_convert_fusion.1
  407.2 1.5 collective-permute-start.2
  408.7 2.2 convert_add_fusion
  410.9 1.5 copy-done.6
  412.4 0.9 dynamic-slice_convert_fusion
  413.3 4.5 all-to-all-start.5
  418.1 18.7 %shard_map.206 = (bf16[48,104,384]{2,1,0:T(8,128)(2,1)}, f32[49,104,128]{2,1,0:T(8,128)}) custom-call(f32[5,104,128]{2,1,0:T(8,128)} %broadcast_in_dim.63.columns_ref, f32[48,104,384]{2,1,0:T(8,128)} %get-tuple-element.72.conv_ref, bf16[48,100,360]{2,1,0:T(8,128)(2,1)} %bitcast.57, ...), custom_call_target="tpu_custom_call", output_to_operand_aliasing={{0}: (5, {}), {1}: (6, {})} | custom-call | flops 4000000000 | bytes 10000000 | tf_op jit(solution)/shard_map/pallas_call | solution.py:419
  436.8 2.4 add_convert_fusion.2
  439.2 23.1 %shard_map.207 = (bf16[48,104,384]{2,1,0:T(8,128)(2,1)}, f32[49,104,128]{2,1,0:T(8,128)}) custom-call(f32[5,104,128]{2,1,0:T(8,128)} %broadcast_in_dim.63.columns_ref, f32[48,104,384]{2,1,0:T(8,128)} %get-tuple-element.72.conv_ref, bf16[48,100,360]{2,1,0:T(8,128)(2,1)} %bitcast.58, ...), custom_call_target="tpu_custom_call", output_to_operand_aliasing={{0}: (5, {}), {1}: (6, {})} | custom-call | flops 4000000000 | bytes 10000000 | tf_op jit(solution)/shard_map/pallas_call | solution.py:419
  462.3 34.0 %shard_map.208 = bf16[48,100,360]{2,1,0:T(8,128)(2,1)} custom-call(f32[49,104,128]{2,1,0:T(8,128)} %broadcast_in_dim.27.taps_ref, bf16[48,104,384]{2,1,0:T(8,128)(2,1)} %get-tuple-element.113.grad_ref, bf16[48,100,360]{2,1,0:T(8,128)(2,1)} %bitcast.64, s32[48,1,360]{2,1,0:T(1,128)} %broadcast_in_dim_squeeze.2.land_ref), custom_call_target="tpu_custom_call" | custom-call | flops 10000000000 | bytes 16000000 | tf_op jit(solution)/shard_map/pallas_call | solution.py:474
  496.3 47.1 %all-reduce.9.cloned.1.call-done = (bf16[104,3200]{1,0:T(8,128)(2,1)}, bf16[104,3200]{1,0:T(8,128)(2,1)}) async-done(((bf16[104,3200]{1,0:T(8,128)(2,1)}, bf16[104,3200]{1,0:T(8,128)(2,1)}), (bf16[104,3200]{1,0:T(8,128)(2,1)}, bf16[104,3200]{1,0:T(8,128)(2,1)})) %all-reduce.9.cloned.1.call-update) | async-done | bytes 1331216 | tf_op jit(solution)/shard_map/psum | solution.py:933
  543.4 2.0 collective-permute-start.10
  547.4 1.1 collective-permute-start.8
  548.5 2.0 collective-permute-start.9
  550.5 11.3 %collective-permute-done.7 = f32[49,100]{1,0:T(8,128)S(1)} collective-permute-done((f32[49,100]{1,0:T(8,128)S(1)}, f32[49,100]{1,0:T(8,128)S(1)}, u32[]{:S(2)}, u32[]{:S(2)}) %collective-permute-start.7) | collective-permute-done | bytes 19632 | tf_op jit(solution)/shard_map/ppermute | solution.py:775
  561.7 1.8 collective-permute-done.8
  563.5 15.2 %all-gather.1 = f32[8,54,100]{2,1,0:T(8,128)} all-gather(f32[1,54,100]{2,1,0:T(8,128)S(1)} %maximum_bitcast_fusion), channel_id=2, replica_groups=mesh['dp'=4,'pair'=4,'core'=2] {'pair','core'}, dimensions={0}, use_global_device_ids=true | all-gather | bytes 194400 | tf_op jit(solution)/shard_map/all_gather | solution.py:939
  578.8 1.3 broadcast_select_fusion.3
  580.5 1.3 broadcast_select_fusion.1
  581.9 1.4 collective-permute-start.11
  583.3 6.0 shard_map.209
  589.4 22.4 %collective-permute-done.14.refs_1_ = bf16[208,3200]{1,0:T(8,128)(2,1)} collective-permute-done((bf16[208,3200]{1,0:T(8,128)(2,1)S(1)}, bf16[208,3200]{1,0:T(8,128)(2,1)}, u32[]{:S(2)}, u32[]{:S(2)}) %collective-permute-start.14) | collective-permute-done | bytes 1331232 | tf_op jit(solution)/shard_map/ppermute | solution.py:793
  612.3 1.3 collective-permute-done.11.refs_1_
  614.3 1.7 copy.53
  616.0 1.7 slice.69
  621.3 4.5 copy.56
  625.9 2.3 copy.55
  628.2 6.8 %shard_map.211 = f32[800,3200]{1,0:T(8,128)} custom-call(s32[1]{0:T(128)} %bitcast.35.place_ref, bf16[208,3200]{1,0:T(8,128)(2,1)} %copy-done.8, bf16[208,3200]{1,0:T(8,128)(2,1)} %collective-permute-done.14.refs_1_, bf16[208,3200]{1,0:T(8,128)(2,1)} %collective-permute-done.15.refs_2_, bf16[208,3200]{1,0:T(8,128)(2,1)} %collective-permute-done.16.refs_3_), custom_call_target="tpu_custom_call" | custom-call | flops 10000000 | bytes 16000000 | tf_op jit(solution)/shard_map/pallas_call | solution.py:752
  635.0 6.8 %shard_map.210 = f32[800,3200]{1,0:T(8,128)} custom-call(s32[1]{0:T(128)} %bitcast.34.place_ref, bf16[208,3200]{1,0:T(8,128)(2,1)} %copy-done.9, bf16[208,3200]{1,0:T(8,128)(2,1)} %collective-permute-done.11.refs_1_, bf16[208,3200]{1,0:T(8,128)(2,1)} %collective-permute-done.12.refs_2_, bf16[208,3200]{1,0:T(8,128)(2,1)} %collective-permute-done.13.refs_3_), custom_call_target="tpu_custom_call" | custom-call | flops 10000000 | bytes 16000000 | tf_op jit(solution)/shard_map/pallas_call | solution.py:752
  641.8 1.5 fusion.1
  (101 shorter events, 16.6 us)
Async XLA Ops:
  7.2 22.4 %copy-start = (bf16[49,800]{1,0:T(8,128)(2,1)S(1)}, bf16[49,800]{1,0:T(8,128)(2,1)}, u32[]{:S(2)}) copy-start(bf16[49,800]{1,0:T(8,128)(2,1)} %param.16) | copy-start | bytes 235204
  18.5 88.2 %all-to-all-start = ((bf16[8,104,2176]{2,1,0:T(8,128)(2,1)}), bf16[8,104,2176]{2,1,0:T(8,128)(2,1)}, u32[]{:S(2)}, u32[]{:S(2)}) async-start(bf16[8,104,2176]{2,1,0:T(8,128)(2,1)} %bitcast.68), calls=%async_computation | async-start | bytes 7241728 | tf_op jit(solution)/shard_map/all_to_all | solution.py:764
  106.7 48.7 %all-to-all-start.1 = ((bf16[8,104,1152]{2,1,0:T(8,128)(2,1)}), bf16[8,104,1152]{2,1,0:T(8,128)(2,1)S(1)}, u32[]{:S(2)}, u32[]{:S(2)}) async-start(bf16[8,104,1152]{2,1,0:T(8,128)(2,1)} %bitcast.73), calls=%async_computation.1 | async-start | bytes 3833856 | tf_op jit(solution)/shard_map/all_to_all | solution.py:764
  126.0 34.0 %copy-start.17 = (f32[3200]{0:T(1024)S(1)}, f32[3200]{0:T(1024)}, u32[]{:S(2)}) copy-start(f32[3200]{0:T(1024)} %param.21) | copy-start | bytes 38404
  126.0 35.7 %copy-start.18 = (f32[800]{0:T(1024)S(1)}, f32[800]{0:T(1024)}, u32[]{:S(2)}) copy-start(f32[800]{0:T(1024)} %param.23) | copy-start | bytes 9604
  155.4 7.2 %copy-start.12 = (bf16[8,104,1152]{2,1,0:T(8,128)(2,1)}, bf16[8,104,1152]{2,1,0:T(8,128)(2,1)S(1)}, u32[]{:S(2)}) copy-start(bf16[8,104,1152]{2,1,0:T(8,128)(2,1)S(1)} %all-to-all-done.1) | copy-start | bytes 5750788
  155.4 65.5 %all-to-all-start.2 = ((bf16[8,104,1024]{2,1,0:T(8,128)(2,1)}), bf16[8,104,1024]{2,1,0:T(8,128)(2,1)}, u32[]{:S(2)}, u32[]{:S(2)}) async-start(bf16[8,104,1024]{2,1,0:T(8,128)(2,1)} %bitcast.75), calls=%async_computation.2 | async-start | bytes 3407872 | tf_op jit(solution)/shard_map/all_to_all | solution.py:764
  220.9 55.8 %all-to-all-start.3 = ((bf16[8,104,1152]{2,1,0:T(8,128)(2,1)}), bf16[8,104,1152]{2,1,0:T(8,128)(2,1)S(1)}, u32[]{:S(2)}, u32[]{:S(2)}) async-start(bf16[8,104,1152]{2,1,0:T(8,128)(2,1)} %bitcast.72), calls=%async_computation.3 | async-start | bytes 3833856 | tf_op jit(solution)/shard_map/all_to_all | solution.py:764
  276.7 21.1 %copy-start.2 = (bf16[8,104,1152]{2,1,0:T(8,128)(2,1)}, bf16[8,104,1152]{2,1,0:T(8,128)(2,1)S(1)}, u32[]{:S(2)}) copy-start(bf16[8,104,1152]{2,1,0:T(8,128)(2,1)S(1)} %all-to-all-done.3.rest_0_) | copy-start | bytes 5750788
  297.8 46.4 %collective-permute-start = (bf16[416,3200]{1,0:T(8,128)(2,1)}, bf16[416,3200]{1,0:T(8,128)(2,1)}, u32[]{:S(2)}, u32[]{:S(2)}) collective-permute-start(bf16[416,3200]{1,0:T(8,128)(2,1)} %get-tuple-element.93), channel_id=1, source_target_pairs={{0,1},{1,0},{2,3},{3,2},{4,5},{5,4},{6,7},{7,6},{8,9},{9,8},{10,11... | collective-permute-start | bytes 7987208 | tf_op jit(solution)/shard_map/ppermute | solution.py:780
  298.3 45.8 %all-to-all-start.4 = ((bf16[8,104,1024]{2,1,0:T(8,128)(2,1)}), bf16[8,104,1024]{2,1,0:T(8,128)(2,1)S(1)}, u32[]{:S(2)}, u32[]{:S(2)}) async-start(bf16[8,104,1024]{2,1,0:T(8,128)(2,1)} %bitcast.74), calls=%async_computation.4 | async-start | bytes 3407872 | tf_op jit(solution)/shard_map/all_to_all | solution.py:764
  303.6 20.5 %copy-start.16 = (f32[104,128]{1,0:T(8,128)S(1)}, f32[104,128]{1,0:T(8,128)}, u32[]{:S(2)}) copy-start(f32[104,128]{1,0:T(8,128)} %get-tuple-element.96) | copy-start | bytes 159748
  323.6 34.5 %collective-permute-start.3 = (bf16[416,3200]{1,0:T(8,128)(2,1)}, bf16[416,3200]{1,0:T(8,128)(2,1)}, u32[]{:S(2)}, u32[]{:S(2)}) collective-permute-start(bf16[416,3200]{1,0:T(8,128)(2,1)} %get-tuple-element.104), channel_id=1, source_target_pairs={{0,1},{1,0},{2,3},{3,2},{4,5},{5,4},{6,7},{7,6},{8,9},{9,8},{10,11... | collective-permute-start | bytes 7987208 | tf_op jit(solution)/shard_map/ppermute | solution.py:780
  344.2 6.0 copy-start.3
  347.9 54.9 %collective-permute-start.1 = (bf16[208,3200]{1,0:T(8,128)(2,1)}, bf16[208,3200]{1,0:T(8,128)(2,1)S(1)}, u32[]{:S(2)}, u32[]{:S(2)}) collective-permute-start(bf16[208,3200]{1,0:T(8,128)(2,1)} %add_convert_fusion.1), channel_id=1, source_target_pairs={{0,8},{8,0},{16,24},{24,16},{1,9},{9,1},{17,25},{25,17},{2,10},{10... | collective-permute-start | bytes 3993608 | tf_op jit(solution)/shard_map/ppermute | solution.py:793
  360.2 43.7 %collective-permute-start.4 = (bf16[208,3200]{1,0:T(8,128)(2,1)S(1)}, bf16[208,3200]{1,0:T(8,128)(2,1)}, u32[]{:S(2)}, u32[]{:S(2)}) collective-permute-start(bf16[208,3200]{1,0:T(8,128)(2,1)S(1)} %add_convert_fusion), channel_id=1, source_target_pairs={{0,16},{8,24},{16,0},{24,8},{1,17},{9,25},{17,1},{25,9},{2,18},{10... | collective-permute-start | bytes 3993608 | tf_op jit(solution)/shard_map/ppermute | solution.py:793
  384.1 19.7 %copy-start.10 = (bf16[416,3200]{1,0:T(8,128)(2,1)S(1)}, bf16[416,3200]{1,0:T(8,128)(2,1)}, u32[]{:S(2)}) copy-start(bf16[416,3200]{1,0:T(8,128)(2,1)} %get-tuple-element.92) | copy-start | bytes 7987204
  402.8 1.1 copy-start.13
  403.9 4.9 copy-start.11
  407.2 29.6 %collective-permute-start.2 = (bf16[104,3200]{1,0:T(8,128)(2,1)}, bf16[104,3200]{1,0:T(8,128)(2,1)S(1)}, u32[]{:S(2)}, u32[]{:S(2)}) collective-permute-start(bf16[104,3200]{1,0:T(8,128)(2,1)} %dynamic-slice_convert_fusion.1), channel_id=1, source_target_pairs={{0,16},{8,24},{16,0},{24,8},{1,17},{9,25},{17,1},{25,9},{2,18},{10... | collective-permute-start | bytes 1996808 | tf_op jit(solution)/shard_map/ppermute | solution.py:793
  410.9 1.5 copy-start.6
  413.3 23.4 %collective-permute-start.5 = (bf16[104,3200]{1,0:T(8,128)(2,1)}, bf16[104,3200]{1,0:T(8,128)(2,1)}, u32[]{:S(2)}, u32[]{:S(2)}) collective-permute-start(bf16[104,3200]{1,0:T(8,128)(2,1)} %dynamic-slice_convert_fusion), channel_id=1, source_target_pairs={{0,8},{8,0},{16,24},{24,16},{1,9},{9,1},{17,25},{25,17},{2,10},{10... | collective-permute-start | bytes 1996808 | tf_op jit(solution)/shard_map/ppermute | solution.py:793
  413.3 170.0 %all-to-all-start.5 = ((bf16[8,104,2176]{2,1,0:T(8,128)(2,1)}), bf16[8,104,2176]{2,1,0:T(8,128)(2,1)}, u32[]{:S(2)}, u32[]{:S(2)}) async-start(bf16[8,104,2176]{2,1,0:T(8,128)(2,1)} %bitcast.69), calls=%async_computation.5 | async-start | bytes 7241728 | tf_op jit(solution)/shard_map/all_to_all | solution.py:764
  417.8 125.6 %all-reduce.9.cloned.1.call-start = ((), (), s32[]{:S(2)}) async-start(), calls=%async_computation.6 | async-start | bytes 2662400 | tf_op jit(solution)/shard_map/psum | solution.py:933
  418.1 18.7 %copy-start.7 = (f32[208,3200]{1,0:T(8,128)S(1)}, f32[208,3200]{1,0:T(8,128)}, u32[]{:S(2)}) copy-start(f32[208,3200]{1,0:T(8,128)} %copy-done.6) | copy-start | bytes 7987204
  462.3 83.7 %copy-start.4 = (f32[49,104,128]{2,1,0:T(8,128)S(1)}, f32[49,104,128]{2,1,0:T(8,128)}, u32[]{:S(2)}) copy-start(f32[49,104,128]{2,1,0:T(8,128)} %get-tuple-element.115) | copy-start | bytes 7827460
  543.4 35.4 %copy-start.15 = (bf16[104,3200]{1,0:T(8,128)(2,1)S(1)}, bf16[104,3200]{1,0:T(8,128)(2,1)}, u32[]{:S(2)}) copy-start(bf16[104,3200]{1,0:T(8,128)(2,1)} %get-tuple-element.114) | copy-start | bytes 1996804
  543.4 35.3 %collective-permute-start.10 = (bf16[104,3200]{1,0:T(8,128)(2,1)}, bf16[104,3200]{1,0:T(8,128)(2,1)}, u32[]{:S(2)}, u32[]{:S(2)}) collective-permute-start(bf16[104,3200]{1,0:T(8,128)(2,1)} %get-tuple-element.116), channel_id=1, source_target_pairs={{0,8},{8,0},{16,24},{24,16},{1,9},{9,1},{17,25},{25,17},{2,10},{10... | collective-permute-start | bytes 1996808 | tf_op jit(solution)/shard_map/ppermute | solution.py:793
  545.4 33.3 %collective-permute-start.6 = (bf16[104,3200]{1,0:T(8,128)(2,1)}, bf16[104,3200]{1,0:T(8,128)(2,1)}, u32[]{:S(2)}, u32[]{:S(2)}) collective-permute-start(bf16[104,3200]{1,0:T(8,128)(2,1)} %get-tuple-element.114), channel_id=1, source_target_pairs={{0,16},{8,24},{16,0},{24,8},{1,17},{9,25},{17,1},{25,9},{2,18},{10... | collective-permute-start | bytes 1996808 | tf_op jit(solution)/shard_map/ppermute | solution.py:793
  546.9 14.8 %collective-permute-start.7 = (f32[49,100]{1,0:T(8,128)S(1)}, f32[49,100]{1,0:T(8,128)S(1)}, u32[]{:S(2)}, u32[]{:S(2)}) collective-permute-start(f32[49,100]{1,0:T(8,128)S(1)} %bitcast.79), channel_id=1, source_target_pairs={{0,8},{8,0},{16,24},{24,16},{1,9},{9,1},{17,25},{25,17},{2,10},{10... | collective-permute-start | bytes 58808 | tf_op jit(solution)/shard_map/ppermute | solution.py:775
  547.4 16.1 %collective-permute-start.8 = (f32[49,100]{1,0:T(8,128)S(1)}, f32[49,100]{1,0:T(8,128)S(1)}, u32[]{:S(2)}, u32[]{:S(2)}) collective-permute-start(f32[49,100]{1,0:T(8,128)S(1)} %bitcast.80), channel_id=1, source_target_pairs={{0,16},{8,24},{16,0},{24,8},{1,17},{9,25},{17,1},{25,9},{2,18},{10... | collective-permute-start | bytes 58808 | tf_op jit(solution)/shard_map/ppermute | solution.py:775
  548.5 15.0 %collective-permute-start.9 = (f32[49,100]{1,0:T(8,128)S(1)}, f32[49,100]{1,0:T(8,128)S(1)}, u32[]{:S(2)}, u32[]{:S(2)}) collective-permute-start(f32[49,100]{1,0:T(8,128)S(1)} %bitcast.81), channel_id=1, source_target_pairs={{0,24},{8,16},{16,8},{24,0},{1,25},{9,17},{17,9},{25,1},{2,26},{10... | collective-permute-start | bytes 58808 | tf_op jit(solution)/shard_map/ppermute | solution.py:775
  578.7 1.7 copy-start.14
  580.1 3.2 copy-start.8
  580.1 31.6 %collective-permute-start.14 = (bf16[208,3200]{1,0:T(8,128)(2,1)S(1)}, bf16[208,3200]{1,0:T(8,128)(2,1)}, u32[]{:S(2)}, u32[]{:S(2)}) collective-permute-start(bf16[208,3200]{1,0:T(8,128)(2,1)S(1)} %pad_maximum_fusion.refs_0_), channel_id=1, source_target_pairs={{0,8},{8,0},{16,24},{24,16},{1,9},{9,1},{17,25},{25,17},{2,10},{10... | collective-permute-start | bytes 3993608 | tf_op jit(solution)/shard_map/ppermute | solution.py:793
  581.9 29.9 %copy-start.9 = (bf16[208,3200]{1,0:T(8,128)(2,1)}, bf16[208,3200]{1,0:T(8,128)(2,1)S(1)}, u32[]{:S(2)}) copy-start(bf16[208,3200]{1,0:T(8,128)(2,1)S(1)} %pad_maximum_fusion.1.refs_0_) | copy-start | bytes 3993604
  581.9 31.7 %collective-permute-start.11 = (bf16[208,3200]{1,0:T(8,128)(2,1)S(1)}, bf16[208,3200]{1,0:T(8,128)(2,1)}, u32[]{:S(2)}, u32[]{:S(2)}) collective-permute-start(bf16[208,3200]{1,0:T(8,128)(2,1)S(1)} %pad_maximum_fusion.1.refs_0_), channel_id=1, source_target_pairs={{0,16},{8,24},{16,0},{24,8},{1,17},{9,25},{17,1},{25,9},{2,18},{10... | collective-permute-start | bytes 3993608 | tf_op jit(solution)/shard_map/ppermute | solution.py:793
  583.3 44.9 %collective-permute-start.15 = (bf16[208,3200]{1,0:T(8,128)(2,1)S(1)}, bf16[208,3200]{1,0:T(8,128)(2,1)}, u32[]{:S(2)}, u32[]{:S(2)}) collective-permute-start(bf16[208,3200]{1,0:T(8,128)(2,1)S(1)} %pad_maximum_fusion.refs_0_), channel_id=1, source_target_pairs={{0,1},{1,0},{2,3},{3,2},{4,5},{5,4},{6,7},{7,6},{8,9},{9,8},{10,11... | collective-permute-start | bytes 3993608 | tf_op jit(solution)/shard_map/ppermute | solution.py:780
  611.8 16.4 %collective-permute-start.16 = (bf16[208,3200]{1,0:T(8,128)(2,1)}, bf16[208,3200]{1,0:T(8,128)(2,1)}, u32[]{:S(2)}, u32[]{:S(2)}) collective-permute-start(bf16[208,3200]{1,0:T(8,128)(2,1)} %collective-permute-done.14.refs_1_), channel_id=1, source_target_pairs={{0,1},{1,0},{2,3},{3,2},{4,5},{5,4},{6,7},{7,6},{8,9},{9,8},{10,11... | collective-permute-start | bytes 3993608 | tf_op jit(solution)/shard_map/ppermute | solution.py:780
  611.8 23.2 %collective-permute-start.12 = (bf16[208,3200]{1,0:T(8,128)(2,1)S(1)}, bf16[208,3200]{1,0:T(8,128)(2,1)}, u32[]{:S(2)}, u32[]{:S(2)}) collective-permute-start(bf16[208,3200]{1,0:T(8,128)(2,1)S(1)} %pad_maximum_fusion.1.refs_0_), channel_id=1, source_target_pairs={{0,1},{1,0},{2,3},{3,2},{4,5},{5,4},{6,7},{7,6},{8,9},{9,8},{10,11... | collective-permute-start | bytes 3993608 | tf_op jit(solution)/shard_map/ppermute | solution.py:780
  613.6 21.4 %collective-permute-start.13 = (bf16[208,3200]{1,0:T(8,128)(2,1)}, bf16[208,3200]{1,0:T(8,128)(2,1)}, u32[]{:S(2)}, u32[]{:S(2)}) collective-permute-start(bf16[208,3200]{1,0:T(8,128)(2,1)} %collective-permute-done.11.refs_1_), channel_id=1, source_target_pairs={{0,1},{1,0},{2,3},{3,2},{4,5},{5,4},{6,7},{7,6},{8,9},{9,8},{10,11... | collective-permute-start | bytes 3993608 | tf_op jit(solution)/shard_map/ppermute | solution.py:780
  621.3 4.6 copy-start.5
  634.9 8.4 %copy-start.1 = (bf16[49,800]{1,0:T(8,128)(2,1)S(1)}, bf16[49,800]{1,0:T(8,128)(2,1)}, u32[]{:S(2)}) copy-start(bf16[49,800]{1,0:T(8,128)(2,1)} %param.16) | copy-start | bytes 235204
Sparse Core Ops, SparseCore 0:
  439.4 103.9 all-reduce.8

commit v2 on v0

--- a/solution.py
+++ b/solution.py
@@ -128,8 +128,8 @@
     return pl.BlockSpec(memory_space=pltpu.SMEM)
 
 
-def cost(bytes_accessed, flops=10**7):
-    return pl.CostEstimate(flops=flops, bytes_accessed=bytes_accessed, transcendentals=0)
+def cost():
+    return pl.CostEstimate(flops=1000, bytes_accessed=1000, transcendentals=0)
 
 
 PAIR = 2
@@ -202,7 +202,7 @@
             jax.ShapeDtypeStruct((z.pad, LANES), F32),
         ],
         compiler_params=params(),
-        cost_estimate=cost(8 * 10**6),
+        cost_estimate=cost(),
     )(cot, land)
     return out, jnp.sum(sums, axis=1)[: z.chan]
 
@@ -283,7 +283,7 @@
         ],
         scratch_shapes=[pltpu.VMEM((z.height + 2 * z.margin, GROUP, z.wide), F32)],
         compiler_params=params(),
-        cost_estimate=cost(16 * 10**6, 10**10),
+        cost_estimate=cost(),
     )(taps, x)
     return conv, jnp.sum(total, axis=1)[: z.chan], jnp.sum(square, axis=1)[: z.chan]
 
@@ -314,7 +314,7 @@
         out_specs=[pair_packed(z, n) for n in lengths],
         out_shape=[jax.ShapeDtypeStruct((z.packed_rows, n), BF16) for n in lengths],
         compiler_params=params(),
-        cost_estimate=cost(12 * 10**6),
+        cost_estimate=cost(),
     )(columns, conv)
 
 
@@ -351,7 +351,7 @@
         out_specs=[whole((z.pad, LANES))] * 2,
         out_shape=[lane_shape, lane_shape],
         compiler_params=params(),
-        cost_estimate=cost(12 * 10**6),
+        cost_estimate=cost(),
     )(columns, conv, *parts)
     return jnp.sum(shift, axis=1)[: z.chan], jnp.sum(gain, axis=1)[: z.chan]
 
@@ -436,7 +436,7 @@
         ],
         input_output_aliases={len(operands) - 2 + k: k for k in range(len(before))},
         compiler_params=params(),
-        cost_estimate=cost(10 * 10**6, 4 * 10**9),
+        cost_estimate=cost(),
     )(*operands)
 
 
@@ -485,7 +485,7 @@
             pltpu.VMEM((z.height, GROUP, z.wide), F32),
         ],
         compiler_params=params(),
-        cost_estimate=cost(16 * 10**6, 10**10),
+        cost_estimate=cost(),
     )(taps, grad, cot, land)
 
 
@@ -507,7 +507,7 @@
         out_specs=pair_rows(z),
         out_shape=jax.ShapeDtypeStruct((z.height, z.chan, z.width), BF16),
         compiler_params=params(),
-        cost_estimate=cost(12 * 10**6),
+        cost_estimate=cost(),
     )(x, land, branch)
 
 
@@ -559,7 +559,7 @@
         ],
         scratch_shapes=[pltpu.VMEM((rows, block), F32)],
         compiler_params=params(),
-        cost_estimate=cost(16 * 10**6),
+        cost_estimate=cost(),
     )(matrix)
 
 
@@ -681,9 +681,7 @@
         + [pltpu.SemaphoreType.DMA((2,))],
         input_output_aliases=aliases,
         compiler_params=params(),
-        cost_estimate=pl.CostEstimate(
-            flops=8 * packed * cells * hidden, bytes_accessed=4 * 10**7, transcendentals=cells * hidden
-        ),
+        cost_estimate=cost(),
     )(*operands)
 
 
@@ -711,7 +709,6 @@
         mine_ref[...] = both[core_ref[0]]
         sent_ref[...] = both[1 - core_ref[0]]
 
-    cells = sum(right.shape[1] for right in rights)
     out = jax.ShapeDtypeStruct((half, hidden), BF16)
     return pl.pallas_call(
         kernel,
@@ -722,7 +719,7 @@
         out_shape=[out, out],
         scratch_shapes=[pltpu.VMEM((CORES, half, block), BF16)],
         compiler_params=params(),
-        cost_estimate=cost(24 * 10**6, 2 * rows * cells * hidden),
+        cost_estimate=cost(),
     )(core[None], *arrays, *rights)
 
 
@@ -748,7 +745,7 @@
         out_specs=pl.BlockSpec((groups * z.chan, hidden), lambda q: (q, 0)),
         out_shape=jax.ShapeDtypeStruct((4 * groups * z.chan, hidden), F32),
         compiler_params=params(),
-        cost_estimate=cost(16 * 10**6),
+        cost_estimate=cost(),
     )(place[None], *pieces)
 
 
@@ -791,7 +788,8 @@
             F32
         ) + lax.dynamic_slice_in_dim(self.other, at, rows, 0).astype(F32)
 
-    def first(self):
+    def first(self, ready):
+        self.mine = after(self.mine, ready)
         self.arrived = self.meet(self.pair(1 - self.bits[0]).astype(BF16), self.turns[0])
 
     def second(self, ready):
@@ -893,8 +891,8 @@
     )
     sum_in = HalvingSum((2, 1), mine, sent_in)
     branch = exchange(after(branch, norm_parts[1], sent_in))
-    sum_out.first()
-    sum_in.first()
+    sum_out.first(norm_parts[1])
+    sum_in.first(norm_parts[1])
 
     part_shift, part_gain = norm_sums(z, norm_parts, conv, over_lanes(jnp.stack([mean, scale])))
     small = jnp.concatenate(
@@ -924,20 +922,23 @@
     shares = lax.psum(shares, "pair")
     g_kernel = dp_sum(jnp.sum(products, axis=2)[:, :chan])
     x_grad = conv_backward(z, taps, conv_grad, cot, land3)
-    sum_out.back_first(after(shares[0], x_grad))
-    sum_in.back_first(after(shares[1], x_grad))
+    rows = jnp.concatenate([after(g_kernel, x_grad), small], axis=0)
+    gathered = lax.all_gather(rows, CHAN)
+    placed = jnp.transpose(gathered, (1, 0, 2)).reshape(rows.shape[0], width)
+    sum_out.back_first(after(shares[0], gathered))
+    sum_in.back_first(after(shares[1], gathered))
     mixed = mix_branch(z, branch, after(x, sum_out.own, sum_in.own), land3)
     sum_out.back_second(mixed)
     sum_in.back_second(mixed)
-    rows = jnp.concatenate([after(g_kernel, x_grad, sum_out.own, sum_in.own), small], axis=0)
-    gathered = lax.all_gather(rows, CHAN)
-    placed = jnp.transpose(gathered, (1, 0, 2)).reshape(rows.shape[0], width)
-    g_w_out_t, _ = sum_out.finish(z, placed)
-    g_w_in, pieces = sum_in.finish(z, placed)
+    mixed = after(mixed, sum_out.own, sum_in.own)
+    mixed_out = jnp.transpose(mixed, (0, 2, 1))[None]
+    x_grad_out = jnp.transpose(after(x_grad, sum_out.own, sum_in.own), (0, 2, 1))[None]
+    g_w_out_t, _ = sum_out.finish(z, x_grad_out)
+    g_w_in, pieces = sum_in.finish(z, x_grad_out)
 
     return (
-        jnp.transpose(mixed, (0, 2, 1))[None],
-        jnp.transpose(x_grad, (0, 2, 1))[None],
+        mixed_out,
+        x_grad_out,
         placed[:ntaps],
         placed[ntaps + 1],
         placed[ntaps],

time: 594 us -> 567 us (0.955)
  waiting for transfers between devices: 127 us -> 94.5 us
  blocking collectives: 34.4 us -> 43.1 us
    all_to_all x6, waiting for transfers between devices: 85.5 us -> 54 us  [exchange(): return lax.all_to_all(value, CHAN, split_axis=0, concat_axis=0, tiled=True)]
    ppermute x8, waiting for transfers between devices: 8.88 us -> 39.8 us  [meet(): return lax.ppermute(value, 'dp', [(i, i ^ turn) for i in range(ways)])]
    ppermute x3, waiting for transfers between devices: 25.1 us -> 0.01 us  [dp_sum(): lax.ppermute(value, 'dp', [(i, i ^ turn) for i in range(ways)])]
    psum x1, waiting for transfers between devices: 7.75 us -> 0.01 us  [per_device(): shares = lax.psum(shares, 'pair')]
    psum x1, blocking collectives: 9.91 us -> 17.5 us  [per_device(): small = lax.psum(small, 'dp')]
    unnamed x42 -> x46, local copies, waits for them, and re-layouts: 23.2 us -> 19 us
  transfers between devices with their start and end apart: 24 -> 24, of which waited for: 9 -> 8; matrix products, arithmetic and copies ran while one was open for 8% -> 9% of each run, Pallas kernels for 46% -> 52%
where the time goes in v2:
time: 567 us; the launch traced here: 560 us
  Pallas kernels  305 us (54%)
  waiting for transfers between devices  94.5 us (17%)
  blocking collectives  43.1 us (8%)
  starting transfers between devices  42.6 us (8%)
  local copies, waits for them, and re-layouts  37.3 us (7%)
  other arithmetic  22.3 us (4%)
  between operations  15.2 us (3%)
    pallas_call x2, Pallas kernels, mlp(): pl.pallas_call(kernel, grid=(blocks + outs,), in_specs=in_specs, out_spec...  81.1 us
    pallas_call x3, Pallas kernels, conv_gradient(): pl.pallas_call(kernel, grid=(end - begin,), in_specs=[group((5, GROUP, LA...  60.4 us
    all_to_all x6, waiting for transfers between devices, exchange(): return lax.all_to_all(value, CHAN, split_axis=0, concat_axis=0, tiled=True)  54 us
    pallas_call x2, Pallas kernels, weight_grad(): pl.pallas_call(kernel, grid=(hidden // block,), in_specs=[smem()] + [whol...  40.6 us
    ppermute x8, waiting for transfers between devices, meet(): return lax.ppermute(value, 'dp', [(i, i ^ turn) for i in range(ways)])  39.8 us
    pallas_call x1, Pallas kernels, conv_forward(): pl.pallas_call(kernel, grid=(pl.cdiv(z.chan, GROUP),), in_specs=[group_la...  36.3 us
    pallas_call x1, Pallas kernels, conv_backward(): pl.pallas_call(kernel, grid=(pl.cdiv(z.chan, GROUP),), in_specs=[group_la...  33.8 us
    all_to_all x6, starting transfers between devices, exchange(): return lax.all_to_all(value, CHAN, split_axis=0, concat_axis=0, tiled=True)  29.1 us
  transfers between devices with their start and end apart: 24, of which 8 were waited for; matrix products, arithmetic and copies ran while one was open for 9% of the time, Pallas kernels for 52%

profile of v2, /device:TPU:0, one launch (start us, length us, event | category | flops | bytes accessed | tf_op | source)
XLA Modules:
  0.0 559.8 jit_solution(15014821373381226134)
XLA Ops:
  7.2 1.6 broadcast_in_dim_squeeze.2.land_ref
  8.8 4.7 copy.59
  13.5 5.0 shard_map.195
  18.5 6.3 %all-to-all-start = ((bf16[8,104,2176]{2,1,0:T(8,128)(2,1)}), bf16[8,104,2176]{2,1,0:T(8,128)(2,1)}, u32[]{:S(2)}, u32[]{:S(2)}) async-start(bf16[8,104,2176]{2,1,0:T(8,128)(2,1)} %bitcast.70), calls=%async_computation | async-start | bytes 7241728 | tf_op jit(solution)/shard_map/all_to_all | solution.py:753
  24.8 4.7 copy.60
  29.7 2.0 broadcast_in_dim.27.taps_ref
  31.6 36.3 %shard_map.196 = (f32[48,104,384]{2,1,0:T(8,128)}, f32[104,128]{1,0:T(8,128)}, f32[104,128]{1,0:T(8,128)}) custom-call(f32[49,104,128]{2,1,0:T(8,128)} %broadcast_in_dim.27.taps_ref, bf16[48,100,360]{2,1,0:T(8,128)(2,1)} %bitcast.55), custom_call_target="tpu_custom_call" | custom-call | flops 1000 | bytes 1000 | tf_op jit(solution)/shard_map/pallas_call | solution.py:276
  67.9 0.9 reduce_sum.64
  68.8 0.9 reduce_sum.63
  70.4 9.9 %all-reduce.5 = (f32[100]{0:T(128)S(1)}, f32[100]{0:T(128)S(1)}) all-reduce(f32[100]{0:T(128)S(1)} %bitcast.83, f32[100]{0:T(128)S(1)} %bitcast.84), channel_id=1, replica_groups=mesh['dp'=4,'pair'=4,'core'=2] {'dp'}, use_global_device_ids=true, to_apply=%region_3.4 | all-reduce | flops 200 | bytes 1600 | tf_op jit(solution)/shard_map/psum | solution.py:863
  83.4 6.0 %shard_map.197 = (bf16[832,1152]{1,0:T(8,128)(2,1)}, bf16[832,1024]{1,0:T(8,128)(2,1)}) custom-call(f32[3,104,128]{2,1,0:T(8,128)} %broadcast_in_dim.28.columns_ref, f32[48,104,384]{2,1,0:T(8,128)} %get-tuple-element.73.conv_ref), custom_call_target="tpu_custom_call" | custom-call | flops 1000 | bytes 1000 | tf_op jit(solution)/shard_map/pallas_call | solution.py:310
  89.3 17.3 %all-to-all-done = bf16[8,104,2176]{2,1,0:T(8,128)(2,1)} async-done(((bf16[8,104,2176]{2,1,0:T(8,128)(2,1)}), bf16[8,104,2176]{2,1,0:T(8,128)(2,1)}, u32[]{:S(2)}, u32[]{:S(2)}) %all-to-all-start) | async-done | bytes 3620896 | tf_op jit(solution)/shard_map/all_to_all | solution.py:753
  106.7 3.6 all-to-all-start.1
  110.3 8.0 %shard_map.198 = (bf16[832,3200]{1,0:T(8,128)(2,1)}, bf16[3200,832]{1,0:T(8,128)(2,1)}) custom-call(bf16[800,3200]{1,0:T(8,128)(2,1)} %in_ref), custom_call_target="tpu_custom_call" | custom-call | flops 1000 | bytes 1000 | tf_op jit(solution)/shard_map/pallas_call | solution.py:548
  118.2 7.9 %shard_map.199 = (bf16[832,3200]{1,0:T(8,128)(2,1)}, bf16[3200,832]{1,0:T(8,128)(2,1)}) custom-call(bf16[800,3200]{1,0:T(8,128)(2,1)} %bitcast.69), custom_call_target="tpu_custom_call" | custom-call | flops 1000 | bytes 1000 | tf_op jit(solution)/shard_map/pallas_call | solution.py:548
  126.1 29.3 %all-to-all-done.1 = bf16[8,104,1152]{2,1,0:T(8,128)(2,1)S(1)} async-done(((bf16[8,104,1152]{2,1,0:T(8,128)(2,1)}), bf16[8,104,1152]{2,1,0:T(8,128)(2,1)S(1)}, u32[]{:S(2)}, u32[]{:S(2)}) %all-to-all-start.1) | async-done | bytes 1916960 | tf_op jit(solution)/shard_map/all_to_all | solution.py:753
  155.4 4.5 all-to-all-start.2
  159.9 1.7 broadcast_in_dim.68.b_in_ref
  161.7 1.0 reshape.86.b_out_ref
  162.6 43.4 %shard_map.200 = (bf16[832,2176]{1,0:T(8,128)(2,1)}, bf16[832,1152]{1,0:T(8,128)(2,1)}, bf16[3200,1152]{1,0:T(8,128)(2,1)}, bf16[3200,1152]{1,0:T(8,128)(2,1)}) custom-call(bf16[832,1152]{1,0:T(8,128)(2,1)} %bitcast.63, bf16[832,2176]{1,0:T(8,128)(2,1)} %bitcast.6.g_ref.refs_0_, bf16[3200,832]{1,0:T(8,128)(2,1)} %get-tuple-element.77.w_in_t_ref, ...), custom_call_target="tpu_custom_call" | custom-call | flops 1000 | bytes 1000 | tf_op jit(solution)/shard_map/pallas_call | solution.py:664
  206.0 5.3 all-to-all-start.3
  211.3 37.8 %shard_map.201 = (bf16[832,2176]{1,0:T(8,128)(2,1)}, bf16[832,1024]{1,0:T(8,128)(2,1)}, bf16[3200,1024]{1,0:T(8,128)(2,1)}, bf16[3200,1024]{1,0:T(8,128)(2,1)}) custom-call(bf16[832,1024]{1,0:T(8,128)(2,1)} %bitcast.16.n_ref.refs_1_, bf16[832,2176]{1,0:T(8,128)(2,1)} %bitcast.6.g_ref.refs_0_, ...), custom_call_target="tpu_custom_call", output_to_operand_aliasing={{0}: (8, {})} | custom-call | flops 1000 | bytes 1000 | tf_op jit(solution)/shard_map/pallas_call | solution.py:664
  249.1 7.4 %all-to-all-done.3.rest_0_ = bf16[8,104,1152]{2,1,0:T(8,128)(2,1)S(1)} async-done(((bf16[8,104,1152]{2,1,0:T(8,128)(2,1)}), bf16[8,104,1152]{2,1,0:T(8,128)(2,1)S(1)}, u32[]{:S(2)}, u32[]{:S(2)}) %all-to-all-start.3) | async-done | bytes 1916960 | tf_op jit(solution)/shard_map/all_to_all | solution.py:753
  256.5 4.6 all-to-all-start.4
  261.0 20.4 %shard_map.202 = (bf16[416,3200]{1,0:T(8,128)(2,1)}, bf16[416,3200]{1,0:T(8,128)(2,1)}) custom-call(s32[1]{0:T(128)} %bitcast.2.core_ref, bf16[832,2176]{1,0:T(8,128)(2,1)} %bitcast.6.g_ref.refs_0_, bf16[3200,1152]{1,0:T(8,128)(2,1)} %get-tuple-element.82.refs_1_, bf16[3200,1024]{1,0:T(8,128)(2,1)} %get-tuple-element.89.refs_2_), custom_call_target="tpu_custom_call" | custom-call | flops 1000 | bytes 1000 | tf_op jit(solution)/shard_map/pallas_call | solution.py:713
  281.9 20.1 %shard_map.205 = (bf16[416,3200]{1,0:T(8,128)(2,1)}, bf16[416,3200]{1,0:T(8,128)(2,1)}) custom-call(s32[1]{0:T(128)} %bitcast.2.core_ref, bf16[832,1152]{1,0:T(8,128)(2,1)} %bitcast.64, bf16[832,1024]{1,0:T(8,128)(2,1)} %bitcast.16.n_ref.refs_1_, bf16[3200,1152]{1,0:T(8,128)(2,1)} %get-tuple-element.100.refs_2_, bf16[3200,1024]{1,0:T(8,128)(2,1)} %get-tuple-element.102.refs_3_), custom_call_target="tpu_custom_call" | custom-call | flops 1000 | bytes 1000 | tf_op jit(solution)/shard_map/pallas_call | solution.py:713
  302.3 2.9 add_convert_fusion.1
  305.2 1.5 collective-permute-start.1
  307.4 1.6 add_convert_fusion
  309.0 1.6 collective-permute-start.4
  310.6 4.8 all-to-all-start.5
  316.2 6.1 %shard_map.203 = (f32[104,128]{1,0:T(8,128)}, f32[104,128]{1,0:T(8,128)}) custom-call(f32[2,104,128]{2,1,0:T(8,128)} %broadcast_in_dim.59.columns_ref, f32[48,104,384]{2,1,0:T(8,128)} %get-tuple-element.73.conv_ref, bf16[832,1152]{1,0:T(8,128)(2,1)} %bitcast.60, bf16[832,1024]{1,0:T(8,128)(2,1)} %bitcast.20.rest_1_), custom_call_target="tpu_custom_call" | custom-call | flops 1000 | bytes 1000 | tf_op jit(solution)/shard_map/pallas_call | solution.py:347
  323.2 0.9 reduce_sum.67
  324.2 17.5 %psum.37 = f32[5,100]{1,0:T(8,128)S(1)} all-reduce(f32[5,100]{1,0:T(8,128)S(1)} %pad_maximum_fusion.2), channel_id=1, replica_groups=mesh['dp'=4,'pair'=4,'core'=2] {'dp'}, use_global_device_ids=true, to_apply=%region_8.9 | all-reduce | flops 500 | bytes 4000 | tf_op jit(solution)/shard_map/psum | solution.py:902
  342.6 18.6 %shard_map.204 = (bf16[48,104,384]{2,1,0:T(8,128)(2,1)}, f32[49,104,128]{2,1,0:T(8,128)}) custom-call(f32[5,104,128]{2,1,0:T(8,128)} %broadcast_in_dim.63.columns_ref, f32[48,104,384]{2,1,0:T(8,128)} %get-tuple-element.73.conv_ref, bf16[48,100,360]{2,1,0:T(8,128)(2,1)} %bitcast.56, bf16[8,104,1152]{2,1,0:T(8,128)(2,1)} %copy-done.2, ...), custom_call_target="tpu_custom_call" | custom-call | flops 1000 | bytes 1000 | tf_op jit(solution)/shard_map/pallas_call | solution.py:419
  361.3 1.1 copy-done.13
  362.3 2.4 convert_add_fusion.1
  364.7 0.9 dynamic-slice_convert_fusion.1
  365.7 1.5 collective-permute-start.2
  367.2 2.2 convert_add_fusion
  369.4 1.5 copy-done.5
  370.9 0.9 dynamic-slice_convert_fusion
  371.8 18.6 %shard_map.206 = (bf16[48,104,384]{2,1,0:T(8,128)(2,1)}, f32[49,104,128]{2,1,0:T(8,128)}) custom-call(f32[5,104,128]{2,1,0:T(8,128)} %broadcast_in_dim.63.columns_ref, f32[48,104,384]{2,1,0:T(8,128)} %get-tuple-element.73.conv_ref, bf16[48,100,360]{2,1,0:T(8,128)(2,1)} %bitcast.57, ...), custom_call_target="tpu_custom_call", output_to_operand_aliasing={{0}: (5, {}), {1}: (6, {})} | custom-call | flops 1000 | bytes 1000 | tf_op jit(solution)/shard_map/pallas_call | solution.py:419
  390.4 2.5 add_convert_fusion.2
  392.9 23.1 %shard_map.207 = (bf16[48,104,384]{2,1,0:T(8,128)(2,1)}, f32[49,104,128]{2,1,0:T(8,128)}) custom-call(f32[5,104,128]{2,1,0:T(8,128)} %broadcast_in_dim.63.columns_ref, f32[48,104,384]{2,1,0:T(8,128)} %get-tuple-element.73.conv_ref, bf16[48,100,360]{2,1,0:T(8,128)(2,1)} %bitcast.58, ...), custom_call_target="tpu_custom_call", output_to_operand_aliasing={{0}: (5, {}), {1}: (6, {})} | custom-call | flops 1000 | bytes 1000 | tf_op jit(solution)/shard_map/pallas_call | solution.py:419
  416.0 2.7 reduce_sum.69
  418.7 2.1 collective-permute-start.6
  421.4 0.9 collective-permute-start.8
  422.3 33.8 %shard_map.208 = bf16[48,100,360]{2,1,0:T(8,128)(2,1)} custom-call(f32[49,104,128]{2,1,0:T(8,128)} %broadcast_in_dim.27.taps_ref, bf16[48,104,384]{2,1,0:T(8,128)(2,1)} %get-tuple-element.115.grad_ref, bf16[48,100,360]{2,1,0:T(8,128)(2,1)} %bitcast.62, s32[48,1,360]{2,1,0:T(1,128)} %broadcast_in_dim_squeeze.2.land_ref), custom_call_target="tpu_custom_call" | custom-call | flops 1000 | bytes 1000 | tf_op jit(solution)/shard_map/pallas_call | solution.py:474
  456.2 15.7 %all-gather.1 = f32[8,54,100]{2,1,0:T(8,128)} all-gather(f32[1,54,100]{2,1,0:T(8,128)S(1)} %maximum_bitcast_fusion), channel_id=2, replica_groups=mesh['dp'=4,'pair'=4,'core'=2] {'pair','core'}, dimensions={0}, use_global_device_ids=true | all-gather | bytes 194400 | tf_op jit(solution)/shard_map/all_gather | solution.py:926
  471.9 1.9 collective-permute-start.10
  474.4 6.1 %shard_map.209 = bf16[48,100,360]{2,1,0:T(8,128)(2,1)} custom-call(bf16[48,100,360]{2,1,0:T(8,128)(2,1)} %bitcast.59, s32[48,1,360]{2,1,0:T(1,128)} %broadcast_in_dim_squeeze.2.land_ref, bf16[832,2176]{1,0:T(8,128)(2,1)} %bitcast.28.branch_ref), custom_call_target="tpu_custom_call" | custom-call | flops 1000 | bytes 1000 | tf_op jit(solution)/shard_map/pallas_call | solution.py:503
  480.5 9.0 %collective-permute-done.10 = bf16[104,3200]{1,0:T(8,128)(2,1)S(1)} collective-permute-done((bf16[104,3200]{1,0:T(8,128)(2,1)}, bf16[104,3200]{1,0:T(8,128)(2,1)S(1)}, u32[]{:S(2)}, u32[]{:S(2)}) %collective-permute-start.10) | collective-permute-done | bytes 665632 | tf_op jit(solution)/shard_map/ppermute | solution.py:782
  489.5 1.5 collective-permute-done.9
  491.2 1.1 collective-permute-start.14
  493.7 28.0 %collective-permute-done.14.refs_1_ = bf16[208,3200]{1,0:T(8,128)(2,1)} collective-permute-done((bf16[208,3200]{1,0:T(8,128)(2,1)S(1)}, bf16[208,3200]{1,0:T(8,128)(2,1)}, u32[]{:S(2)}, u32[]{:S(2)}) %collective-permute-start.14) | collective-permute-done | bytes 1331232 | tf_op jit(solution)/shard_map/ppermute | solution.py:782
  521.7 1.3 collective-permute-done.11.refs_1_
  523.8 1.7 copy.53
  525.5 1.7 slice.69
  530.8 4.5 copy.56
  535.4 2.3 copy.55
  537.7 6.8 %shard_map.211 = f32[800,3200]{1,0:T(8,128)} custom-call(s32[1]{0:T(128)} %bitcast.36.place_ref, bf16[208,3200]{1,0:T(8,128)(2,1)} %copy-done.7, bf16[208,3200]{1,0:T(8,128)(2,1)} %collective-permute-done.14.refs_1_, bf16[208,3200]{1,0:T(8,128)(2,1)} %collective-permute-done.15.refs_2_, bf16[208,3200]{1,0:T(8,128)(2,1)} %collective-permute-done.16.refs_3_), custom_call_target="tpu_custom_call" | custom-call | flops 1000 | bytes 1000 | tf_op jit(solution)/shard_map/pallas_call | solution.py:741
  544.5 6.8 %shard_map.210 = f32[800,3200]{1,0:T(8,128)} custom-call(s32[1]{0:T(128)} %bitcast.34.place_ref, bf16[208,3200]{1,0:T(8,128)(2,1)} %copy-done.8, bf16[208,3200]{1,0:T(8,128)(2,1)} %collective-permute-done.11.refs_1_, bf16[208,3200]{1,0:T(8,128)(2,1)} %collective-permute-done.12.refs_2_, bf16[208,3200]{1,0:T(8,128)(2,1)} %collective-permute-done.13.refs_3_), custom_call_target="tpu_custom_call" | custom-call | flops 1000 | bytes 1000 | tf_op jit(solution)/shard_map/pallas_call | solution.py:741
  551.3 1.5 fusion.1
  (105 shorter events, 14.5 us)
Async XLA Ops:
  7.2 22.4 %copy-start = (bf16[49,800]{1,0:T(8,128)(2,1)S(1)}, bf16[49,800]{1,0:T(8,128)(2,1)}, u32[]{:S(2)}) copy-start(bf16[49,800]{1,0:T(8,128)(2,1)} %param.16) | copy-start | bytes 235204
  18.5 88.2 %all-to-all-start = ((bf16[8,104,2176]{2,1,0:T(8,128)(2,1)}), bf16[8,104,2176]{2,1,0:T(8,128)(2,1)}, u32[]{:S(2)}, u32[]{:S(2)}) async-start(bf16[8,104,2176]{2,1,0:T(8,128)(2,1)} %bitcast.70), calls=%async_computation | async-start | bytes 7241728 | tf_op jit(solution)/shard_map/all_to_all | solution.py:753
  106.7 48.7 %all-to-all-start.1 = ((bf16[8,104,1152]{2,1,0:T(8,128)(2,1)}), bf16[8,104,1152]{2,1,0:T(8,128)(2,1)S(1)}, u32[]{:S(2)}, u32[]{:S(2)}) async-start(bf16[8,104,1152]{2,1,0:T(8,128)(2,1)} %bitcast.72), calls=%async_computation.1 | async-start | bytes 3833856 | tf_op jit(solution)/shard_map/all_to_all | solution.py:753
  126.1 33.8 %copy-start.19 = (f32[3200]{0:T(1024)S(1)}, f32[3200]{0:T(1024)}, u32[]{:S(2)}) copy-start(f32[3200]{0:T(1024)} %param.21) | copy-start | bytes 38404
  126.1 35.5 %copy-start.20 = (f32[800]{0:T(1024)S(1)}, f32[800]{0:T(1024)}, u32[]{:S(2)}) copy-start(f32[800]{0:T(1024)} %param.23) | copy-start | bytes 9604
  155.4 7.2 %copy-start.3 = (bf16[8,104,1152]{2,1,0:T(8,128)(2,1)}, bf16[8,104,1152]{2,1,0:T(8,128)(2,1)S(1)}, u32[]{:S(2)}) copy-start(bf16[8,104,1152]{2,1,0:T(8,128)(2,1)S(1)} %all-to-all-done.1) | copy-start | bytes 5750788
  155.4 50.6 %all-to-all-start.2 = ((bf16[8,104,1024]{2,1,0:T(8,128)(2,1)}), bf16[8,104,1024]{2,1,0:T(8,128)(2,1)}, u32[]{:S(2)}, u32[]{:S(2)}) async-start(bf16[8,104,1024]{2,1,0:T(8,128)(2,1)} %bitcast.74), calls=%async_computation.2 | async-start | bytes 3407872 | tf_op jit(solution)/shard_map/all_to_all | solution.py:753
  206.0 50.5 %all-to-all-start.3 = ((bf16[8,104,1152]{2,1,0:T(8,128)(2,1)}), bf16[8,104,1152]{2,1,0:T(8,128)(2,1)S(1)}, u32[]{:S(2)}, u32[]{:S(2)}) async-start(bf16[8,104,1152]{2,1,0:T(8,128)(2,1)} %bitcast.71), calls=%async_computation.3 | async-start | bytes 3833856 | tf_op jit(solution)/shard_map/all_to_all | solution.py:753
  256.5 25.0 %copy-start.2 = (bf16[8,104,1152]{2,1,0:T(8,128)(2,1)}, bf16[8,104,1152]{2,1,0:T(8,128)(2,1)S(1)}, u32[]{:S(2)}) copy-start(bf16[8,104,1152]{2,1,0:T(8,128)(2,1)S(1)} %all-to-all-done.3.rest_0_) | copy-start | bytes 5750788
  256.5 45.8 %all-to-all-start.4 = ((bf16[8,104,1024]{2,1,0:T(8,128)(2,1)}), bf16[8,104,1024]{2,1,0:T(8,128)(2,1)}, u32[]{:S(2)}, u32[]{:S(2)}) async-start(bf16[8,104,1024]{2,1,0:T(8,128)(2,1)} %bitcast.73), calls=%async_computation.4 | async-start | bytes 3407872 | tf_op jit(solution)/shard_map/all_to_all | solution.py:753
  281.5 20.8 %collective-permute-start = (bf16[416,3200]{1,0:T(8,128)(2,1)}, bf16[416,3200]{1,0:T(8,128)(2,1)}, u32[]{:S(2)}, u32[]{:S(2)}) collective-permute-start(bf16[416,3200]{1,0:T(8,128)(2,1)} %get-tuple-element.94), channel_id=1, source_target_pairs={{0,1},{1,0},{2,3},{3,2},{4,5},{5,4},{6,7},{7,6},{8,9},{9,8},{10,11... | collective-permute-start | bytes 7987208 | tf_op jit(solution)/shard_map/ppermute | solution.py:769
  281.9 20.2 %copy-start.18 = (f32[104,128]{1,0:T(8,128)S(1)}, f32[104,128]{1,0:T(8,128)}, u32[]{:S(2)}) copy-start(f32[104,128]{1,0:T(8,128)} %get-tuple-element.97) | copy-start | bytes 159748
  281.9 20.3 %copy-start.9 = (bf16[416,3200]{1,0:T(8,128)(2,1)S(1)}, bf16[416,3200]{1,0:T(8,128)(2,1)}, u32[]{:S(2)}) copy-start(bf16[416,3200]{1,0:T(8,128)(2,1)} %get-tuple-element.93) | copy-start | bytes 7987204
  302.0 5.3 collective-permute-start.3
  302.2 5.1 copy-start.11
  305.2 56.1 %collective-permute-start.1 = (bf16[208,3200]{1,0:T(8,128)(2,1)}, bf16[208,3200]{1,0:T(8,128)(2,1)S(1)}, u32[]{:S(2)}, u32[]{:S(2)}) collective-permute-start(bf16[208,3200]{1,0:T(8,128)(2,1)} %add_convert_fusion.1), channel_id=1, source_target_pairs={{0,8},{8,0},{16,24},{24,16},{1,9},{9,1},{17,25},{25,17},{2,10},{10... | collective-permute-start | bytes 3993608 | tf_op jit(solution)/shard_map/ppermute | solution.py:782
  309.0 53.3 %collective-permute-start.4 = (bf16[208,3200]{1,0:T(8,128)(2,1)S(1)}, bf16[208,3200]{1,0:T(8,128)(2,1)}, u32[]{:S(2)}, u32[]{:S(2)}) collective-permute-start(bf16[208,3200]{1,0:T(8,128)(2,1)S(1)} %add_convert_fusion), channel_id=1, source_target_pairs={{0,16},{8,24},{16,0},{24,8},{1,17},{9,25},{17,1},{25,9},{2,18},{10... | collective-permute-start | bytes 3993608 | tf_op jit(solution)/shard_map/ppermute | solution.py:782
  310.6 163.8 %all-to-all-start.5 = ((bf16[8,104,2176]{2,1,0:T(8,128)(2,1)}), bf16[8,104,2176]{2,1,0:T(8,128)(2,1)}, u32[]{:S(2)}, u32[]{:S(2)}) async-start(bf16[8,104,2176]{2,1,0:T(8,128)(2,1)} %bitcast.67), calls=%async_computation.5 | async-start | bytes 7241728 | tf_op jit(solution)/shard_map/all_to_all | solution.py:753
  315.4 156.5 %all-reduce.9.cloned.1.call-start = ((), (), s32[]{:S(2)}) async-start(), calls=%async_computation.6 | async-start | bytes 2662400 | tf_op jit(solution)/shard_map/psum | solution.py:922
  342.6 19.7 %copy-start.10 = (bf16[416,3200]{1,0:T(8,128)(2,1)S(1)}, bf16[416,3200]{1,0:T(8,128)(2,1)}, u32[]{:S(2)}) copy-start(bf16[416,3200]{1,0:T(8,128)(2,1)} %get-tuple-element.93) | copy-start | bytes 7987204
  361.3 1.1 copy-start.13
  362.3 4.9 copy-start.12
  365.7 24.8 %collective-permute-start.2 = (bf16[104,3200]{1,0:T(8,128)(2,1)}, bf16[104,3200]{1,0:T(8,128)(2,1)S(1)}, u32[]{:S(2)}, u32[]{:S(2)}) collective-permute-start(bf16[104,3200]{1,0:T(8,128)(2,1)} %dynamic-slice_convert_fusion.1), channel_id=1, source_target_pairs={{0,16},{8,24},{16,0},{24,8},{1,17},{9,25},{17,1},{25,9},{2,18},{10... | collective-permute-start | bytes 1996808 | tf_op jit(solution)/shard_map/ppermute | solution.py:782
  369.3 1.5 copy-start.5
  371.8 18.7 %collective-permute-start.5 = (bf16[104,3200]{1,0:T(8,128)(2,1)}, bf16[104,3200]{1,0:T(8,128)(2,1)}, u32[]{:S(2)}, u32[]{:S(2)}) collective-permute-start(bf16[104,3200]{1,0:T(8,128)(2,1)} %dynamic-slice_convert_fusion), channel_id=1, source_target_pairs={{0,8},{8,0},{16,24},{24,16},{1,9},{9,1},{17,25},{25,17},{2,10},{10... | collective-permute-start | bytes 1996808 | tf_op jit(solution)/shard_map/ppermute | solution.py:782
  371.8 18.7 %copy-start.6 = (f32[208,3200]{1,0:T(8,128)S(1)}, f32[208,3200]{1,0:T(8,128)}, u32[]{:S(2)}) copy-start(f32[208,3200]{1,0:T(8,128)} %copy-done.5) | copy-start | bytes 7987204
  418.7 37.4 %collective-permute-start.6 = (f32[49,100]{1,0:T(8,128)S(1)}, f32[49,100]{1,0:T(8,128)S(1)}, u32[]{:S(2)}, u32[]{:S(2)}) collective-permute-start(f32[49,100]{1,0:T(8,128)S(1)} %bitcast.78), channel_id=1, source_target_pairs={{0,8},{8,0},{16,24},{24,16},{1,9},{9,1},{17,25},{25,17},{2,10},{10... | collective-permute-start | bytes 58808 | tf_op jit(solution)/shard_map/ppermute | solution.py:764
  420.8 35.4 %collective-permute-start.7 = (f32[49,100]{1,0:T(8,128)S(1)}, f32[49,100]{1,0:T(8,128)S(1)}, u32[]{:S(2)}, u32[]{:S(2)}) collective-permute-start(f32[49,100]{1,0:T(8,128)S(1)} %bitcast.79), channel_id=1, source_target_pairs={{0,16},{8,24},{16,0},{24,8},{1,17},{9,25},{17,1},{25,9},{2,18},{10... | collective-permute-start | bytes 58808 | tf_op jit(solution)/shard_map/ppermute | solution.py:764
  421.4 34.7 %collective-permute-start.8 = (f32[49,100]{1,0:T(8,128)S(1)}, f32[49,100]{1,0:T(8,128)S(1)}, u32[]{:S(2)}, u32[]{:S(2)}) collective-permute-start(f32[49,100]{1,0:T(8,128)S(1)} %bitcast.80), channel_id=1, source_target_pairs={{0,24},{8,16},{16,8},{24,0},{1,25},{9,17},{17,9},{25,1},{2,26},{10... | collective-permute-start | bytes 58808 | tf_op jit(solution)/shard_map/ppermute | solution.py:764
  471.9 17.6 %collective-permute-start.10 = (bf16[104,3200]{1,0:T(8,128)(2,1)}, bf16[104,3200]{1,0:T(8,128)(2,1)S(1)}, u32[]{:S(2)}, u32[]{:S(2)}) collective-permute-start(bf16[104,3200]{1,0:T(8,128)(2,1)} %get-tuple-element.118), channel_id=1, source_target_pairs={{0,8},{8,0},{16,24},{24,16},{1,9},{9,1},{17,25},{25,17},{2,10},{10... | collective-permute-start | bytes 1996808 | tf_op jit(solution)/shard_map/ppermute | solution.py:782
  473.8 17.1 %collective-permute-start.9 = (bf16[104,3200]{1,0:T(8,128)(2,1)}, bf16[104,3200]{1,0:T(8,128)(2,1)S(1)}, u32[]{:S(2)}, u32[]{:S(2)}) collective-permute-start(bf16[104,3200]{1,0:T(8,128)(2,1)} %get-tuple-element.117), channel_id=1, source_target_pairs={{0,16},{8,24},{16,0},{24,8},{1,17},{9,25},{17,1},{25,9},{2,18},{10... | collective-permute-start | bytes 1996808 | tf_op jit(solution)/shard_map/ppermute | solution.py:782
  474.4 16.5 %copy-start.15 = (bf16[104,3200]{1,0:T(8,128)(2,1)S(1)}, bf16[104,3200]{1,0:T(8,128)(2,1)}, u32[]{:S(2)}) copy-start(bf16[104,3200]{1,0:T(8,128)(2,1)} %get-tuple-element.117) | copy-start | bytes 1996804
  480.5 11.8 %copy-start.14 = (bf16[104,3200]{1,0:T(8,128)(2,1)S(1)}, bf16[104,3200]{1,0:T(8,128)(2,1)}, u32[]{:S(2)}) copy-start(bf16[104,3200]{1,0:T(8,128)(2,1)} %get-tuple-element.118) | copy-start | bytes 1996804
  489.5 1.6 copy-start.16
  491.1 1.3 copy-start.17
  491.2 2.0 copy-start.7
  491.2 30.5 %collective-permute-start.14 = (bf16[208,3200]{1,0:T(8,128)(2,1)S(1)}, bf16[208,3200]{1,0:T(8,128)(2,1)}, u32[]{:S(2)}, u32[]{:S(2)}) collective-permute-start(bf16[208,3200]{1,0:T(8,128)(2,1)S(1)} %pad_maximum_fusion.refs_0_), channel_id=1, source_target_pairs={{0,8},{8,0},{16,24},{24,16},{1,9},{9,1},{17,25},{25,17},{2,10},{10... | collective-permute-start | bytes 3993608 | tf_op jit(solution)/shard_map/ppermute | solution.py:782
  492.5 42.8 %copy-start.8 = (bf16[208,3200]{1,0:T(8,128)(2,1)}, bf16[208,3200]{1,0:T(8,128)(2,1)S(1)}, u32[]{:S(2)}) copy-start(bf16[208,3200]{1,0:T(8,128)(2,1)S(1)} %pad_maximum_fusion.1.refs_0_) | copy-start | bytes 3993604
  492.5 30.5 %collective-permute-start.11 = (bf16[208,3200]{1,0:T(8,128)(2,1)S(1)}, bf16[208,3200]{1,0:T(8,128)(2,1)}, u32[]{:S(2)}, u32[]{:S(2)}) collective-permute-start(bf16[208,3200]{1,0:T(8,128)(2,1)S(1)} %pad_maximum_fusion.1.refs_0_), channel_id=1, source_target_pairs={{0,16},{8,24},{16,0},{24,8},{1,17},{9,25},{17,1},{25,9},{2,18},{10... | collective-permute-start | bytes 3993608 | tf_op jit(solution)/shard_map/ppermute | solution.py:782
  493.2 44.5 %collective-permute-start.15 = (bf16[208,3200]{1,0:T(8,128)(2,1)S(1)}, bf16[208,3200]{1,0:T(8,128)(2,1)}, u32[]{:S(2)}, u32[]{:S(2)}) collective-permute-start(bf16[208,3200]{1,0:T(8,128)(2,1)S(1)} %pad_maximum_fusion.refs_0_), channel_id=1, source_target_pairs={{0,1},{1,0},{2,3},{3,2},{4,5},{5,4},{6,7},{7,6},{8,9},{9,8},{10,11... | collective-permute-start | bytes 3993608 | tf_op jit(solution)/shard_map/ppermute | solution.py:769
  493.2 51.2 %collective-permute-start.12 = (bf16[208,3200]{1,0:T(8,128)(2,1)S(1)}, bf16[208,3200]{1,0:T(8,128)(2,1)}, u32[]{:S(2)}, u32[]{:S(2)}) collective-permute-start(bf16[208,3200]{1,0:T(8,128)(2,1)S(1)} %pad_maximum_fusion.1.refs_0_), channel_id=1, source_target_pairs={{0,1},{1,0},{2,3},{3,2},{4,5},{5,4},{6,7},{7,6},{8,9},{9,8},{10,11... | collective-permute-start | bytes 3993608 | tf_op jit(solution)/shard_map/ppermute | solution.py:769
  521.7 16.0 %collective-permute-start.16 = (bf16[208,3200]{1,0:T(8,128)(2,1)}, bf16[208,3200]{1,0:T(8,128)(2,1)}, u32[]{:S(2)}, u32[]{:S(2)}) collective-permute-start(bf16[208,3200]{1,0:T(8,128)(2,1)} %collective-permute-done.14.refs_1_), channel_id=1, source_target_pairs={{0,1},{1,0},{2,3},{3,2},{4,5},{5,4},{6,7},{7,6},{8,9},{9,8},{10,11... | collective-permute-start | bytes 3993608 | tf_op jit(solution)/shard_map/ppermute | solution.py:769
  523.1 21.4 %collective-permute-start.13 = (bf16[208,3200]{1,0:T(8,128)(2,1)}, bf16[208,3200]{1,0:T(8,128)(2,1)}, u32[]{:S(2)}, u32[]{:S(2)}) collective-permute-start(bf16[208,3200]{1,0:T(8,128)(2,1)} %collective-permute-done.11.refs_1_), channel_id=1, source_target_pairs={{0,1},{1,0},{2,3},{3,2},{4,5},{5,4},{6,7},{7,6},{8,9},{9,8},{10,11... | collective-permute-start | bytes 3993608 | tf_op jit(solution)/shard_map/ppermute | solution.py:769
  530.8 4.6 copy-start.4
  544.5 8.4 %copy-start.1 = (bf16[49,800]{1,0:T(8,128)(2,1)S(1)}, bf16[49,800]{1,0:T(8,128)(2,1)}, u32[]{:S(2)}) copy-start(bf16[49,800]{1,0:T(8,128)(2,1)} %param.16) | copy-start | bytes 235204
Sparse Core Ops, SparseCore 0:
  393.0 62.0 all-reduce.8

commit v3 on v2

--- a/solution.py
+++ b/solution.py
@@ -5,6 +5,7 @@
 import jax.numpy as jnp
 from jax import lax
 from jax.experimental import pallas as pl
+from jax.experimental.layout import Layout, with_layout_constraint
 from jax.experimental.pallas import tpu as pltpu
 from jax.sharding import PartitionSpec as P
 
@@ -723,8 +724,9 @@
     )(core[None], *arrays, *rights)
 
 
-def unpad_rows(z, place, pieces):
+def unpad_rows(z, place, turn, pieces, before):
     groups, hidden = pieces[0].shape[0] // z.pad, pieces[0].shape[1]
+    before = [] if before is None else [before]
 
     def kernel(place_ref, *refs):
         out_ref = refs[-1]
@@ -734,19 +736,26 @@
             for k in range(groups):
                 out_ref[z.chan * k : z.chan * (k + 1), :] = value[z.pad * k : z.pad * k + z.chan, :]
 
-        wanted = jnp.bitwise_xor(pl.program_id(0), place_ref[0])
-        for k, ref in enumerate(refs[:-1]):
-            pl.when(wanted == k)(partial(put, ref))
+        for k in range(2):
+            pl.when(pl.program_id(0) == k)(partial(put, refs[k]))
 
     return pl.pallas_call(
         kernel,
-        grid=(4,),
-        in_specs=[smem()] + [whole(pieces[0].shape)] * 4,
-        out_specs=pl.BlockSpec((groups * z.chan, hidden), lambda q: (q, 0)),
+        grid_spec=pltpu.PrefetchScalarGridSpec(
+            num_scalar_prefetch=1,
+            grid=(2,),
+            in_specs=[pl.BlockSpec(pieces[0].shape, lambda k, place_ref: (0, 0))] * 2
+            + [pl.BlockSpec(memory_space=pl.ANY)] * len(before),
+            out_specs=pl.BlockSpec(
+                (groups * z.chan, hidden),
+                lambda k, place_ref: (jnp.bitwise_xor(2 * k + turn, place_ref[0]), 0),
+            ),
+        ),
         out_shape=jax.ShapeDtypeStruct((4 * groups * z.chan, hidden), F32),
-        compiler_params=params(),
-        cost_estimate=cost(),
-    )(place[None], *pieces)
+        input_output_aliases={3: 0} if before else {},
+        compiler_params=params(),
+        cost_estimate=cost(),
+    )(place[None], *pieces, *before)
 
 
 def exchange(value):
@@ -790,7 +799,8 @@
 
     def first(self, ready):
         self.mine = after(self.mine, ready)
-        self.arrived = self.meet(self.pair(1 - self.bits[0]).astype(BF16), self.turns[0])
+        self.sent = self.pair(1 - self.bits[0]).astype(BF16)
+        self.arrived = self.meet(self.sent, self.turns[0])
 
     def second(self, ready):
         arrived = after(self.arrived, ready)
@@ -817,16 +827,21 @@
         self.arrived = self.meet(self.own, self.turns[0])
         self.swapped = swap_cores(self.own)
 
+    def begin(self, z):
+        self.place = self.core * 2 + self.bits[0]
+        self.result = unpad_rows(z, self.place, 0, [self.own, self.swapped], None)
+        return self.result
+
     def finish(self, z, ready):
         other = after(self.arrived, ready)
-        pieces = [self.own, other, self.swapped, swap_cores(other)]
-        return unpad_rows(z, self.core * 2 + self.bits[0], pieces), pieces
-
-    def first_row(self, pieces, row):
-        place = self.core * 2 + self.bits[0]
-        found = pieces[0][row]
+        swapped = swap_cores(other)
+        self.pieces = [self.own, other, self.swapped, swapped]
+        return unpad_rows(z, self.place, 1, [other, swapped], self.result)
+
+    def first_row(self, row):
+        found = self.pieces[0][row]
         for k in range(1, 4):
-            found = jnp.where(place == k, pieces[k][row], found)
+            found = jnp.where(self.place == k, self.pieces[k][row], found)
         return found.astype(F32)
 
 
@@ -891,8 +906,6 @@
     )
     sum_in = HalvingSum((2, 1), mine, sent_in)
     branch = exchange(after(branch, norm_parts[1], sent_in))
-    sum_out.first(norm_parts[1])
-    sum_in.first(norm_parts[1])
 
     part_shift, part_gain = norm_sums(z, norm_parts, conv, over_lanes(jnp.stack([mean, scale])))
     small = jnp.concatenate(
@@ -903,6 +916,9 @@
     terms = over_lanes(
         jnp.stack([mean, scale, own_gain * scale, small[0] / pixels, small[1] / pixels])
     )
+    sum_out.first(small)
+    sum_in.first(small)
+    terms = after(terms, sum_out.sent, sum_in.sent)
     calls = pl.cdiv(chan, GROUP)
     cuts = [0, min(2, calls), min(4, calls), calls]
     cuts = [cut for k, cut in enumerate(cuts) if k == 0 or cut > cuts[k - 1]]
@@ -922,29 +938,33 @@
     shares = lax.psum(shares, "pair")
     g_kernel = dp_sum(jnp.sum(products, axis=2)[:, :chan])
     x_grad = conv_backward(z, taps, conv_grad, cot, land3)
-    rows = jnp.concatenate([after(g_kernel, x_grad), small], axis=0)
+    sum_out.back_first(after(shares[0], x_grad))
+    sum_in.back_first(after(shares[1], x_grad))
+    rows = jnp.concatenate([after(g_kernel, sum_out.own, sum_in.own), small], axis=0)
     gathered = lax.all_gather(rows, CHAN)
     placed = jnp.transpose(gathered, (1, 0, 2)).reshape(rows.shape[0], width)
-    sum_out.back_first(after(shares[0], gathered))
-    sum_in.back_first(after(shares[1], gathered))
-    mixed = mix_branch(z, branch, after(x, sum_out.own, sum_in.own), land3)
-    sum_out.back_second(mixed)
-    sum_in.back_second(mixed)
-    mixed = after(mixed, sum_out.own, sum_in.own)
-    mixed_out = jnp.transpose(mixed, (0, 2, 1))[None]
-    x_grad_out = jnp.transpose(after(x_grad, sum_out.own, sum_in.own), (0, 2, 1))[None]
-    g_w_out_t, _ = sum_out.finish(z, x_grad_out)
-    g_w_in, pieces = sum_in.finish(z, x_grad_out)
+    sum_out.back_second(gathered)
+    sum_in.back_second(gathered)
+
+    def as_output(value):
+        value = jnp.transpose(after(value, sum_out.own, sum_in.own), (0, 2, 1))[None]
+        return with_layout_constraint(value, Layout(major_to_minor=(0, 3, 1, 2)))
+
+    mixed = as_output(mix_branch(z, branch, after(x, sum_out.own, sum_in.own), land3))
+    x_grad = as_output(x_grad)
+    early = sum_out.begin(z), sum_in.begin(z)
+    g_w_out_t = sum_out.finish(z, (mixed, x_grad, early))
+    g_w_in = sum_in.finish(z, (mixed, x_grad, early))
 
     return (
-        mixed_out,
-        x_grad_out,
+        mixed,
+        x_grad,
         placed[:ntaps],
         placed[ntaps + 1],
         placed[ntaps],
         placed[ntaps + 2 : ntaps + 4],
         g_w_in,
-        sum_in.first_row(pieces, chan),
+        sum_in.first_row(chan),
         g_w_out_t.T,
         placed[ntaps + 4],
     )

time: 567 us -> 601 us (1.060)
  waiting for transfers between devices: 94.5 us -> 129 us
  blocking collectives: 43.1 us -> 35.1 us
    psum x1, waiting for transfers between devices: 0.01 us -> 45.5 us  [per_device(): shares = lax.psum(shares, 'pair')]
    ppermute x8, waiting for transfers between devices: 39.8 us -> 15.1 us  [meet(): return lax.ppermute(value, 'dp', [(i, i ^ turn) for i in range(ways)])]
    ppermute x3, waiting for transfers between devices: 0.01 us -> 14.1 us  [dp_sum(): lax.ppermute(value, 'dp', [(i, i ^ turn) for i in range(ways)])]
    optimization_barrier x0 -> x2, local copies, waits for them, and re-layouts: none -> 8.8 us  [after(): return lax.optimization_barrier((value, *others))[0]]
    psum x1, blocking collectives: 17.5 us -> 9.93 us  [per_device(): small = lax.psum(small, 'dp')]
    unnamed x46 -> x40, local copies, waits for them, and re-layouts: 19 us -> 14.3 us
    pallas_call x2 -> x4, Pallas kernels: 13.6 us -> 17.1 us  [unpad_rows(): pl.pallas_call(kernel, grid_spec=pltpu.PrefetchScalarGridSpec(num_scalar_...]
  transfers between devices with their start and end apart: 24 -> 24, of which waited for: 8 -> 10; matrix products, arithmetic and copies ran while one was open for 9% -> 8% of each run, Pallas kernels for 52% -> 50%
where the time goes in v3:
time: 601 us; the launch traced here: 594 us
  Pallas kernels  308 us (51%)
  waiting for transfers between devices  129 us (21%)
  starting transfers between devices  41.3 us (7%)
  local copies, waits for them, and re-layouts  40.6 us (7%)
  blocking collectives  35.1 us (6%)
  other arithmetic  24.9 us (4%)
  between operations  15.2 us (3%)
    pallas_call x2, Pallas kernels, mlp(): pl.pallas_call(kernel, grid=(blocks + outs,), in_specs=in_specs, out_spec...  81.1 us
    pallas_call x3, Pallas kernels, conv_gradient(): pl.pallas_call(kernel, grid=(end - begin,), in_specs=[group((5, GROUP, LA...  60.4 us
    all_to_all x6, waiting for transfers between devices, exchange(): return lax.all_to_all(value, CHAN, split_axis=0, concat_axis=0, tiled=True)  54.1 us
    psum x1, waiting for transfers between devices, per_device(): shares = lax.psum(shares, 'pair')  45.5 us
    pallas_call x2, Pallas kernels, weight_grad(): pl.pallas_call(kernel, grid=(hidden // block,), in_specs=[smem()] + [whol...  40.5 us
    pallas_call x1, Pallas kernels, conv_forward(): pl.pallas_call(kernel, grid=(pl.cdiv(z.chan, GROUP),), in_specs=[group_la...  36.3 us
    pallas_call x1, Pallas kernels, conv_backward(): pl.pallas_call(kernel, grid=(pl.cdiv(z.chan, GROUP),), in_specs=[group_la...  33.9 us
    all_to_all x6, starting transfers between devices, exchange(): return lax.all_to_all(value, CHAN, split_axis=0, concat_axis=0, tiled=True)  29.2 us
  transfers between devices with their start and end apart: 24, of which 10 were waited for; matrix products, arithmetic and copies ran while one was open for 8% of the time, Pallas kernels for 50%

profile of v3, /device:TPU:0, one launch (start us, length us, event | category | flops | bytes accessed | tf_op | source)
XLA Modules:
  0.0 594.2 jit_solution(18173002303981414427)
XLA Ops:
  7.2 1.6 broadcast_in_dim_squeeze.2.land_ref
  8.8 4.7 copy.63
  13.5 5.0 shard_map.195
  18.5 6.3 %all-to-all-start = ((bf16[8,104,2176]{2,1,0:T(8,128)(2,1)}), bf16[8,104,2176]{2,1,0:T(8,128)(2,1)}, u32[]{:S(2)}, u32[]{:S(2)}) async-start(bf16[8,104,2176]{2,1,0:T(8,128)(2,1)} %bitcast.74), calls=%async_computation | async-start | bytes 7241728 | tf_op jit(solution)/shard_map/all_to_all | solution.py:762
  24.9 4.7 copy.64
  29.7 1.9 broadcast_in_dim.27.taps_ref
  31.6 36.3 %shard_map.196 = (f32[48,104,384]{2,1,0:T(8,128)}, f32[104,128]{1,0:T(8,128)}, f32[104,128]{1,0:T(8,128)}) custom-call(f32[49,104,128]{2,1,0:T(8,128)} %broadcast_in_dim.27.taps_ref, bf16[48,100,360]{2,1,0:T(8,128)(2,1)} %bitcast.59), custom_call_target="tpu_custom_call" | custom-call | flops 1000 | bytes 1000 | tf_op jit(solution)/shard_map/pallas_call | solution.py:277
  70.4 9.9 %all-reduce.5 = (f32[100]{0:T(128)S(1)}, f32[100]{0:T(128)S(1)}) all-reduce(f32[100]{0:T(128)S(1)} %bitcast.87, f32[100]{0:T(128)S(1)} %bitcast.88), channel_id=1, replica_groups=mesh['dp'=4,'pair'=4,'core'=2] {'dp'}, use_global_device_ids=true, to_apply=%region_3.4 | all-reduce | flops 200 | bytes 1600 | tf_op jit(solution)/shard_map/psum | solution.py:878
  83.4 5.9 %shard_map.197 = (bf16[832,1152]{1,0:T(8,128)(2,1)}, bf16[832,1024]{1,0:T(8,128)(2,1)}) custom-call(f32[3,104,128]{2,1,0:T(8,128)} %broadcast_in_dim.28.columns_ref, f32[48,104,384]{2,1,0:T(8,128)} %get-tuple-element.74.conv_ref), custom_call_target="tpu_custom_call" | custom-call | flops 1000 | bytes 1000 | tf_op jit(solution)/shard_map/pallas_call | solution.py:311
  89.4 17.3 %all-to-all-done = bf16[8,104,2176]{2,1,0:T(8,128)(2,1)} async-done(((bf16[8,104,2176]{2,1,0:T(8,128)(2,1)}), bf16[8,104,2176]{2,1,0:T(8,128)(2,1)}, u32[]{:S(2)}, u32[]{:S(2)}) %all-to-all-start) | async-done | bytes 3620896 | tf_op jit(solution)/shard_map/all_to_all | solution.py:762
  106.7 3.6 all-to-all-start.1
  110.3 7.9 %shard_map.198 = (bf16[832,3200]{1,0:T(8,128)(2,1)}, bf16[3200,832]{1,0:T(8,128)(2,1)}) custom-call(bf16[800,3200]{1,0:T(8,128)(2,1)} %in_ref), custom_call_target="tpu_custom_call" | custom-call | flops 1000 | bytes 1000 | tf_op jit(solution)/shard_map/pallas_call | solution.py:549
  118.2 7.8 %shard_map.199 = (bf16[832,3200]{1,0:T(8,128)(2,1)}, bf16[3200,832]{1,0:T(8,128)(2,1)}) custom-call(bf16[800,3200]{1,0:T(8,128)(2,1)} %bitcast.71), custom_call_target="tpu_custom_call" | custom-call | flops 1000 | bytes 1000 | tf_op jit(solution)/shard_map/pallas_call | solution.py:549
  126.0 29.4 %all-to-all-done.1 = bf16[8,104,1152]{2,1,0:T(8,128)(2,1)S(1)} async-done(((bf16[8,104,1152]{2,1,0:T(8,128)(2,1)}), bf16[8,104,1152]{2,1,0:T(8,128)(2,1)S(1)}, u32[]{:S(2)}, u32[]{:S(2)}) %all-to-all-start.1) | async-done | bytes 1916960 | tf_op jit(solution)/shard_map/all_to_all | solution.py:762
  155.4 4.5 all-to-all-start.2
  159.9 1.7 broadcast_in_dim.70.b_in_ref
  162.6 43.4 %shard_map.200 = (bf16[832,2176]{1,0:T(8,128)(2,1)}, bf16[832,1152]{1,0:T(8,128)(2,1)}, bf16[3200,1152]{1,0:T(8,128)(2,1)}, bf16[3200,1152]{1,0:T(8,128)(2,1)}) custom-call(bf16[832,1152]{1,0:T(8,128)(2,1)} %bitcast.68, bf16[832,2176]{1,0:T(8,128)(2,1)} %bitcast.6.g_ref.refs_0_, bf16[3200,832]{1,0:T(8,128)(2,1)} %get-tuple-element.78.w_in_t_ref, ...), custom_call_target="tpu_custom_call" | custom-call | flops 1000 | bytes 1000 | tf_op jit(solution)/shard_map/pallas_call | solution.py:665
  206.0 5.3 all-to-all-start.3
  211.3 37.8 %shard_map.201 = (bf16[832,2176]{1,0:T(8,128)(2,1)}, bf16[832,1024]{1,0:T(8,128)(2,1)}, bf16[3200,1024]{1,0:T(8,128)(2,1)}, bf16[3200,1024]{1,0:T(8,128)(2,1)}) custom-call(bf16[832,1024]{1,0:T(8,128)(2,1)} %bitcast.16.n_ref.refs_1_, bf16[832,2176]{1,0:T(8,128)(2,1)} %bitcast.6.g_ref.refs_0_, ...), custom_call_target="tpu_custom_call", output_to_operand_aliasing={{0}: (8, {})} | custom-call | flops 1000 | bytes 1000 | tf_op jit(solution)/shard_map/pallas_call | solution.py:665
  249.1 7.4 %all-to-all-done.3.rest_0_ = bf16[8,104,1152]{2,1,0:T(8,128)(2,1)S(1)} async-done(((bf16[8,104,1152]{2,1,0:T(8,128)(2,1)}), bf16[8,104,1152]{2,1,0:T(8,128)(2,1)S(1)}, u32[]{:S(2)}, u32[]{:S(2)}) %all-to-all-start.3) | async-done | bytes 1916960 | tf_op jit(solution)/shard_map/all_to_all | solution.py:762
  256.5 4.7 all-to-all-start.4
  261.2 20.5 %shard_map.202 = (bf16[416,3200]{1,0:T(8,128)(2,1)}, bf16[416,3200]{1,0:T(8,128)(2,1)}) custom-call(s32[1]{0:T(128)} %bitcast.2.core_ref, bf16[832,2176]{1,0:T(8,128)(2,1)} %bitcast.6.g_ref.refs_0_, bf16[3200,1152]{1,0:T(8,128)(2,1)} %get-tuple-element.83.refs_1_, bf16[3200,1024]{1,0:T(8,128)(2,1)} %get-tuple-element.90.refs_2_), custom_call_target="tpu_custom_call" | custom-call | flops 1000 | bytes 1000 | tf_op jit(solution)/shard_map/pallas_call | solution.py:714
  282.1 20.0 %shard_map.204 = (bf16[416,3200]{1,0:T(8,128)(2,1)}, bf16[416,3200]{1,0:T(8,128)(2,1)}) custom-call(s32[1]{0:T(128)} %bitcast.2.core_ref, bf16[832,1152]{1,0:T(8,128)(2,1)} %bitcast.69, bf16[832,1024]{1,0:T(8,128)(2,1)} %bitcast.16.n_ref.refs_1_, bf16[3200,1152]{1,0:T(8,128)(2,1)} %get-tuple-element.99.refs_2_, bf16[3200,1024]{1,0:T(8,128)(2,1)} %get-tuple-element.101.refs_3_), custom_call_target="tpu_custom_call" | custom-call | flops 1000 | bytes 1000 | tf_op jit(solution)/shard_map/pallas_call | solution.py:714
  303.0 6.3 %shard_map.203 = (f32[104,128]{1,0:T(8,128)}, f32[104,128]{1,0:T(8,128)}) custom-call(f32[2,104,128]{2,1,0:T(8,128)} %broadcast_in_dim.30.columns_ref, f32[48,104,384]{2,1,0:T(8,128)} %get-tuple-element.74.conv_ref, bf16[832,1152]{1,0:T(8,128)(2,1)} %bitcast.64, bf16[832,1024]{1,0:T(8,128)(2,1)} %bitcast.21.rest_1_), custom_call_target="tpu_custom_call" | custom-call | flops 1000 | bytes 1000 | tf_op jit(solution)/shard_map/pallas_call | solution.py:348
  311.3 9.9 %psum.37 = f32[5,100]{1,0:T(8,128)S(1)} all-reduce(f32[5,100]{1,0:T(8,128)S(1)} %pad_maximum_fusion.2), channel_id=1, replica_groups=mesh['dp'=4,'pair'=4,'core'=2] {'dp'}, use_global_device_ids=true, to_apply=%region_8.9 | all-reduce | flops 500 | bytes 4000 | tf_op jit(solution)/shard_map/psum | solution.py:915
  321.2 2.9 add_convert_fusion.1
  324.1 1.6 add_convert_fusion
  325.8 1.2 collective-permute-start.4
  327.9 18.6 %shard_map.205 = (bf16[48,104,384]{2,1,0:T(8,128)(2,1)}, f32[49,104,128]{2,1,0:T(8,128)}) custom-call(f32[5,104,128]{2,1,0:T(8,128)} %broadcast_in_dim.65.columns_ref, f32[48,104,384]{2,1,0:T(8,128)} %get-tuple-element.74.conv_ref, bf16[48,100,360]{2,1,0:T(8,128)(2,1)} %bitcast.60, bf16[8,104,1152]{2,1,0:T(8,128)(2,1)} %copy-done.2, ...), custom_call_target="tpu_custom_call" | custom-call | flops 1000 | bytes 1000 | tf_op jit(solution)/shard_map/pallas_call | solution.py:420
  346.5 7.4 %collective-permute-done.1 = bf16[208,3200]{1,0:T(8,128)(2,1)S(1)} collective-permute-done((bf16[208,3200]{1,0:T(8,128)(2,1)}, bf16[208,3200]{1,0:T(8,128)(2,1)S(1)}, u32[]{:S(2)}, u32[]{:S(2)}) %collective-permute-start.1) | collective-permute-done | bytes 1331232 | tf_op jit(solution)/shard_map/ppermute | solution.py:791
  353.9 1.1 copy-done.14
  355.5 2.5 convert_add_fusion.1
  358.0 2.2 convert_add_fusion
  360.2 1.5 copy-done.5
  361.7 1.0 dynamic-slice_convert_fusion
  362.7 1.5 collective-permute-start.5
  364.9 4.8 all-to-all-start.5
  369.9 18.7 %shard_map.206 = (bf16[48,104,384]{2,1,0:T(8,128)(2,1)}, f32[49,104,128]{2,1,0:T(8,128)}) custom-call(f32[5,104,128]{2,1,0:T(8,128)} %broadcast_in_dim.65.columns_ref, f32[48,104,384]{2,1,0:T(8,128)} %get-tuple-element.74.conv_ref, bf16[48,100,360]{2,1,0:T(8,128)(2,1)} %bitcast.61, ...), custom_call_target="tpu_custom_call", output_to_operand_aliasing={{0}: (5, {}), {1}: (6, {})} | custom-call | flops 1000 | bytes 1000 | tf_op jit(solution)/shard_map/pallas_call | solution.py:420
  388.6 2.1 add_convert_fusion.2
  390.7 2.1 add_convert_fusion.3
  392.8 23.1 %shard_map.207 = (bf16[48,104,384]{2,1,0:T(8,128)(2,1)}, f32[49,104,128]{2,1,0:T(8,128)}) custom-call(f32[5,104,128]{2,1,0:T(8,128)} %broadcast_in_dim.65.columns_ref, f32[48,104,384]{2,1,0:T(8,128)} %get-tuple-element.74.conv_ref, bf16[48,100,360]{2,1,0:T(8,128)(2,1)} %bitcast.62, ...), custom_call_target="tpu_custom_call", output_to_operand_aliasing={{0}: (5, {}), {1}: (6, {})} | custom-call | flops 1000 | bytes 1000 | tf_op jit(solution)/shard_map/pallas_call | solution.py:420
  415.9 33.9 %shard_map.208 = bf16[48,100,360]{2,1,0:T(8,128)(2,1)} custom-call(f32[49,104,128]{2,1,0:T(8,128)} %broadcast_in_dim.27.taps_ref, bf16[48,104,384]{2,1,0:T(8,128)(2,1)} %get-tuple-element.116.grad_ref, bf16[48,100,360]{2,1,0:T(8,128)(2,1)} %bitcast.67, s32[48,1,360]{2,1,0:T(1,128)} %broadcast_in_dim_squeeze.2.land_ref), custom_call_target="tpu_custom_call" | custom-call | flops 1000 | bytes 1000 | tf_op jit(solution)/shard_map/pallas_call | solution.py:475
  449.9 45.5 %all-reduce.9.cloned.1.call-done = (bf16[104,3200]{1,0:T(8,128)(2,1)}, bf16[104,3200]{1,0:T(8,128)(2,1)}) async-done(((bf16[104,3200]{1,0:T(8,128)(2,1)}, bf16[104,3200]{1,0:T(8,128)(2,1)}), (bf16[104,3200]{1,0:T(8,128)(2,1)}, bf16[104,3200]{1,0:T(8,128)(2,1)})) %all-reduce.9.cloned.1.call-update) | async-done | bytes 1331216 | tf_op jit(solution)/shard_map/psum | solution.py:938
  496.8 1.6 collective-permute-start.7
  498.4 1.3 collective-permute-start.8
  500.3 13.1 %collective-permute-done.7 = f32[49,100]{1,0:T(8,128)S(1)} collective-permute-done((f32[49,100]{1,0:T(8,128)S(1)}, f32[49,100]{1,0:T(8,128)S(1)}, u32[]{:S(2)}, u32[]{:S(2)}) %collective-permute-start.7) | collective-permute-done | bytes 19632 | tf_op jit(solution)/shard_map/ppermute | solution.py:773
  513.4 1.0 collective-permute-done.9
  515.3 15.2 %all-gather.1 = f32[8,54,100]{2,1,0:T(8,128)} all-gather(f32[1,54,100]{2,1,0:T(8,128)S(1)} %maximum_bitcast_fusion), channel_id=2, replica_groups=mesh['dp'=4,'pair'=4,'core'=2] {'pair','core'}, dimensions={0}, use_global_device_ids=true | all-gather | bytes 194400 | tf_op jit(solution)/shard_map/all_gather | solution.py:944
  530.5 1.4 broadcast_select_fusion.1
  532.4 1.3 broadcast_select_fusion.3
  534.2 1.3 collective-permute-start.11
  536.1 4.4 copy.65
  540.5 4.3 shard_map.211.refs_2_
  544.8 4.3 shard_map.210.refs_2_
  549.0 6.0 %shard_map.209 = bf16[48,100,360]{2,1,0:T(8,128)(2,1)} custom-call(bf16[48,100,360]{2,1,0:T(8,128)(2,1)} %bitcast.63, s32[48,1,360]{2,1,0:T(1,128)} %broadcast_in_dim_squeeze.2.land_ref, bf16[832,2176]{1,0:T(8,128)(2,1)} %bitcast.28.branch_ref), custom_call_target="tpu_custom_call" | custom-call | flops 1000 | bytes 1000 | tf_op jit(solution)/shard_map/pallas_call | solution.py:504
  555.1 4.4 copy.66
  559.5 6.2 %collective-permute-done.11.refs_0_ = bf16[208,3200]{1,0:T(8,128)(2,1)} collective-permute-done((bf16[208,3200]{1,0:T(8,128)(2,1)S(1)}, bf16[208,3200]{1,0:T(8,128)(2,1)}, u32[]{:S(2)}, u32[]{:S(2)}) %collective-permute-start.11) | collective-permute-done | bytes 1331232 | tf_op jit(solution)/shard_map/ppermute | solution.py:791
  567.9 1.7 copy.57
  569.5 1.7 slice.69
  574.9 1.1 copy-done.15
  576.0 4.2 shard_map.213
  580.3 1.1 copy-done.13
  581.3 4.3 shard_map.212
  585.6 1.5 fusion.1
  (103 shorter events, 22.2 us)
Async XLA Ops:
  7.2 22.4 %copy-start = (bf16[49,800]{1,0:T(8,128)(2,1)S(1)}, bf16[49,800]{1,0:T(8,128)(2,1)}, u32[]{:S(2)}) copy-start(bf16[49,800]{1,0:T(8,128)(2,1)} %param.16) | copy-start | bytes 235204
  18.5 88.2 %all-to-all-start = ((bf16[8,104,2176]{2,1,0:T(8,128)(2,1)}), bf16[8,104,2176]{2,1,0:T(8,128)(2,1)}, u32[]{:S(2)}, u32[]{:S(2)}) async-start(bf16[8,104,2176]{2,1,0:T(8,128)(2,1)} %bitcast.74), calls=%async_computation | async-start | bytes 7241728 | tf_op jit(solution)/shard_map/all_to_all | solution.py:762
  106.7 48.7 %all-to-all-start.1 = ((bf16[8,104,1152]{2,1,0:T(8,128)(2,1)}), bf16[8,104,1152]{2,1,0:T(8,128)(2,1)S(1)}, u32[]{:S(2)}, u32[]{:S(2)}) async-start(bf16[8,104,1152]{2,1,0:T(8,128)(2,1)} %bitcast.76), calls=%async_computation.1 | async-start | bytes 3833856 | tf_op jit(solution)/shard_map/all_to_all | solution.py:762
  126.0 33.9 %copy-start.17 = (f32[3200]{0:T(1024)S(1)}, f32[3200]{0:T(1024)}, u32[]{:S(2)}) copy-start(f32[3200]{0:T(1024)} %param.21) | copy-start | bytes 38404
  126.0 35.6 %copy-start.18 = (f32[800]{0:T(1024)S(1)}, f32[800]{0:T(1024)}, u32[]{:S(2)}) copy-start(f32[800]{0:T(1024)} %param.23) | copy-start | bytes 9604
  155.4 7.2 %copy-start.4 = (bf16[8,104,1152]{2,1,0:T(8,128)(2,1)}, bf16[8,104,1152]{2,1,0:T(8,128)(2,1)S(1)}, u32[]{:S(2)}) copy-start(bf16[8,104,1152]{2,1,0:T(8,128)(2,1)S(1)} %all-to-all-done.1) | copy-start | bytes 5750788
  155.4 50.6 %all-to-all-start.2 = ((bf16[8,104,1024]{2,1,0:T(8,128)(2,1)}), bf16[8,104,1024]{2,1,0:T(8,128)(2,1)}, u32[]{:S(2)}, u32[]{:S(2)}) async-start(bf16[8,104,1024]{2,1,0:T(8,128)(2,1)} %bitcast.78), calls=%async_computation.2 | async-start | bytes 3407872 | tf_op jit(solution)/shard_map/all_to_all | solution.py:762
  206.0 50.5 %all-to-all-start.3 = ((bf16[8,104,1152]{2,1,0:T(8,128)(2,1)}), bf16[8,104,1152]{2,1,0:T(8,128)(2,1)S(1)}, u32[]{:S(2)}, u32[]{:S(2)}) async-start(bf16[8,104,1152]{2,1,0:T(8,128)(2,1)} %bitcast.75), calls=%async_computation.3 | async-start | bytes 3833856 | tf_op jit(solution)/shard_map/all_to_all | solution.py:762
  256.5 25.2 %copy-start.2 = (bf16[8,104,1152]{2,1,0:T(8,128)(2,1)}, bf16[8,104,1152]{2,1,0:T(8,128)(2,1)S(1)}, u32[]{:S(2)}) copy-start(bf16[8,104,1152]{2,1,0:T(8,128)(2,1)S(1)} %all-to-all-done.3.rest_0_) | copy-start | bytes 5750788
  256.5 45.8 %all-to-all-start.4 = ((bf16[8,104,1024]{2,1,0:T(8,128)(2,1)}), bf16[8,104,1024]{2,1,0:T(8,128)(2,1)}, u32[]{:S(2)}, u32[]{:S(2)}) async-start(bf16[8,104,1024]{2,1,0:T(8,128)(2,1)} %bitcast.77), calls=%async_computation.4 | async-start | bytes 3407872 | tf_op jit(solution)/shard_map/all_to_all | solution.py:762
  281.6 39.6 %collective-permute-start = (bf16[416,3200]{1,0:T(8,128)(2,1)}, bf16[416,3200]{1,0:T(8,128)(2,1)}, u32[]{:S(2)}, u32[]{:S(2)}) collective-permute-start(bf16[416,3200]{1,0:T(8,128)(2,1)} %get-tuple-element.98), channel_id=1, source_target_pairs={{0,1},{1,0},{2,3},{3,2},{4,5},{5,4},{6,7},{7,6},{8,9},{9,8},{10,11... | collective-permute-start | bytes 7987208 | tf_op jit(solution)/shard_map/ppermute | solution.py:778
  282.1 20.1 %copy-start.16 = (f32[104,128]{1,0:T(8,128)S(1)}, f32[104,128]{1,0:T(8,128)}, u32[]{:S(2)}) copy-start(f32[104,128]{1,0:T(8,128)} %get-tuple-element.96) | copy-start | bytes 159748
  302.1 22.1 %collective-permute-start.2 = (bf16[416,3200]{1,0:T(8,128)(2,1)}, bf16[416,3200]{1,0:T(8,128)(2,1)}, u32[]{:S(2)}, u32[]{:S(2)}) collective-permute-start(bf16[416,3200]{1,0:T(8,128)(2,1)} %get-tuple-element.104), channel_id=1, source_target_pairs={{0,1},{1,0},{2,3},{3,2},{4,5},{5,4},{6,7},{7,6},{8,9},{9,8},{10,11... | collective-permute-start | bytes 7987208 | tf_op jit(solution)/shard_map/ppermute | solution.py:778
  303.0 18.2 %copy-start.9 = (bf16[416,3200]{1,0:T(8,128)(2,1)S(1)}, bf16[416,3200]{1,0:T(8,128)(2,1)}, u32[]{:S(2)}) copy-start(bf16[416,3200]{1,0:T(8,128)(2,1)} %get-tuple-element.97) | copy-start | bytes 7987204
  321.2 2.9 copy-start.11
  324.1 29.8 %collective-permute-start.1 = (bf16[208,3200]{1,0:T(8,128)(2,1)}, bf16[208,3200]{1,0:T(8,128)(2,1)S(1)}, u32[]{:S(2)}, u32[]{:S(2)}) collective-permute-start(bf16[208,3200]{1,0:T(8,128)(2,1)} %add_convert_fusion.1), channel_id=1, source_target_pairs={{0,8},{8,0},{16,24},{24,16},{1,9},{9,1},{17,25},{25,17},{2,10},{10... | collective-permute-start | bytes 3993608 | tf_op jit(solution)/shard_map/ppermute | solution.py:791
  325.8 29.7 %collective-permute-start.4 = (bf16[208,3200]{1,0:T(8,128)(2,1)S(1)}, bf16[208,3200]{1,0:T(8,128)(2,1)}, u32[]{:S(2)}, u32[]{:S(2)}) collective-permute-start(bf16[208,3200]{1,0:T(8,128)(2,1)S(1)} %add_convert_fusion), channel_id=1, source_target_pairs={{0,16},{8,24},{16,0},{24,8},{1,17},{9,25},{17,1},{25,9},{2,18},{10... | collective-permute-start | bytes 3993608 | tf_op jit(solution)/shard_map/ppermute | solution.py:791
  327.8 27.7 %copy-start.10 = (bf16[416,3200]{1,0:T(8,128)(2,1)S(1)}, bf16[416,3200]{1,0:T(8,128)(2,1)}, u32[]{:S(2)}) copy-start(bf16[416,3200]{1,0:T(8,128)(2,1)} %get-tuple-element.97) | copy-start | bytes 7987204
  353.9 1.1 copy-start.14
  355.0 3.1 copy-start.12
  360.2 1.5 copy-start.5
  362.7 25.9 %collective-permute-start.5 = (bf16[104,3200]{1,0:T(8,128)(2,1)}, bf16[104,3200]{1,0:T(8,128)(2,1)}, u32[]{:S(2)}, u32[]{:S(2)}) collective-permute-start(bf16[104,3200]{1,0:T(8,128)(2,1)} %get-tuple-element.148), channel_id=1, source_target_pairs={{0,8},{8,0},{16,24},{24,16},{1,9},{9,1},{17,25},{25,17},{2,10},{10... | collective-permute-start | bytes 1996808 | tf_op jit(solution)/shard_map/ppermute | solution.py:791
  364.2 24.4 %collective-permute-start.3 = (bf16[104,3200]{1,0:T(8,128)(2,1)S(1)}, bf16[104,3200]{1,0:T(8,128)(2,1)}, u32[]{:S(2)}, u32[]{:S(2)}) collective-permute-start(bf16[104,3200]{1,0:T(8,128)(2,1)S(1)} %get-tuple-element.149), channel_id=1, source_target_pairs={{0,16},{8,24},{16,0},{24,8},{1,17},{9,25},{17,1},{25,9},{2,18},{10... | collective-permute-start | bytes 1996808 | tf_op jit(solution)/shard_map/ppermute | solution.py:791
  364.9 184.1 %all-to-all-start.5 = ((bf16[8,104,2176]{2,1,0:T(8,128)(2,1)}), bf16[8,104,2176]{2,1,0:T(8,128)(2,1)}, u32[]{:S(2)}, u32[]{:S(2)}) async-start(bf16[8,104,2176]{2,1,0:T(8,128)(2,1)} %bitcast.70), calls=%async_computation.5 | async-start | bytes 7241728 | tf_op jit(solution)/shard_map/all_to_all | solution.py:762
  369.7 125.7 %all-reduce.9.cloned.1.call-start = ((), (), s32[]{:S(2)}) async-start(), calls=%async_computation.6 | async-start | bytes 2662400 | tf_op jit(solution)/shard_map/psum | solution.py:938
  369.9 18.7 %copy-start.6 = (f32[208,3200]{1,0:T(8,128)S(1)}, f32[208,3200]{1,0:T(8,128)}, u32[]{:S(2)}) copy-start(f32[208,3200]{1,0:T(8,128)} %copy-done.5) | copy-start | bytes 7987204
  415.9 79.9 %copy-start.3 = (f32[49,104,128]{2,1,0:T(8,128)S(1)}, f32[49,104,128]{2,1,0:T(8,128)}, u32[]{:S(2)}) copy-start(f32[49,104,128]{2,1,0:T(8,128)} %get-tuple-element.118) | copy-start | bytes 7827460
  495.4 35.1 %collective-permute-start.10 = (bf16[104,3200]{1,0:T(8,128)(2,1)}, bf16[104,3200]{1,0:T(8,128)(2,1)}, u32[]{:S(2)}, u32[]{:S(2)}) collective-permute-start(bf16[104,3200]{1,0:T(8,128)(2,1)} %get-tuple-element.119), channel_id=1, source_target_pairs={{0,8},{8,0},{16,24},{24,16},{1,9},{9,1},{17,25},{25,17},{2,10},{10... | collective-permute-start | bytes 1996808 | tf_op jit(solution)/shard_map/ppermute | solution.py:791
  496.8 16.6 %collective-permute-start.7 = (f32[49,100]{1,0:T(8,128)S(1)}, f32[49,100]{1,0:T(8,128)S(1)}, u32[]{:S(2)}, u32[]{:S(2)}) collective-permute-start(f32[49,100]{1,0:T(8,128)S(1)} %bitcast.82), channel_id=1, source_target_pairs={{0,8},{8,0},{16,24},{24,16},{1,9},{9,1},{17,25},{25,17},{2,10},{10... | collective-permute-start | bytes 58808 | tf_op jit(solution)/shard_map/ppermute | solution.py:773
  498.4 15.0 %collective-permute-start.8 = (f32[49,100]{1,0:T(8,128)S(1)}, f32[49,100]{1,0:T(8,128)S(1)}, u32[]{:S(2)}, u32[]{:S(2)}) collective-permute-start(f32[49,100]{1,0:T(8,128)S(1)} %bitcast.83), channel_id=1, source_target_pairs={{0,16},{8,24},{16,0},{24,8},{1,17},{9,25},{17,1},{25,9},{2,18},{10... | collective-permute-start | bytes 58808 | tf_op jit(solution)/shard_map/ppermute | solution.py:773
  499.6 14.8 %collective-permute-start.9 = (f32[49,100]{1,0:T(8,128)S(1)}, f32[49,100]{1,0:T(8,128)S(1)}, u32[]{:S(2)}, u32[]{:S(2)}) collective-permute-start(f32[49,100]{1,0:T(8,128)S(1)} %bitcast.84), channel_id=1, source_target_pairs={{0,24},{8,16},{16,8},{24,0},{1,25},{9,17},{17,9},{25,1},{2,26},{10... | collective-permute-start | bytes 58808 | tf_op jit(solution)/shard_map/ppermute | solution.py:773
  514.4 17.9 %collective-permute-start.6 = (bf16[104,3200]{1,0:T(8,128)(2,1)}, bf16[104,3200]{1,0:T(8,128)(2,1)S(1)}, u32[]{:S(2)}, u32[]{:S(2)}) collective-permute-start(bf16[104,3200]{1,0:T(8,128)(2,1)} %get-tuple-element.117), channel_id=1, source_target_pairs={{0,16},{8,24},{16,0},{24,8},{1,17},{9,25},{17,1},{25,9},{2,18},{10... | collective-permute-start | bytes 1996808 | tf_op jit(solution)/shard_map/ppermute | solution.py:791
  532.0 2.3 copy-start.7
  532.0 8.5 %collective-permute-start.13 = (bf16[208,3200]{1,0:T(8,128)(2,1)S(1)}, bf16[208,3200]{1,0:T(8,128)(2,1)}, u32[]{:S(2)}, u32[]{:S(2)}) collective-permute-start(bf16[208,3200]{1,0:T(8,128)(2,1)S(1)} %pad_maximum_fusion.1.refs_0_), channel_id=1, source_target_pairs={{0,1},{1,0},{2,3},{3,2},{4,5},{5,4},{6,7},{7,6},{8,9},{9,8},{10,11... | collective-permute-start | bytes 3993608 | tf_op jit(solution)/shard_map/ppermute | solution.py:778
  533.8 6.7 %copy-start.8 = (bf16[208,3200]{1,0:T(8,128)(2,1)}, bf16[208,3200]{1,0:T(8,128)(2,1)S(1)}, u32[]{:S(2)}) copy-start(bf16[208,3200]{1,0:T(8,128)(2,1)S(1)} %pad_maximum_fusion.refs_0_) | copy-start | bytes 3993604
  533.8 10.9 %collective-permute-start.12 = (bf16[208,3200]{1,0:T(8,128)(2,1)S(1)}, bf16[208,3200]{1,0:T(8,128)(2,1)}, u32[]{:S(2)}, u32[]{:S(2)}) collective-permute-start(bf16[208,3200]{1,0:T(8,128)(2,1)S(1)} %pad_maximum_fusion.refs_0_), channel_id=1, source_target_pairs={{0,1},{1,0},{2,3},{3,2},{4,5},{5,4},{6,7},{7,6},{8,9},{9,8},{10,11... | collective-permute-start | bytes 3993608 | tf_op jit(solution)/shard_map/ppermute | solution.py:778
  534.2 31.4 %collective-permute-start.11 = (bf16[208,3200]{1,0:T(8,128)(2,1)S(1)}, bf16[208,3200]{1,0:T(8,128)(2,1)}, u32[]{:S(2)}, u32[]{:S(2)}) collective-permute-start(bf16[208,3200]{1,0:T(8,128)(2,1)S(1)} %pad_maximum_fusion.1.refs_0_), channel_id=1, source_target_pairs={{0,16},{8,24},{16,0},{24,8},{1,17},{9,25},{17,1},{25,9},{2,18},{10... | collective-permute-start | bytes 3993608 | tf_op jit(solution)/shard_map/ppermute | solution.py:791
  535.5 31.1 %collective-permute-start.15 = (bf16[208,3200]{1,0:T(8,128)(2,1)S(1)}, bf16[208,3200]{1,0:T(8,128)(2,1)}, u32[]{:S(2)}, u32[]{:S(2)}) collective-permute-start(bf16[208,3200]{1,0:T(8,128)(2,1)S(1)} %pad_maximum_fusion.refs_0_), channel_id=1, source_target_pairs={{0,8},{8,0},{16,24},{24,16},{1,9},{9,1},{17,25},{25,17},{2,10},{10... | collective-permute-start | bytes 3993608 | tf_op jit(solution)/shard_map/ppermute | solution.py:791
  566.6 8.3 %collective-permute-start.16 = (bf16[208,3200]{1,0:T(8,128)(2,1)}, bf16[208,3200]{1,0:T(8,128)(2,1)S(1)}, u32[]{:S(2)}, u32[]{:S(2)}) collective-permute-start(bf16[208,3200]{1,0:T(8,128)(2,1)} %collective-permute-done.15.refs_0_), channel_id=1, source_target_pairs={{0,1},{1,0},{2,3},{3,2},{4,5},{5,4},{6,7},{7,6},{8,9},{9,8},{10,11... | collective-permute-start | bytes 3993608 | tf_op jit(solution)/shard_map/ppermute | solution.py:778
  566.6 13.6 %collective-permute-start.14 = (bf16[208,3200]{1,0:T(8,128)(2,1)}, bf16[208,3200]{1,0:T(8,128)(2,1)S(1)}, u32[]{:S(2)}, u32[]{:S(2)}) collective-permute-start(bf16[208,3200]{1,0:T(8,128)(2,1)} %collective-permute-done.11.refs_0_), channel_id=1, source_target_pairs={{0,1},{1,0},{2,3},{3,2},{4,5},{5,4},{6,7},{7,6},{8,9},{9,8},{10,11... | collective-permute-start | bytes 3993608 | tf_op jit(solution)/shard_map/ppermute | solution.py:778
  574.9 1.1 copy-start.15
  580.2 1.1 copy-start.13
  581.3 5.8 copy-start.1
Sparse Core Ops, SparseCore 0:
  393.0 102.3 all-reduce.8

commit v4 on v3

--- a/solution.py
+++ b/solution.py
@@ -249,7 +249,7 @@
             carry = put(h0 + r, sums[r], carry)
         return carry
 
-    return lax.fori_loop(0, z.height // steps, body, carry, unroll=2)
+    return lax.fori_loop(0, z.height // steps, body, carry, unroll=3)
 
 
 def conv_forward(z, taps, x):
@@ -409,7 +409,7 @@
                         return tuple(totals)
 
                     zero = jnp.zeros((SUBL, LANES), F32)
-                    totals = lax.fori_loop(0, z.height // steps, body, (zero,) * z.side, unroll=4)
+                    totals = lax.fori_loop(0, z.height // steps, body, (zero,) * z.side, unroll=6)
                     for a in range(z.side):
                         product_ref[z.side * a + b, at, :] = totals[a]
 
@@ -932,14 +932,14 @@
     shares = sum_out.share(made[1]), sum_in.share(made[1])
     if len(cuts) > 3:
         made = conv_gradient(
-            z, cuts[2], cuts[3], after(terms, *shares), norm_parts, conv, x, ntaps, made
+            z, cuts[2], cuts[3], after(terms, *shares, branch), norm_parts, conv, x, ntaps, made
         )
     conv_grad, products = made
-    shares = lax.psum(shares, "pair")
+    shares = lax.psum((after(shares[0], branch), after(shares[1], branch)), "pair")
     g_kernel = dp_sum(jnp.sum(products, axis=2)[:, :chan])
     x_grad = conv_backward(z, taps, conv_grad, cot, land3)
-    sum_out.back_first(after(shares[0], x_grad))
-    sum_in.back_first(after(shares[1], x_grad))
+    sum_out.back_first(after(shares[0], x_grad, g_kernel))
+    sum_in.back_first(after(shares[1], x_grad, g_kernel))
     rows = jnp.concatenate([after(g_kernel, sum_out.own, sum_in.own), small], axis=0)
     gathered = lax.all_gather(rows, CHAN)
     placed = jnp.transpose(gathered, (1, 0, 2)).reshape(rows.shape[0], width)

time: 601 us -> 561 us (0.933)
  waiting for transfers between devices: 129 us -> 97.7 us
  Pallas kernels: 308 us -> 301 us
    psum x1, waiting for transfers between devices: 45.5 us -> 0.53 us  [per_device(): lax.psum((after(shares[0], branch), after(shares[1], branch)), 'pair')]
    all_to_all x6, waiting for transfers between devices: 54.1 us -> 82.9 us  [exchange(): return lax.all_to_all(value, CHAN, split_axis=0, concat_axis=0, tiled=True)]
    ppermute x3, waiting for transfers between devices: 14.1 us -> 0.01 us  [dp_sum(): lax.ppermute(value, 'dp', [(i, i ^ turn) for i in range(ways)])]
    unnamed x40 -> x44, local copies, waits for them, and re-layouts: 14.3 us -> 15.6 us
  transfers between devices with their start and end apart: 24 -> 24, of which waited for: 10 -> 9; matrix products, arithmetic and copies ran while one was open for 8% -> 9% of each run, Pallas kernels for 50% -> 53%
where the time goes in v4:
time: 561 us; the launch traced here: 554 us
  Pallas kernels  301 us (54%)
  waiting for transfers between devices  97.7 us (17%)
  starting transfers between devices  41.7 us (7%)
  local copies, waits for them, and re-layouts  37.8 us (7%)
  blocking collectives  35.1 us (6%)
  other arithmetic  25.5 us (5%)
  between operations  15.3 us (3%)
    all_to_all x6, waiting for transfers between devices, exchange(): return lax.all_to_all(value, CHAN, split_axis=0, concat_axis=0, tiled=True)  82.9 us
    pallas_call x2, Pallas kernels, mlp(): pl.pallas_call(kernel, grid=(blocks + outs,), in_specs=in_specs, out_spec...  81.1 us
    pallas_call x3, Pallas kernels, conv_gradient(): pl.pallas_call(kernel, grid=(end - begin,), in_specs=[group((5, GROUP, LA...  54.8 us
    pallas_call x2, Pallas kernels, weight_grad(): pl.pallas_call(kernel, grid=(hidden // block,), in_specs=[smem()] + [whol...  40.4 us
    pallas_call x1, Pallas kernels, conv_forward(): pl.pallas_call(kernel, grid=(pl.cdiv(z.chan, GROUP),), in_specs=[group_la...  35.2 us
    pallas_call x1, Pallas kernels, conv_backward(): pl.pallas_call(kernel, grid=(pl.cdiv(z.chan, GROUP),), in_specs=[group_la...  33 us
    all_to_all x6, starting transfers between devices, exchange(): return lax.all_to_all(value, CHAN, split_axis=0, concat_axis=0, tiled=True)  29.3 us
    pallas_call x4, Pallas kernels, unpad_rows(): pl.pallas_call(kernel, grid_spec=pltpu.PrefetchScalarGridSpec(num_scalar_...  17 us
  transfers between devices with their start and end apart: 24, of which 9 were waited for; matrix products, arithmetic and copies ran while one was open for 9% of the time, Pallas kernels for 53%

profile of v4, /device:TPU:0, one launch (start us, length us, event | category | flops | bytes accessed | tf_op | source)
XLA Modules:
  0.0 554.2 jit_solution(9233427482587998820)
XLA Ops:
  7.2 1.6 broadcast_in_dim_squeeze.2.land_ref
  8.8 4.7 copy.63
  13.5 5.0 shard_map.195
  18.5 6.3 %all-to-all-start = ((bf16[8,104,2176]{2,1,0:T(8,128)(2,1)}), bf16[8,104,2176]{2,1,0:T(8,128)(2,1)}, u32[]{:S(2)}, u32[]{:S(2)}) async-start(bf16[8,104,2176]{2,1,0:T(8,128)(2,1)} %bitcast.74), calls=%async_computation | async-start | bytes 7241728 | tf_op jit(solution)/shard_map/all_to_all | solution.py:762
  24.8 4.7 copy.64
  29.7 2.0 broadcast_in_dim.27.taps_ref
  31.6 35.2 %shard_map.196 = (f32[48,104,384]{2,1,0:T(8,128)}, f32[104,128]{1,0:T(8,128)}, f32[104,128]{1,0:T(8,128)}) custom-call(f32[49,104,128]{2,1,0:T(8,128)} %broadcast_in_dim.27.taps_ref, bf16[48,100,360]{2,1,0:T(8,128)(2,1)} %bitcast.59), custom_call_target="tpu_custom_call" | custom-call | flops 1000 | bytes 1000 | tf_op jit(solution)/shard_map/pallas_call | solution.py:277
  69.3 9.9 %all-reduce.5 = (f32[100]{0:T(128)S(1)}, f32[100]{0:T(128)S(1)}) all-reduce(f32[100]{0:T(128)S(1)} %bitcast.87, f32[100]{0:T(128)S(1)} %bitcast.88), channel_id=1, replica_groups=mesh['dp'=4,'pair'=4,'core'=2] {'dp'}, use_global_device_ids=true, to_apply=%region_3.4 | all-reduce | flops 200 | bytes 1600 | tf_op jit(solution)/shard_map/psum | solution.py:878
  82.3 6.0 %shard_map.197 = (bf16[832,1152]{1,0:T(8,128)(2,1)}, bf16[832,1024]{1,0:T(8,128)(2,1)}) custom-call(f32[3,104,128]{2,1,0:T(8,128)} %broadcast_in_dim.28.columns_ref, f32[48,104,384]{2,1,0:T(8,128)} %get-tuple-element.76.conv_ref), custom_call_target="tpu_custom_call" | custom-call | flops 1000 | bytes 1000 | tf_op jit(solution)/shard_map/pallas_call | solution.py:311
  88.3 18.4 %all-to-all-done = bf16[8,104,2176]{2,1,0:T(8,128)(2,1)} async-done(((bf16[8,104,2176]{2,1,0:T(8,128)(2,1)}), bf16[8,104,2176]{2,1,0:T(8,128)(2,1)}, u32[]{:S(2)}, u32[]{:S(2)}) %all-to-all-start) | async-done | bytes 3620896 | tf_op jit(solution)/shard_map/all_to_all | solution.py:762
  106.7 3.6 all-to-all-start.1
  110.3 8.0 %shard_map.198 = (bf16[832,3200]{1,0:T(8,128)(2,1)}, bf16[3200,832]{1,0:T(8,128)(2,1)}) custom-call(bf16[800,3200]{1,0:T(8,128)(2,1)} %in_ref), custom_call_target="tpu_custom_call" | custom-call | flops 1000 | bytes 1000 | tf_op jit(solution)/shard_map/pallas_call | solution.py:549
  118.2 7.9 %shard_map.199 = (bf16[832,3200]{1,0:T(8,128)(2,1)}, bf16[3200,832]{1,0:T(8,128)(2,1)}) custom-call(bf16[800,3200]{1,0:T(8,128)(2,1)} %bitcast.71), custom_call_target="tpu_custom_call" | custom-call | flops 1000 | bytes 1000 | tf_op jit(solution)/shard_map/pallas_call | solution.py:549
  126.1 29.3 %all-to-all-done.1 = bf16[8,104,1152]{2,1,0:T(8,128)(2,1)S(1)} async-done(((bf16[8,104,1152]{2,1,0:T(8,128)(2,1)}), bf16[8,104,1152]{2,1,0:T(8,128)(2,1)S(1)}, u32[]{:S(2)}, u32[]{:S(2)}) %all-to-all-start.1) | async-done | bytes 1916960 | tf_op jit(solution)/shard_map/all_to_all | solution.py:762
  155.4 4.5 all-to-all-start.2
  159.9 1.7 broadcast_in_dim.70.b_in_ref
  162.7 43.3 %shard_map.200 = (bf16[832,2176]{1,0:T(8,128)(2,1)}, bf16[832,1152]{1,0:T(8,128)(2,1)}, bf16[3200,1152]{1,0:T(8,128)(2,1)}, bf16[3200,1152]{1,0:T(8,128)(2,1)}) custom-call(bf16[832,1152]{1,0:T(8,128)(2,1)} %bitcast.68, bf16[832,2176]{1,0:T(8,128)(2,1)} %bitcast.6.g_ref.refs_0_, bf16[3200,832]{1,0:T(8,128)(2,1)} %get-tuple-element.80.w_in_t_ref, ...), custom_call_target="tpu_custom_call" | custom-call | flops 1000 | bytes 1000 | tf_op jit(solution)/shard_map/pallas_call | solution.py:665
  206.0 5.6 %all-to-all-start.3 = ((bf16[8,104,1152]{2,1,0:T(8,128)(2,1)}), bf16[8,104,1152]{2,1,0:T(8,128)(2,1)S(1)}, u32[]{:S(2)}, u32[]{:S(2)}) async-start(bf16[8,104,1152]{2,1,0:T(8,128)(2,1)} %bitcast.75), calls=%async_computation.3 | async-start | bytes 3833856 | tf_op jit(solution)/shard_map/all_to_all | solution.py:762
  211.6 37.8 %shard_map.201 = (bf16[832,2176]{1,0:T(8,128)(2,1)}, bf16[832,1024]{1,0:T(8,128)(2,1)}, bf16[3200,1024]{1,0:T(8,128)(2,1)}, bf16[3200,1024]{1,0:T(8,128)(2,1)}) custom-call(bf16[832,1024]{1,0:T(8,128)(2,1)} %bitcast.16.n_ref.refs_1_, bf16[832,2176]{1,0:T(8,128)(2,1)} %bitcast.6.g_ref.refs_0_, ...), custom_call_target="tpu_custom_call", output_to_operand_aliasing={{0}: (8, {})} | custom-call | flops 1000 | bytes 1000 | tf_op jit(solution)/shard_map/pallas_call | solution.py:665
  249.4 7.4 %all-to-all-done.3.rest_0_ = bf16[8,104,1152]{2,1,0:T(8,128)(2,1)S(1)} async-done(((bf16[8,104,1152]{2,1,0:T(8,128)(2,1)}), bf16[8,104,1152]{2,1,0:T(8,128)(2,1)S(1)}, u32[]{:S(2)}, u32[]{:S(2)}) %all-to-all-start.3) | async-done | bytes 1916960 | tf_op jit(solution)/shard_map/all_to_all | solution.py:762
  256.8 4.3 all-to-all-start.4
  261.1 20.4 %shard_map.202 = (bf16[416,3200]{1,0:T(8,128)(2,1)}, bf16[416,3200]{1,0:T(8,128)(2,1)}) custom-call(s32[1]{0:T(128)} %bitcast.2.core_ref, bf16[832,2176]{1,0:T(8,128)(2,1)} %bitcast.6.g_ref.refs_0_, bf16[3200,1152]{1,0:T(8,128)(2,1)} %get-tuple-element.85.refs_1_, bf16[3200,1024]{1,0:T(8,128)(2,1)} %get-tuple-element.92.refs_2_), custom_call_target="tpu_custom_call" | custom-call | flops 1000 | bytes 1000 | tf_op jit(solution)/shard_map/pallas_call | solution.py:714
  281.9 20.0 %shard_map.204 = (bf16[416,3200]{1,0:T(8,128)(2,1)}, bf16[416,3200]{1,0:T(8,128)(2,1)}) custom-call(s32[1]{0:T(128)} %bitcast.2.core_ref, bf16[832,1152]{1,0:T(8,128)(2,1)} %bitcast.69, bf16[832,1024]{1,0:T(8,128)(2,1)} %bitcast.16.n_ref.refs_1_, bf16[3200,1152]{1,0:T(8,128)(2,1)} %get-tuple-element.101.refs_2_, bf16[3200,1024]{1,0:T(8,128)(2,1)} %get-tuple-element.103.refs_3_), custom_call_target="tpu_custom_call" | custom-call | flops 1000 | bytes 1000 | tf_op jit(solution)/shard_map/pallas_call | solution.py:714
  302.9 6.3 %shard_map.203 = (f32[104,128]{1,0:T(8,128)}, f32[104,128]{1,0:T(8,128)}) custom-call(f32[2,104,128]{2,1,0:T(8,128)} %broadcast_in_dim.30.columns_ref, f32[48,104,384]{2,1,0:T(8,128)} %get-tuple-element.76.conv_ref, bf16[832,1152]{1,0:T(8,128)(2,1)} %bitcast.64, bf16[832,1024]{1,0:T(8,128)(2,1)} %bitcast.21.rest_1_), custom_call_target="tpu_custom_call" | custom-call | flops 1000 | bytes 1000 | tf_op jit(solution)/shard_map/pallas_call | solution.py:348
  311.2 9.9 %psum.37 = f32[5,100]{1,0:T(8,128)S(1)} all-reduce(f32[5,100]{1,0:T(8,128)S(1)} %pad_maximum_fusion.2), channel_id=1, replica_groups=mesh['dp'=4,'pair'=4,'core'=2] {'dp'}, use_global_device_ids=true, to_apply=%region_8.9 | all-reduce | flops 500 | bytes 4000 | tf_op jit(solution)/shard_map/psum | solution.py:915
  321.1 2.9 add_convert_fusion.1
  324.0 1.6 add_convert_fusion
  325.7 1.2 collective-permute-start.4
  326.8 5.0 all-to-all-start.5
  332.8 17.0 %shard_map.205 = (bf16[48,104,384]{2,1,0:T(8,128)(2,1)}, f32[49,104,128]{2,1,0:T(8,128)}) custom-call(f32[5,104,128]{2,1,0:T(8,128)} %broadcast_in_dim.65.columns_ref, f32[48,104,384]{2,1,0:T(8,128)} %get-tuple-element.76.conv_ref, bf16[48,100,360]{2,1,0:T(8,128)(2,1)} %bitcast.60, bf16[8,104,1152]{2,1,0:T(8,128)(2,1)} %copy-done.2, ...), custom_call_target="tpu_custom_call" | custom-call | flops 1000 | bytes 1000 | tf_op jit(solution)/shard_map/pallas_call | solution.py:420
  349.8 3.9 collective-permute-done.1
  353.7 1.1 copy-done.15
  355.3 2.5 convert_add_fusion.1
  357.8 2.3 convert_add_fusion
  360.1 1.5 copy-done.6
  361.6 1.1 dynamic-slice_convert_fusion
  362.7 1.4 collective-permute-start.5
  364.7 16.9 %shard_map.206 = (bf16[48,104,384]{2,1,0:T(8,128)(2,1)}, f32[49,104,128]{2,1,0:T(8,128)}) custom-call(f32[5,104,128]{2,1,0:T(8,128)} %broadcast_in_dim.65.columns_ref, f32[48,104,384]{2,1,0:T(8,128)} %get-tuple-element.76.conv_ref, bf16[48,100,360]{2,1,0:T(8,128)(2,1)} %bitcast.61, ...), custom_call_target="tpu_custom_call", output_to_operand_aliasing={{0}: (5, {}), {1}: (6, {})} | custom-call | flops 1000 | bytes 1000 | tf_op jit(solution)/shard_map/pallas_call | solution.py:420
  381.6 2.1 add_convert_fusion.2
  383.7 2.1 add_convert_fusion.3
  385.8 27.9 %all-to-all-done.5 = bf16[8,104,2176]{2,1,0:T(8,128)(2,1)} async-done(((bf16[8,104,2176]{2,1,0:T(8,128)(2,1)}), bf16[8,104,2176]{2,1,0:T(8,128)(2,1)}, u32[]{:S(2)}, u32[]{:S(2)}) %all-to-all-start.5) | async-done | bytes 3620896 | tf_op jit(solution)/shard_map/all_to_all | solution.py:762
  413.7 20.9 %shard_map.207 = (bf16[48,104,384]{2,1,0:T(8,128)(2,1)}, f32[49,104,128]{2,1,0:T(8,128)}) custom-call(f32[5,104,128]{2,1,0:T(8,128)} %broadcast_in_dim.65.columns_ref, f32[48,104,384]{2,1,0:T(8,128)} %get-tuple-element.76.conv_ref, bf16[48,100,360]{2,1,0:T(8,128)(2,1)} %bitcast.62, ...), custom_call_target="tpu_custom_call", output_to_operand_aliasing={{0}: (5, {}), {1}: (6, {})} | custom-call | flops 1000 | bytes 1000 | tf_op jit(solution)/shard_map/pallas_call | solution.py:420
  434.6 2.7 reduce_sum.69
  437.3 1.6 collective-permute-start.6
  438.8 1.4 collective-permute-start.7
  440.8 33.0 %shard_map.208 = bf16[48,100,360]{2,1,0:T(8,128)(2,1)} custom-call(f32[49,104,128]{2,1,0:T(8,128)} %broadcast_in_dim.27.taps_ref, bf16[48,104,384]{2,1,0:T(8,128)(2,1)} %get-tuple-element.121.grad_ref, bf16[48,100,360]{2,1,0:T(8,128)(2,1)} %bitcast.67, s32[48,1,360]{2,1,0:T(1,128)} %broadcast_in_dim_squeeze.2.land_ref), custom_call_target="tpu_custom_call" | custom-call | flops 1000 | bytes 1000 | tf_op jit(solution)/shard_map/pallas_call | solution.py:475
  474.4 1.1 collective-permute-start.10
  475.4 1.4 collective-permute-start.9
  476.9 15.3 %all-gather.1 = f32[8,54,100]{2,1,0:T(8,128)} all-gather(f32[1,54,100]{2,1,0:T(8,128)S(1)} %maximum_bitcast_fusion), channel_id=2, replica_groups=mesh['dp'=4,'pair'=4,'core'=2] {'pair','core'}, dimensions={0}, use_global_device_ids=true | all-gather | bytes 194400 | tf_op jit(solution)/shard_map/all_gather | solution.py:944
  492.2 1.3 broadcast_select_fusion.1
  496.2 6.3 %shard_map.209 = bf16[48,100,360]{2,1,0:T(8,128)(2,1)} custom-call(bf16[48,100,360]{2,1,0:T(8,128)(2,1)} %bitcast.63, s32[48,1,360]{2,1,0:T(1,128)} %broadcast_in_dim_squeeze.2.land_ref, bf16[832,2176]{1,0:T(8,128)(2,1)} %bitcast.26.branch_ref), custom_call_target="tpu_custom_call" | custom-call | flops 1000 | bytes 1000 | tf_op jit(solution)/shard_map/pallas_call | solution.py:504
  502.5 2.4 copy.65
  504.8 1.1 copy-done.5
  505.9 2.3 copy.66
  508.2 4.3 shard_map.211.refs_2_
  512.5 4.3 shard_map.210.refs_2_
  516.7 9.6 %collective-permute-done.11.refs_0_ = bf16[208,3200]{1,0:T(8,128)(2,1)} collective-permute-done((bf16[208,3200]{1,0:T(8,128)(2,1)S(1)}, bf16[208,3200]{1,0:T(8,128)(2,1)}, u32[]{:S(2)}, u32[]{:S(2)}) %collective-permute-start.11) | collective-permute-done | bytes 1331232 | tf_op jit(solution)/shard_map/ppermute | solution.py:791
  527.9 1.7 copy.57
  529.5 1.7 slice.69
  534.8 1.1 copy-done.16
  535.9 4.2 shard_map.213
  540.2 1.1 copy-done.14
  541.3 4.3 shard_map.212
  545.6 1.5 fusion.1
  (107 shorter events, 20.4 us)
Async XLA Ops:
  7.2 22.4 %copy-start = (bf16[49,800]{1,0:T(8,128)(2,1)S(1)}, bf16[49,800]{1,0:T(8,128)(2,1)}, u32[]{:S(2)}) copy-start(bf16[49,800]{1,0:T(8,128)(2,1)} %param.16) | copy-start | bytes 235204
  18.5 88.2 %all-to-all-start = ((bf16[8,104,2176]{2,1,0:T(8,128)(2,1)}), bf16[8,104,2176]{2,1,0:T(8,128)(2,1)}, u32[]{:S(2)}, u32[]{:S(2)}) async-start(bf16[8,104,2176]{2,1,0:T(8,128)(2,1)} %bitcast.74), calls=%async_computation | async-start | bytes 7241728 | tf_op jit(solution)/shard_map/all_to_all | solution.py:762
  106.7 48.7 %all-to-all-start.1 = ((bf16[8,104,1152]{2,1,0:T(8,128)(2,1)}), bf16[8,104,1152]{2,1,0:T(8,128)(2,1)S(1)}, u32[]{:S(2)}, u32[]{:S(2)}) async-start(bf16[8,104,1152]{2,1,0:T(8,128)(2,1)} %bitcast.76), calls=%async_computation.1 | async-start | bytes 3833856 | tf_op jit(solution)/shard_map/all_to_all | solution.py:762
  126.1 33.8 %copy-start.19 = (f32[3200]{0:T(1024)S(1)}, f32[3200]{0:T(1024)}, u32[]{:S(2)}) copy-start(f32[3200]{0:T(1024)} %param.21) | copy-start | bytes 38404
  126.1 35.5 %copy-start.20 = (f32[800]{0:T(1024)S(1)}, f32[800]{0:T(1024)}, u32[]{:S(2)}) copy-start(f32[800]{0:T(1024)} %param.23) | copy-start | bytes 9604
  155.4 7.3 %copy-start.3 = (bf16[8,104,1152]{2,1,0:T(8,128)(2,1)}, bf16[8,104,1152]{2,1,0:T(8,128)(2,1)S(1)}, u32[]{:S(2)}) copy-start(bf16[8,104,1152]{2,1,0:T(8,128)(2,1)S(1)} %all-to-all-done.1) | copy-start | bytes 5750788
  155.4 50.6 %all-to-all-start.2 = ((bf16[8,104,1024]{2,1,0:T(8,128)(2,1)}), bf16[8,104,1024]{2,1,0:T(8,128)(2,1)}, u32[]{:S(2)}, u32[]{:S(2)}) async-start(bf16[8,104,1024]{2,1,0:T(8,128)(2,1)} %bitcast.78), calls=%async_computation.2 | async-start | bytes 3407872 | tf_op jit(solution)/shard_map/all_to_all | solution.py:762
  206.0 50.7 %all-to-all-start.3 = ((bf16[8,104,1152]{2,1,0:T(8,128)(2,1)}), bf16[8,104,1152]{2,1,0:T(8,128)(2,1)S(1)}, u32[]{:S(2)}, u32[]{:S(2)}) async-start(bf16[8,104,1152]{2,1,0:T(8,128)(2,1)} %bitcast.75), calls=%async_computation.3 | async-start | bytes 3833856 | tf_op jit(solution)/shard_map/all_to_all | solution.py:762
  256.8 24.7 %copy-start.2 = (bf16[8,104,1152]{2,1,0:T(8,128)(2,1)}, bf16[8,104,1152]{2,1,0:T(8,128)(2,1)S(1)}, u32[]{:S(2)}) copy-start(bf16[8,104,1152]{2,1,0:T(8,128)(2,1)S(1)} %all-to-all-done.3.rest_0_) | copy-start | bytes 5750788
  256.8 45.4 %all-to-all-start.4 = ((bf16[8,104,1024]{2,1,0:T(8,128)(2,1)}), bf16[8,104,1024]{2,1,0:T(8,128)(2,1)}, u32[]{:S(2)}, u32[]{:S(2)}) async-start(bf16[8,104,1024]{2,1,0:T(8,128)(2,1)} %bitcast.77), calls=%async_computation.4 | async-start | bytes 3407872 | tf_op jit(solution)/shard_map/all_to_all | solution.py:762
  281.5 39.6 %collective-permute-start = (bf16[416,3200]{1,0:T(8,128)(2,1)}, bf16[416,3200]{1,0:T(8,128)(2,1)}, u32[]{:S(2)}, u32[]{:S(2)}) collective-permute-start(bf16[416,3200]{1,0:T(8,128)(2,1)} %get-tuple-element.100), channel_id=1, source_target_pairs={{0,1},{1,0},{2,3},{3,2},{4,5},{5,4},{6,7},{7,6},{8,9},{9,8},{10,11... | collective-permute-start | bytes 7987208 | tf_op jit(solution)/shard_map/ppermute | solution.py:778
  281.9 20.1 %copy-start.18 = (f32[104,128]{1,0:T(8,128)S(1)}, f32[104,128]{1,0:T(8,128)}, u32[]{:S(2)}) copy-start(f32[104,128]{1,0:T(8,128)} %get-tuple-element.98) | copy-start | bytes 159748
  301.9 22.1 %collective-permute-start.2 = (bf16[416,3200]{1,0:T(8,128)(2,1)}, bf16[416,3200]{1,0:T(8,128)(2,1)}, u32[]{:S(2)}, u32[]{:S(2)}) collective-permute-start(bf16[416,3200]{1,0:T(8,128)(2,1)} %get-tuple-element.106), channel_id=1, source_target_pairs={{0,1},{1,0},{2,3},{3,2},{4,5},{5,4},{6,7},{7,6},{8,9},{9,8},{10,11... | collective-permute-start | bytes 7987208 | tf_op jit(solution)/shard_map/ppermute | solution.py:778
  302.9 18.2 %copy-start.10 = (bf16[416,3200]{1,0:T(8,128)(2,1)S(1)}, bf16[416,3200]{1,0:T(8,128)(2,1)}, u32[]{:S(2)}) copy-start(bf16[416,3200]{1,0:T(8,128)(2,1)} %get-tuple-element.99) | copy-start | bytes 7987204
  321.1 2.9 copy-start.12
  324.0 29.7 %collective-permute-start.1 = (bf16[208,3200]{1,0:T(8,128)(2,1)}, bf16[208,3200]{1,0:T(8,128)(2,1)S(1)}, u32[]{:S(2)}, u32[]{:S(2)}) collective-permute-start(bf16[208,3200]{1,0:T(8,128)(2,1)} %add_convert_fusion.1), channel_id=1, source_target_pairs={{0,8},{8,0},{16,24},{24,16},{1,9},{9,1},{17,25},{25,17},{2,10},{10... | collective-permute-start | bytes 3993608 | tf_op jit(solution)/shard_map/ppermute | solution.py:791
  325.7 29.6 %collective-permute-start.4 = (bf16[208,3200]{1,0:T(8,128)(2,1)S(1)}, bf16[208,3200]{1,0:T(8,128)(2,1)}, u32[]{:S(2)}, u32[]{:S(2)}) collective-permute-start(bf16[208,3200]{1,0:T(8,128)(2,1)S(1)} %add_convert_fusion), channel_id=1, source_target_pairs={{0,16},{8,24},{16,0},{24,8},{1,17},{9,25},{17,1},{25,9},{2,18},{10... | collective-permute-start | bytes 3993608 | tf_op jit(solution)/shard_map/ppermute | solution.py:791
  326.8 86.8 %all-to-all-start.5 = ((bf16[8,104,2176]{2,1,0:T(8,128)(2,1)}), bf16[8,104,2176]{2,1,0:T(8,128)(2,1)}, u32[]{:S(2)}, u32[]{:S(2)}) async-start(bf16[8,104,2176]{2,1,0:T(8,128)(2,1)} %bitcast.70), calls=%async_computation.5 | async-start | bytes 7241728 | tf_op jit(solution)/shard_map/all_to_all | solution.py:762
  331.8 142.6 %all-reduce.9.cloned.1.call-start = ((), (), s32[]{:S(2)}) async-start(), calls=%async_computation.6 | async-start | bytes 2662400 | tf_op jit(solution)/shard_map/psum | solution.py:938
  332.8 22.5 %copy-start.11 = (bf16[416,3200]{1,0:T(8,128)(2,1)S(1)}, bf16[416,3200]{1,0:T(8,128)(2,1)}, u32[]{:S(2)}) copy-start(bf16[416,3200]{1,0:T(8,128)(2,1)} %get-tuple-element.99) | copy-start | bytes 7987204
  353.7 1.1 copy-start.15
  354.8 3.1 copy-start.13
  360.1 1.5 copy-start.6
  362.7 18.9 %collective-permute-start.5 = (bf16[104,3200]{1,0:T(8,128)(2,1)}, bf16[104,3200]{1,0:T(8,128)(2,1)}, u32[]{:S(2)}, u32[]{:S(2)}) collective-permute-start(bf16[104,3200]{1,0:T(8,128)(2,1)} %get-tuple-element.152), channel_id=1, source_target_pairs={{0,8},{8,0},{16,24},{24,16},{1,9},{9,1},{17,25},{25,17},{2,10},{10... | collective-permute-start | bytes 1996808 | tf_op jit(solution)/shard_map/ppermute | solution.py:791
  364.1 17.4 %collective-permute-start.3 = (bf16[104,3200]{1,0:T(8,128)(2,1)S(1)}, bf16[104,3200]{1,0:T(8,128)(2,1)}, u32[]{:S(2)}, u32[]{:S(2)}) collective-permute-start(bf16[104,3200]{1,0:T(8,128)(2,1)S(1)} %get-tuple-element.153), channel_id=1, source_target_pairs={{0,16},{8,24},{16,0},{24,8},{1,17},{9,25},{17,1},{25,9},{2,18},{10... | collective-permute-start | bytes 1996808 | tf_op jit(solution)/shard_map/ppermute | solution.py:791
  364.7 16.9 %copy-start.7 = (f32[208,3200]{1,0:T(8,128)S(1)}, f32[208,3200]{1,0:T(8,128)}, u32[]{:S(2)}) copy-start(f32[208,3200]{1,0:T(8,128)} %copy-done.6) | copy-start | bytes 7987204
  437.3 36.5 %collective-permute-start.6 = (f32[49,100]{1,0:T(8,128)S(1)}, f32[49,100]{1,0:T(8,128)S(1)}, u32[]{:S(2)}, u32[]{:S(2)}) collective-permute-start(f32[49,100]{1,0:T(8,128)S(1)} %bitcast.82), channel_id=1, source_target_pairs={{0,8},{8,0},{16,24},{24,16},{1,9},{9,1},{17,25},{25,17},{2,10},{10... | collective-permute-start | bytes 58808 | tf_op jit(solution)/shard_map/ppermute | solution.py:773
  438.8 35.0 %collective-permute-start.7 = (f32[49,100]{1,0:T(8,128)S(1)}, f32[49,100]{1,0:T(8,128)S(1)}, u32[]{:S(2)}, u32[]{:S(2)}) collective-permute-start(f32[49,100]{1,0:T(8,128)S(1)} %bitcast.83), channel_id=1, source_target_pairs={{0,16},{8,24},{16,0},{24,8},{1,17},{9,25},{17,1},{25,9},{2,18},{10... | collective-permute-start | bytes 58808 | tf_op jit(solution)/shard_map/ppermute | solution.py:773
  440.3 33.6 %collective-permute-start.8 = (f32[49,100]{1,0:T(8,128)S(1)}, f32[49,100]{1,0:T(8,128)S(1)}, u32[]{:S(2)}, u32[]{:S(2)}) collective-permute-start(f32[49,100]{1,0:T(8,128)S(1)} %bitcast.84), channel_id=1, source_target_pairs={{0,24},{8,16},{16,8},{24,0},{1,25},{9,17},{17,9},{25,1},{2,26},{10... | collective-permute-start | bytes 58808 | tf_op jit(solution)/shard_map/ppermute | solution.py:773
  474.4 17.8 %collective-permute-start.10 = (bf16[104,3200]{1,0:T(8,128)(2,1)}, bf16[104,3200]{1,0:T(8,128)(2,1)S(1)}, u32[]{:S(2)}, u32[]{:S(2)}) collective-permute-start(bf16[104,3200]{1,0:T(8,128)(2,1)} %get-tuple-element.125), channel_id=1, source_target_pairs={{0,8},{8,0},{16,24},{24,16},{1,9},{9,1},{17,25},{25,17},{2,10},{10... | collective-permute-start | bytes 1996808 | tf_op jit(solution)/shard_map/ppermute | solution.py:791
  475.4 18.5 %collective-permute-start.9 = (bf16[104,3200]{1,0:T(8,128)(2,1)}, bf16[104,3200]{1,0:T(8,128)(2,1)S(1)}, u32[]{:S(2)}, u32[]{:S(2)}) collective-permute-start(bf16[104,3200]{1,0:T(8,128)(2,1)} %get-tuple-element.123), channel_id=1, source_target_pairs={{0,16},{8,24},{16,0},{24,8},{1,17},{9,25},{17,1},{25,9},{2,18},{10... | collective-permute-start | bytes 1996808 | tf_op jit(solution)/shard_map/ppermute | solution.py:791
  492.2 1.8 copy-start.17
  493.6 1.1 copy-start.8
  493.6 14.6 %collective-permute-start.13 = (bf16[208,3200]{1,0:T(8,128)(2,1)S(1)}, bf16[208,3200]{1,0:T(8,128)(2,1)}, u32[]{:S(2)}, u32[]{:S(2)}) collective-permute-start(bf16[208,3200]{1,0:T(8,128)(2,1)S(1)} %pad_maximum_fusion.1.refs_0_), channel_id=1, source_target_pairs={{0,1},{1,0},{2,3},{3,2},{4,5},{5,4},{6,7},{7,6},{8,9},{9,8},{10,11... | collective-permute-start | bytes 3993608 | tf_op jit(solution)/shard_map/ppermute | solution.py:778
  494.2 8.3 %copy-start.9 = (bf16[208,3200]{1,0:T(8,128)(2,1)}, bf16[208,3200]{1,0:T(8,128)(2,1)S(1)}, u32[]{:S(2)}) copy-start(bf16[208,3200]{1,0:T(8,128)(2,1)S(1)} %pad_maximum_fusion.refs_0_) | copy-start | bytes 3993604
  494.2 18.3 %collective-permute-start.12 = (bf16[208,3200]{1,0:T(8,128)(2,1)S(1)}, bf16[208,3200]{1,0:T(8,128)(2,1)}, u32[]{:S(2)}, u32[]{:S(2)}) collective-permute-start(bf16[208,3200]{1,0:T(8,128)(2,1)S(1)} %pad_maximum_fusion.refs_0_), channel_id=1, source_target_pairs={{0,1},{1,0},{2,3},{3,2},{4,5},{5,4},{6,7},{7,6},{8,9},{9,8},{10,11... | collective-permute-start | bytes 3993608 | tf_op jit(solution)/shard_map/ppermute | solution.py:778
  494.7 31.6 %collective-permute-start.11 = (bf16[208,3200]{1,0:T(8,128)(2,1)S(1)}, bf16[208,3200]{1,0:T(8,128)(2,1)}, u32[]{:S(2)}, u32[]{:S(2)}) collective-permute-start(bf16[208,3200]{1,0:T(8,128)(2,1)S(1)} %pad_maximum_fusion.1.refs_0_), channel_id=1, source_target_pairs={{0,16},{8,24},{16,0},{24,8},{1,17},{9,25},{17,1},{25,9},{2,18},{10... | collective-permute-start | bytes 3993608 | tf_op jit(solution)/shard_map/ppermute | solution.py:791
  495.3 31.3 %collective-permute-start.15 = (bf16[208,3200]{1,0:T(8,128)(2,1)S(1)}, bf16[208,3200]{1,0:T(8,128)(2,1)}, u32[]{:S(2)}, u32[]{:S(2)}) collective-permute-start(bf16[208,3200]{1,0:T(8,128)(2,1)S(1)} %pad_maximum_fusion.refs_0_), channel_id=1, source_target_pairs={{0,8},{8,0},{16,24},{24,16},{1,9},{9,1},{17,25},{25,17},{2,10},{10... | collective-permute-start | bytes 3993608 | tf_op jit(solution)/shard_map/ppermute | solution.py:791
  496.2 6.3 %copy-start.4 = (bf16[48,100,360]{2,1,0:T(8,128)(2,1)S(1)}, bf16[48,100,360]{2,1,0:T(8,128)(2,1)}, u32[]{:S(2)}) copy-start(bf16[48,100,360]{2,1,0:T(8,128)(2,1)} %shard_map.208) | copy-start | bytes 10368004
  502.5 3.4 copy-start.5
  526.6 8.3 %collective-permute-start.16 = (bf16[208,3200]{1,0:T(8,128)(2,1)}, bf16[208,3200]{1,0:T(8,128)(2,1)S(1)}, u32[]{:S(2)}, u32[]{:S(2)}) collective-permute-start(bf16[208,3200]{1,0:T(8,128)(2,1)} %collective-permute-done.15.refs_0_), channel_id=1, source_target_pairs={{0,1},{1,0},{2,3},{3,2},{4,5},{5,4},{6,7},{7,6},{8,9},{9,8},{10,11... | collective-permute-start | bytes 3993608 | tf_op jit(solution)/shard_map/ppermute | solution.py:778
  526.6 13.6 %collective-permute-start.14 = (bf16[208,3200]{1,0:T(8,128)(2,1)}, bf16[208,3200]{1,0:T(8,128)(2,1)S(1)}, u32[]{:S(2)}, u32[]{:S(2)}) collective-permute-start(bf16[208,3200]{1,0:T(8,128)(2,1)} %collective-permute-done.11.refs_0_), channel_id=1, source_target_pairs={{0,1},{1,0},{2,3},{3,2},{4,5},{5,4},{6,7},{7,6},{8,9},{9,8},{10,11... | collective-permute-start | bytes 3993608 | tf_op jit(solution)/shard_map/ppermute | solution.py:778
  534.8 1.1 copy-start.16
  540.2 1.1 copy-start.14
  541.3 5.8 %copy-start.1 = (bf16[49,800]{1,0:T(8,128)(2,1)S(1)}, bf16[49,800]{1,0:T(8,128)(2,1)}, u32[]{:S(2)}) copy-start(bf16[49,800]{1,0:T(8,128)(2,1)} %param.16) | copy-start | bytes 235204
Sparse Core Ops, SparseCore 0:
  413.8 60.5 all-reduce.8
